TPU v7x, 512 devices: a whole 4x4x16 slice. The times are simulated.
512 devices in a mesh: dp: 64 (over x, z), tensor: 8 (over y, core).
Axes of the slice: x: 4, y: 4, z: 16, core: 2. Of those that a mesh axis runs over, the one named last changes fastest.
Arguments:
- acts: bfloat16 [128, 4, 64, 4096], P('dp', None, None, 'tensor'), may hold values from -6 to 6
- noise_draws: bfloat16 [128, 4, 64, 2048], P('dp', None, None, 'tensor'), may hold values from -6 to 6
- times: float32 [128, 4], P('dp'), may hold values from 0 to 1
- cond: int32 [128, 16], P('dp'), may hold values from 0 to 1023
- emb: bfloat16 [1024, 2048], P(None, 'tensor'), may hold values from -1.5 to 1.5
- weight: bfloat16 [4096, 2048], P('dp', 'tensor'), may hold values from -0.09375 to 0.09375
- noise: float32 [4096, 2048], P('dp', 'tensor'), may hold values from -6 to 6
Outputs:
- clipped_sum: float32 [4096, 2048], P('dp', 'tensor')
- update: float32 [4096, 2048], P('dp', 'tensor')
- norms: float32 [128], P('dp')
All inputs are finite; a program needn't handle non-finite values.
Results may differ from a plain program's by a relative error of at most 0.0017.
Values may be sent and summed in bfloat16 or wider, within the bound.
No kernel may reach another device: no remote copies, remote signals or barrier semaphores. Data moves between devices by JAX's collectives and lax.ppermute only.
A program may use at most 64 MiB of HBM per device.

v0:
```python
import math

import jax
import jax.numpy as jnp
from jax import lax
from jax.sharding import PartitionSpec as P

D = 4096
DO = 2048


def on_device(acts, noise_draws, times, cond, emb, weight, noise):
    recs = acts.shape[0]
    draws = acts.shape[1]
    events = acts.shape[2]
    rows_rec = draws * events
    local_out = weight.shape[1]
    full = lax.all_gather(acts, "tensor", axis=3, tiled=True)
    hflat = full.reshape(recs * rows_rec, D)
    projected = jnp.dot(
        hflat, lax.all_gather(weight, "dp", axis=0, tiled=True), preferred_element_type=jnp.float32
    )
    vocab_ids = lax.broadcasted_iota(jnp.int32, (1, 1, emb.shape[0]), 2)
    counts = jnp.sum((cond[:, :, None] == vocab_ids).astype(jnp.float32), axis=1).astype(
        jnp.bfloat16
    )
    bias = jnp.dot(counts, emb, preferred_element_type=jnp.float32)
    pred = projected.reshape(recs, rows_rec, local_out) + bias[:, None, :]
    weights_t = 1.0 / (times + 0.25)
    wrow = jnp.repeat(weights_t, events, axis=1)[:, :, None]
    scale = 1.0 / math.sqrt(rows_rec)
    targets = noise_draws.reshape(recs, rows_rec, local_out).astype(jnp.float32)
    grads = (wrow * (pred - targets) * scale).astype(jnp.bfloat16)
    hrec = full.reshape(recs, rows_rec, D)
    gram_g = jnp.einsum("rsd,rtd->rst", grads, grads, preferred_element_type=jnp.float32)
    gram_h = jnp.einsum("rsd,rtd->rst", hrec, hrec, preferred_element_type=jnp.float32)
    partial_sq = jnp.sum(gram_h * gram_g, axis=(1, 2))
    squares = lax.psum(partial_sq, "tensor")
    norms = jnp.sqrt(squares)
    bound = 2.0 * math.sqrt(D * DO)
    clip = bound / jnp.maximum(norms, bound)
    block = jnp.einsum("rsd,rso->rdo", hrec, grads, preferred_element_type=jnp.float32)
    clipped_sum = lax.psum_scatter(
        jnp.sum(clip[:, None, None] * block, axis=0), "dp", scatter_dimension=0, tiled=True
    )
    total_recs = recs * lax.axis_size("dp")
    update = (clipped_sum + bound * noise) / total_recs
    return (clipped_sum, update, norms)


def solution(mesh):
    in_specs = (
        P("dp", None, None, "tensor"),
        P("dp", None, None, "tensor"),
        P("dp", None),
        P("dp", None),
        P(None, "tensor"),
        P("dp", "tensor"),
        P("dp", "tensor"),
    )
    out_specs = (P("dp", "tensor"), P("dp", "tensor"), P("dp"))
    return jax.shard_map(
        on_device, mesh=mesh, in_specs=in_specs, out_specs=out_specs, check_vma=False
    )
```

profile of v0, /device:TPU:8, one launch (start us, length us, event | category | flops | bytes accessed | tf_op | source)
XLA Modules:
  0.0 932.2 jit_solution(14444615633590350833)
XLA Ops:
  7.2 0.0 all-gather.5.cloned.1.call-start
  7.2 0.7 all-gather.5.cloned.1.call-update
  7.9 0.0 all-gather.3.cloned.1.call-start
  8.0 0.7 all-gather.3.cloned.1.call-update
  8.7 0.0 reduce-scatter.4.cloned.1.call-start
  8.7 0.7 add_divide_fusion
  9.4 0.1 broadcast_in_dim.2
  9.5 0.1 mul.34
  9.6 0.8 convert_reduce_fusion
  10.4 0.2 fusion.21
  10.5 145.8 %all-gather.5.cloned.1.call-done = bf16[4096,256]{1,0:T(8,128)(2,1)} async-done(((bf16[64,256]{1,0:T(8,128)(2,1)}), bf16[4096,256]{1,0:T(8,128)(2,1)}) %all-gather.5.cloned.1.call-update) | async-done | bytes 2097168 | tf_op jit(solution)/shard_map/all_gather | solution.py:21
  156.3 37.0 %all-gather.3.cloned.1.call-done = bf16[2,4,64,4096]{3,2,1,0:T(8,128)(2,1)} async-done(((bf16[2,4,64,512]{3,2,1,0:T(8,128)(2,1)}), bf16[2,4,64,4096]{3,2,1,0:T(8,128)(2,1)}) %all-gather.3.cloned.1.call-update) | async-done | bytes 4194320 | tf_op jit(solution)/shard_map/all_gather | solution.py:18
  193.2 4.2 fusion.14
  197.5 0.2 fusion.20
  197.7 1.4 fusion.17
  199.1 11.4 %psum.7 = f32[2]{0:T(128)S(1)} all-reduce(f32[2]{0:T(128)S(1)} %fusion.17), channel_id=1, replica_groups=mesh['dp'=64,'tensor'=8] {'tensor'}, use_global_device_ids=true, to_apply=%region_2.0 | all-reduce | flops 2 | bytes 16 | tf_op jit(solution)/shard_map/psum | solution.py:38
  210.5 0.5 maximum_divide_fusion
  211.1 6.1 multiply_reduce_fusion
  217.1 5.6 copy.24
  222.7 0.8 copy-done.2
  223.6 0.1 copy.20
  223.6 700.4 %reduce-scatter.4.cloned.1.call-done = f32[64,256]{1,0:T(8,128)} async-done(((f32[4096,256]{1,0:T(8,128)}), f32[64,256]{1,0:T(8,128)}) %reduce-scatter.4.cloned.1.call-update) | async-done | bytes 65552
  924.0 0.9 copy.25
  925.0 0.7 copy.22
  (7 shorter events, 0.1 us)
Async XLA Ops:
  7.2 3.2 copy-start
  7.2 149.1 %all-gather.5.cloned.1.call-start = ((), (), s32[]{:S(2)}) async-start(), calls=%async_computation.2 | async-start | bytes 2129920 | tf_op jit(solution)/shard_map/all_gather | solution.py:21
  7.9 185.3 %all-gather.3.cloned.1.call-start = ((), (), s32[]{:S(2)}) async-start(), calls=%async_computation.1 | async-start | bytes 4718592 | tf_op jit(solution)/shard_map/all_gather | solution.py:18
  8.7 915.3 %reduce-scatter.4.cloned.1.call-start = ((), (), s32[]{:S(2)}) async-start(), calls=%async_computation.3 | async-start | bytes 4259840
  193.2 4.5 copy-start.1
  222.7 0.8 copy-start.2
Sparse Core Ops, SparseCore 0:
  11.0 145.2 all-gather.4
  158.4 34.7 all-gather.2
  222.9 701.0 reduce-scatter.3
where the time goes:
time: 933 us; the launch traced here: 932 us
  waiting for transfers between devices  884 us (95%)
  between operations  13.8 us (1%)
  matrix products  12.1 us (1%)
  blocking collectives  11.4 us (1%)
    unnamed x4, waiting for transfers between devices  702 us
    all_gather x1, waiting for transfers between devices, on_device(): lax.all_gather(weight, 'dp', axis=0, tiled=True)  146 us
    all_gather x1, waiting for transfers between devices, on_device(): full = lax.all_gather(acts, 'tensor', axis=3, tiled=True)  37 us
  transfers between devices with their start and end apart: 3, of which 3 were waited for; matrix products, arithmetic and copies ran while one was open for 0% of the time, Pallas kernels for 0%

commit v1 on v0

v1 whole, which is shorter than its diff:
```python
import functools
import math

import jax
import jax.numpy as jnp
from jax import lax
from jax.experimental import pallas as pl
from jax.experimental.pallas import tpu as pltpu
from jax.sharding import Mesh, PartitionSpec as P

D = 4096
DO = 2048
F32 = jnp.float32
BF16 = jnp.bfloat16
VMEM_LIMIT = 40 * 1024 * 1024


def params(**kw):
    return pltpu.CompilerParams(vmem_limit_bytes=VMEM_LIMIT, **kw)


def dot(a, b, ca, cb):
    return lax.dot_general(a, b, (((ca,), (cb,)), ((), ())), preferred_element_type=F32)


def gram_kernel(h_ref, o_ref):
    @pl.when(pl.program_id(0) == 0)
    def _():
        o_ref[...] = jnp.zeros_like(o_ref)

    recs, rows, _ = o_ref.shape
    for j in range(h_ref.shape[0]):
        for r in range(recs):
            h = h_ref[j, r * rows : (r + 1) * rows, :]
            o_ref[r] += dot(h, h, 1, 1)


def grad_kernel(h_ref, w_ref, n_ref, b_ref, t_ref, gh_ref, g_ref, sq_ref, acc):
    i = pl.program_id(0)
    blocks = h_ref.shape[0]
    feats = h_ref.shape[2]
    part = dot(h_ref[0], w_ref[0:feats, :], 1, 0)
    for j in range(1, blocks):
        part += dot(h_ref[j], w_ref[j * feats : (j + 1) * feats, :], 1, 0)

    @pl.when(i == 0)
    def _():
        acc[...] = part

    @pl.when(i > 0)
    def _():
        acc[...] += part

    @pl.when(i == pl.num_programs(0) - 1)
    def _():
        recs, rows, _ = gh_ref.shape
        lane = lax.broadcasted_iota(jnp.int32, sq_ref.shape, 1)
        out = jnp.zeros(sq_ref.shape, F32)
        for r in range(recs):
            at = slice(r * rows, (r + 1) * rows)
            pred = acc[at, :] + b_ref[r : r + 1, :]
            g = (t_ref[at, :] * (pred - n_ref[at, :].astype(F32))).astype(BF16)
            g_ref[at, :] = g
            out = jnp.where(lane == r, jnp.sum(gh_ref[r] * dot(g, g, 1, 1)), out)
        sq_ref[...] = out


def sum_kernel(sq_ref, h_ref, g_ref, c_ref, *, bound, recs):
    rows = g_ref.shape[0] // recs
    feats = h_ref.shape[2]
    norms = jnp.sqrt(jnp.sum(sq_ref[...], axis=0, keepdims=True))
    clip = bound / jnp.maximum(norms, bound)
    for j in range(h_ref.shape[0]):
        total = None
        for r in range(recs):
            at = slice(r * rows, (r + 1) * rows)
            block = dot(h_ref[j, at, :], g_ref[at, :], 0, 0) * clip[0:1, r : r + 1]
            total = block if total is None else total + block
        c_ref[j * feats : (j + 1) * feats, :] = total.astype(BF16)


def add_kernel(x_ref, o_ref):
    step = 128

    @pl.loop(0, o_ref.shape[0] // step)
    def _(i):
        at = pl.ds(pl.multiple_of(i * step, step), step)
        total = x_ref[0, at, :].astype(F32)
        for k in range(1, x_ref.shape[0]):
            total += x_ref[k, at, :].astype(F32)
        o_ref[at, :] = total.astype(o_ref.dtype)


def gather(v, axis):
    n = lax.axis_size(axis)
    return lax.all_to_all(jnp.broadcast_to(v[None], (n,) + v.shape), axis, 0, 0)


def on_device(acts, noise_draws, times, cond, emb, weight, noise):
    recs, draws, events, feats = acts.shape
    rows = draws * events
    local_out = weight.shape[1]
    tensor = ("y", "core")
    nt = lax.axis_size("y") * lax.axis_size("core")
    nx, nz = lax.axis_size("x"), lax.axis_size("z")
    bound = 2.0 * math.sqrt(D * DO)

    full = lax.all_gather(acts.reshape(recs * rows, feats), tensor, axis=0, tiled=False)

    wz = gather(weight, "z").reshape(nz * weight.shape[0], local_out)
    wfull = gather(wz, "x").reshape(D, local_out)

    vocab_ids = lax.broadcasted_iota(jnp.int32, (1, 1, emb.shape[0]), 2)
    counts = jnp.sum((cond[:, :, None] == vocab_ids).astype(F32), axis=1).astype(BF16)
    bias = jnp.dot(counts, emb, preferred_element_type=F32)
    wrow = jnp.repeat(
        (1.0 / (times + 0.25)).reshape(recs * draws) * (1.0 / math.sqrt(rows)), events
    )[:, None]

    step = 2
    grid = nt // step
    h_spec = pl.BlockSpec((step, recs * rows, feats), lambda i: (i, 0, 0))
    whole = lambda *shape: pl.BlockSpec(shape, lambda i: (0,) * len(shape))
    gram_h = pl.pallas_call(
        gram_kernel,
        grid=(grid,),
        in_specs=[h_spec],
        out_specs=whole(recs, rows, rows),
        out_shape=jax.ShapeDtypeStruct((recs, rows, rows), F32),
        compiler_params=params(),
        cost_estimate=pl.CostEstimate(
            flops=2 * recs * rows * rows * D, bytes_accessed=2 * recs * rows * D, transcendentals=0
        ),
    )(full)
    grads, sq = pl.pallas_call(
        grad_kernel,
        grid=(grid,),
        in_specs=[
            h_spec,
            pl.BlockSpec((step * feats, local_out), lambda i: (i, 0)),
            whole(recs * rows, local_out),
            whole(recs, local_out),
            whole(recs * rows, 1),
            whole(recs, rows, rows),
        ],
        out_specs=[whole(recs * rows, local_out), whole(nt, 128)],
        out_shape=[
            jax.ShapeDtypeStruct((recs * rows, local_out), BF16),
            jax.ShapeDtypeStruct((nt, 128), F32),
        ],
        scratch_shapes=[pltpu.VMEM((recs * rows, local_out), F32)],
        compiler_params=params(),
        cost_estimate=pl.CostEstimate(
            flops=2 * recs * rows * local_out * D,
            bytes_accessed=2 * recs * rows * D + 2 * D * local_out,
            transcendentals=0,
        ),
    )(full, wfull, noise_draws.reshape(recs * rows, local_out), bias, wrow, gram_h)

    sq_all = lax.all_to_all(sq.reshape(nt, 1, 128), tensor, 0, 0).reshape(nt, 128)
    norms = jnp.sqrt(jnp.sum(sq_all[:, :recs], axis=0))

    partial = pl.pallas_call(
        functools.partial(sum_kernel, bound=bound, recs=recs),
        grid=(grid,),
        in_specs=[whole(nt, 128), h_spec, whole(recs * rows, local_out)],
        out_specs=pl.BlockSpec((step * feats, local_out), lambda i: (i, 0)),
        out_shape=jax.ShapeDtypeStruct((D, local_out), BF16),
        compiler_params=params(),
        cost_estimate=pl.CostEstimate(
            flops=2 * recs * rows * local_out * D,
            bytes_accessed=2 * recs * rows * D + 2 * D * local_out,
            transcendentals=0,
        ),
    )(sq_all, full, grads)

    over_x = lax.all_to_all(partial.reshape(nx, D // nx, local_out), "x", 0, 0)
    sum_x = pl.pallas_call(
        add_kernel,
        out_shape=jax.ShapeDtypeStruct((D // nx, local_out), BF16),
        compiler_params=params(),
    )(over_x)
    over_z = lax.all_to_all(sum_x.reshape(nz, D // nx // nz, local_out), "z", 0, 0)
    clipped_sum = jnp.sum(over_z.astype(F32), axis=0)
    total_recs = recs * nx * nz
    update = (clipped_sum + bound * noise) / total_recs
    return (clipped_sum, update, norms)


def solution(mesh):
    grid = Mesh(mesh.devices.reshape(4, 16, 4, 2), ("x", "z", "y", "core"))
    dp, tensor = ("x", "z"), ("y", "core")
    in_specs = (
        P(dp, None, None, tensor),
        P(dp, None, None, tensor),
        P(dp, None),
        P(dp, None),
        P(None, tensor),
        P(dp, tensor),
        P(dp, tensor),
    )
    out_specs = (P(dp, tensor), P(dp, tensor), P(dp))
    return jax.shard_map(
        on_device, mesh=grid, in_specs=in_specs, out_specs=out_specs, check_vma=False
    )
```

time: 933 us -> 175 us (0.19)
  the two profiles are of different devices: /device:TPU:8 before, /device:TPU:32 now
where the time goes in v1:
time: 175 us; the launch traced here: 174 us
  blocking collectives  81.8 us (47%)
  waiting for transfers between devices  45 us (26%)
  starting transfers between devices  15.8 us (9%)
  between operations  14.1 us (8%)
  local copies, waits for them, and re-layouts  8.51 us (5%)
  Pallas kernels  7.8 us (4%)
    all_to_all x1, blocking collectives, gather(): return lax.all_to_all(jnp.broadcast_to(v[None], (n,) + v.shape), axis, 0, 0)  43.2 us
    all_to_all x1, blocking collectives, on_device(): over_x = lax.all_to_all(partial.reshape(nx, D // nx, local_out), 'x', 0, 0)  29.1 us
    all_to_all x1, waiting for transfers between devices, on_device(): lax.all_to_all(sum_x.reshape(nz, D // nx // nz, local_out), 'z', 0, 0)  26.9 us
    all_to_all x1, waiting for transfers between devices, gather(): return lax.all_to_all(jnp.broadcast_to(v[None], (n,) + v.shape), axis, 0, 0)  17.5 us
    all_to_all x1, starting transfers between devices, on_device(): lax.all_to_all(sum_x.reshape(nz, D // nx // nz, local_out), 'z', 0, 0)  11.3 us
    all_to_all x1, blocking collectives, on_device(): lax.all_to_all(sq.reshape(nt, 1, 128), tensor, 0, 0).reshape(nt, 128)  9.53 us
    unnamed x16, local copies, waits for them, and re-layouts  5.36 us
    all_to_all x1, starting transfers between devices, gather(): return lax.all_to_all(jnp.broadcast_to(v[None], (n,) + v.shape), axis, 0, 0)  4.42 us
  transfers between devices with their start and end apart: 3, of which 2 were waited for; matrix products, arithmetic and copies ran while one was open for 2% of the time, Pallas kernels for 1%

profile of v1, /device:TPU:32, one launch (start us, length us, event | category | flops | bytes accessed | tf_op | source)
XLA Modules:
  0.0 174.1 jit_solution(3479403913055366064)
XLA Ops:
  7.2 0.7 all-gather.2.cloned.1.call-update
  7.9 0.8 broadcast_in_dim.8
  8.7 43.2 %all_to_all.25 = bf16[16,64,256]{2,1,0:T(8,128)(2,1)S(1)} all-to-all(bf16[16,64,256]{2,1,0:T(8,128)(2,1)S(1)} %broadcast_in_dim.8), channel_id=1, replica_groups=mesh['x'=4,'z'=16,'y'=4,'core'=2] {'z'}, dimensions={0} | all-to-all | bytes 1048576 | tf_op jit(solution)/shard_map/all_to_all | solution.py:96
  52.0 1.5 broadcast_in_dim.19
  53.4 4.4 %all-to-all-start.1 = ((bf16[4,1024,256]{2,1,0:T(8,128)(2,1)}), bf16[4,1024,256]{2,1,0:T(8,128)(2,1)S(1)}, u32[]{:S(2)}, u32[]{:S(2)}) async-start(bf16[4,1024,256]{2,1,0:T(8,128)(2,1)} %broadcast_in_dim.19), calls=%async_computation.1 | async-start | bytes 4194304 | tf_op jit(solution)/shard_map/all_to_all | solution.py:96
  57.9 0.1 mul.13
  58.0 0.2 broadcast_in_dim_reshape.5.t_ref
  58.2 0.1 convert_reduce_fusion.1
  58.4 0.2 fusion.2.b_ref
  58.5 2.2 %copy-done.1 = bf16[8,512,512]{2,1,0:T(8,128)(2,1)S(1)} copy-done((bf16[8,512,512]{2,1,0:T(8,128)(2,1)S(1)}, bf16[8,512,512]{2,1,0:T(8,128)(2,1)}, u32[]{:S(2)}) %copy-start.1) | copy-done | bytes 4194328
  60.7 2.0 %shard_map.94.gh_ref = f32[2,256,256]{2,1,0:T(8,128)S(1)} custom-call(bf16[8,512,512]{2,1,0:T(8,128)(2,1)S(1)} %copy-done.1), custom_call_target="tpu_custom_call" | custom-call | flops 1073741824 | bytes 4194304 | tf_op jit(solution)/shard_map/pallas_call | solution.py:124
  62.7 17.5 %all-to-all-done.1 = bf16[4,1024,256]{2,1,0:T(8,128)(2,1)S(1)} async-done(((bf16[4,1024,256]{2,1,0:T(8,128)(2,1)}), bf16[4,1024,256]{2,1,0:T(8,128)(2,1)S(1)}, u32[]{:S(2)}, u32[]{:S(2)}) %all-to-all-start.1) | async-done | bytes 2097184 | tf_op jit(solution)/shard_map/all_to_all | solution.py:96
  80.2 2.2 %copy-done.2 = bf16[8,512,512]{2,1,0:T(8,128)(2,1)S(1)} copy-done((bf16[8,512,512]{2,1,0:T(8,128)(2,1)S(1)}, bf16[8,512,512]{2,1,0:T(8,128)(2,1)}, u32[]{:S(2)}) %copy-start.2) | copy-done | bytes 4194328
  82.4 0.9 copy-done.3
  83.3 2.4 %shard_map.95 = (bf16[512,256]{1,0:T(8,128)(2,1)S(1)}, f32[8,128]{1,0:T(8,128)S(1)}) custom-call(bf16[8,512,512]{2,1,0:T(8,128)(2,1)S(1)} %copy-done.2, bf16[4096,256]{1,0:T(8,128)(2,1)S(1)} %bitcast.12, bf16[512,256]{1,0:T(8,128)(2,1)S(1)} %bitcast.14, f32[2,256]{1,0:T(2,128)S(1)} %fusion.2.b_ref, f32[512,1]{1,0:T(8,128)S(1)} %broadcast_in_dim_reshape.5.t_ref, ...), custom_call_target="tpu_custom_call" | custom-call | flops 1073741824 | bytes 6291456 | tf_op jit(solution)/shard_map/pallas_call | solution.py:135
  85.8 9.5 %all_to_all.26 = f32[8,1,128]{2,1,0:T(1,128)S(1)} all-to-all(f32[8,1,128]{2,1,0:T(1,128)S(1)} %bitcast.17), channel_id=1, replica_groups=mesh['x'=4,'z'=16,'y'=4,'core'=2] {'y','core'}, dimensions={0} | all-to-all | bytes 8192 | tf_op jit(solution)/shard_map/all_to_all | solution.py:160
  95.3 2.3 %shard_map.96 = bf16[4096,256]{1,0:T(8,128)(2,1)S(1)} custom-call(f32[8,128]{1,0:T(8,128)S(1)} %bitcast.15, bf16[8,512,512]{2,1,0:T(8,128)(2,1)S(1)} %copy-done.2, bf16[512,256]{1,0:T(8,128)(2,1)S(1)} %get-tuple-element.6.g_ref), custom_call_target="tpu_custom_call" | custom-call | flops 1073741824 | bytes 6291456 | tf_op jit(solution)/shard_map/pallas_call | solution.py:163
  97.6 29.1 %all_to_all.27.x_ref = bf16[4,1024,256]{2,1,0:T(8,128)(2,1)S(1)} all-to-all(bf16[4,1024,256]{2,1,0:T(8,128)(2,1)S(1)} %bitcast.13), channel_id=1, replica_groups=mesh['x'=4,'z'=16,'y'=4,'core'=2] {'x'}, dimensions={0} | all-to-all | bytes 4194304 | tf_op jit(solution)/shard_map/all_to_all | solution.py:177
  126.7 1.1 shard_map.97
  127.8 11.3 %all-to-all-start.4 = ((bf16[16,64,256]{2,1,0:T(8,128)(2,1)}), bf16[16,64,256]{2,1,0:T(8,128)(2,1)S(1)}, u32[]{:S(2)}, u32[]{:S(2)}) async-start(bf16[16,64,256]{2,1,0:T(8,128)(2,1)} %bitcast.8), calls=%async_computation.4 | async-start | bytes 1048576 | tf_op jit(solution)/shard_map/all_to_all | solution.py:183
  139.1 0.5 sqrt.3
  139.6 26.9 %all-to-all-done.4 = bf16[16,64,256]{2,1,0:T(8,128)(2,1)S(1)} async-done(((bf16[16,64,256]{2,1,0:T(8,128)(2,1)}), bf16[16,64,256]{2,1,0:T(8,128)(2,1)S(1)}, u32[]{:S(2)}, u32[]{:S(2)}) %all-to-all-start.4) | async-done | bytes 524320 | tf_op jit(solution)/shard_map/all_to_all | solution.py:183
  166.5 0.1 convert_reduce_fusion
  166.6 0.6 add_multiply_fusion
  (18 shorter events, 0.2 us)
Async XLA Ops:
  7.2 51.2 %copy-start = (bf16[1024,256]{1,0:T(8,128)(2,1)S(1)}, bf16[1024,256]{1,0:T(8,128)(2,1)}, u32[]{:S(2)}) copy-start(bf16[1024,256]{1,0:T(8,128)(2,1)} %param.11) | copy-start | bytes 1572868
  7.2 51.4 %all-gather.2.cloned.1.call-start = ((), (), s32[]{:S(2)}) async-start(), calls=%async_computation.5 | async-start | bytes 4718592 | tf_op jit(solution)/shard_map/all_gather | solution.py:108
  53.4 4.4 %copy-start.7 = (f32[2,4]{1,0:T(2,128)S(1)}, f32[2,4]{1,0:T(2,128)}, u32[]{:S(2)}) copy-start(f32[2,4]{1,0:T(2,128)} %param.9) | copy-start | bytes 100
  53.4 4.8 %copy-start.6 = (s32[2,16]{1,0:T(2,128)S(1)}, s32[2,16]{1,0:T(2,128)}, u32[]{:S(2)}) copy-start(s32[2,16]{1,0:T(2,128)} %param.10) | copy-start | bytes 388
  53.4 26.7 %all-to-all-start.1 = ((bf16[4,1024,256]{2,1,0:T(8,128)(2,1)}), bf16[4,1024,256]{2,1,0:T(8,128)(2,1)S(1)}, u32[]{:S(2)}, u32[]{:S(2)}) async-start(bf16[4,1024,256]{2,1,0:T(8,128)(2,1)} %broadcast_in_dim.19), calls=%async_computation.1 | async-start | bytes 4194304 | tf_op jit(solution)/shard_map/all_to_all | solution.py:96
  58.5 2.2 %copy-start.1 = (bf16[8,512,512]{2,1,0:T(8,128)(2,1)S(1)}, bf16[8,512,512]{2,1,0:T(8,128)(2,1)}, u32[]{:S(2)}) copy-start(bf16[8,512,512]{2,1,0:T(8,128)(2,1)} %all-gather.2.cloned.1.call-done.h_ref) | copy-start | bytes 12582916
  80.2 2.2 %copy-start.2 = (bf16[8,512,512]{2,1,0:T(8,128)(2,1)S(1)}, bf16[8,512,512]{2,1,0:T(8,128)(2,1)}, u32[]{:S(2)}) copy-start(bf16[8,512,512]{2,1,0:T(8,128)(2,1)} %all-gather.2.cloned.1.call-done.h_ref) | copy-start | bytes 12582916
  82.4 0.9 copy-start.3
  126.7 39.9 %copy-start.5 = (f32[64,256]{1,0:T(8,128)S(1)}, f32[64,256]{1,0:T(8,128)}, u32[]{:S(2)}) copy-start(f32[64,256]{1,0:T(8,128)} %param.13) | copy-start | bytes 196612
  127.8 38.7 %all-to-all-start.4 = ((bf16[16,64,256]{2,1,0:T(8,128)(2,1)}), bf16[16,64,256]{2,1,0:T(8,128)(2,1)S(1)}, u32[]{:S(2)}, u32[]{:S(2)}) async-start(bf16[16,64,256]{2,1,0:T(8,128)(2,1)} %bitcast.8), calls=%async_computation.4 | async-start | bytes 1048576 | tf_op jit(solution)/shard_map/all_to_all | solution.py:183
  166.6 0.7 copy-start.4
Sparse Core Ops, SparseCore 0:
  10.2 43.9 all-gather.1

commit v2 on v1

--- a/solution.py
+++ b/solution.py
@@ -12,7 +12,9 @@
 DO = 2048
 F32 = jnp.float32
 BF16 = jnp.bfloat16
-VMEM_LIMIT = 40 * 1024 * 1024
+F16 = jnp.float16
+SCALE = 256.0
+VMEM_LIMIT = 60 * 1024 * 1024
 
 
 def params(**kw):
@@ -76,19 +78,16 @@
             at = slice(r * rows, (r + 1) * rows)
             block = dot(h_ref[j, at, :], g_ref[at, :], 0, 0) * clip[0:1, r : r + 1]
             total = block if total is None else total + block
-        c_ref[j * feats : (j + 1) * feats, :] = total.astype(BF16)
-
-
-def add_kernel(x_ref, o_ref):
-    step = 128
-
-    @pl.loop(0, o_ref.shape[0] // step)
-    def _(i):
-        at = pl.ds(pl.multiple_of(i * step, step), step)
-        total = x_ref[0, at, :].astype(F32)
-        for k in range(1, x_ref.shape[0]):
-            total += x_ref[k, at, :].astype(F32)
-        o_ref[at, :] = total.astype(o_ref.dtype)
+        c_ref[j * feats : (j + 1) * feats, :] = root(total)
+
+
+def root(v):
+    return v * lax.rsqrt(jnp.maximum(jnp.abs(v), 1e-30)) * SCALE
+
+
+def unroot(v):
+    v = v.astype(F32)
+    return v * jnp.abs(v) * (1.0 / (SCALE * SCALE))
 
 
 def gather(v, axis):
@@ -165,7 +164,7 @@
         grid=(grid,),
         in_specs=[whole(nt, 128), h_spec, whole(recs * rows, local_out)],
         out_specs=pl.BlockSpec((step * feats, local_out), lambda i: (i, 0)),
-        out_shape=jax.ShapeDtypeStruct((D, local_out), BF16),
+        out_shape=jax.ShapeDtypeStruct((D, local_out), F32),
         compiler_params=params(),
         cost_estimate=pl.CostEstimate(
             flops=2 * recs * rows * local_out * D,
@@ -174,14 +173,10 @@
         ),
     )(sq_all, full, grads)
 
-    over_x = lax.all_to_all(partial.reshape(nx, D // nx, local_out), "x", 0, 0)
-    sum_x = pl.pallas_call(
-        add_kernel,
-        out_shape=jax.ShapeDtypeStruct((D // nx, local_out), BF16),
-        compiler_params=params(),
-    )(over_x)
-    over_z = lax.all_to_all(sum_x.reshape(nz, D // nx // nz, local_out), "z", 0, 0)
-    clipped_sum = jnp.sum(over_z.astype(F32), axis=0)
+    sent = partial.astype(F16).reshape(nx, D // nx, local_out)
+    sum_x = jnp.sum(unroot(lax.all_to_all(sent, "x", 0, 0)), axis=0)
+    sent = root(sum_x).astype(F16).reshape(nz, D // nx // nz, local_out)
+    clipped_sum = jnp.sum(unroot(lax.all_to_all(sent, "z", 0, 0)), axis=0)
     total_recs = recs * nx * nz
     update = (clipped_sum + bound * noise) / total_recs
     return (clipped_sum, update, norms)

time: 175 us -> 183 us (1.046)
  Pallas kernels: 7.8 us -> 16.9 us
  other arithmetic: 0.84 us -> 5.16 us
  local copies, waits for them, and re-layouts: 8.51 us -> 5.19 us
  waiting for transfers between devices: 45 us -> 43.1 us
    unnamed x16 -> x14, local copies, waits for them, and re-layouts: 5.36 us -> 1.34 us
    pallas_call x1, Pallas kernels: 2.33 us -> 6.24 us  [on_device(): pl.pallas_call(functools.partial(sum_kernel, bound=bound, recs=recs), gri...]
    convert_element_type x0 -> x2, other arithmetic: none -> 3.48 us  [the longest x1 2.46 us: on_device(): sent = partial.astype(F16).reshape(nx, D // nx, local_out)]
    pallas_call x1, Pallas kernels: 2.44 us -> 5.85 us  [on_device(): pl.pallas_call(grad_kernel, grid=(grid,), in_specs=[h_spec, pl.BlockSpec(...]
    pallas_call x1, Pallas kernels: 1.95 us -> 4.79 us  [on_device(): pl.pallas_call(gram_kernel, grid=(grid,), in_specs=[h_spec], out_specs=wh...]
    all_to_all x1, waiting for transfers between devices: 17.5 us -> 15.6 us  [gather(): return lax.all_to_all(jnp.broadcast_to(v[None], (n,) + v.shape), axis, 0, 0)]
  transfers between devices with their start and end apart: 3 -> 3, of which waited for: 2 -> 2; matrix products, arithmetic and copies ran while one was open for 2% -> 3% of each run, Pallas kernels for 1% -> 3%
where the time goes in v2:
time: 183 us
  blocking collectives  81.9 us (45%)
  waiting for transfers between devices  43.1 us (24%)
  Pallas kernels  16.9 us (9%)
  starting transfers between devices  15.6 us (9%)
  between operations  14.1 us (8%)
  local copies, waits for them, and re-layouts  5.19 us (3%)
  other arithmetic  5.16 us (3%)
    all_to_all x1, blocking collectives, gather(): return lax.all_to_all(jnp.broadcast_to(v[None], (n,) + v.shape), axis, 0, 0)  43.2 us
    all_to_all x1, blocking collectives, on_device(): sum_x = jnp.sum(unroot(lax.all_to_all(sent, 'x', 0, 0)), axis=0)  28.9 us
    all_to_all x1, waiting for transfers between devices, on_device(): clipped_sum = jnp.sum(unroot(lax.all_to_all(sent, 'z', 0, 0)), axis=0)  26.9 us
    all_to_all x1, waiting for transfers between devices, gather(): return lax.all_to_all(jnp.broadcast_to(v[None], (n,) + v.shape), axis, 0, 0)  15.6 us
    all_to_all x1, starting transfers between devices, on_device(): clipped_sum = jnp.sum(unroot(lax.all_to_all(sent, 'z', 0, 0)), axis=0)  11.3 us
    all_to_all x1, blocking collectives, on_device(): lax.all_to_all(sq.reshape(nt, 1, 128), tensor, 0, 0).reshape(nt, 128)  9.75 us
    pallas_call x1, Pallas kernels, on_device(): pl.pallas_call(functools.partial(sum_kernel, bound=bound, recs=recs), gri...  6.24 us
    pallas_call x1, Pallas kernels, on_device(): pl.pallas_call(grad_kernel, grid=(grid,), in_specs=[h_spec, pl.BlockSpec(...  5.85 us
  transfers between devices with their start and end apart: 3, of which 2 were waited for; matrix products, arithmetic and copies ran while one was open for 3% of the time, Pallas kernels for 3%

profile of v2, /device:TPU:32, one launch (start us, length us, event | category | flops | bytes accessed | tf_op | source)
XLA Modules:
  0.0 182.7 jit_solution(15930550578869037108)
XLA Ops:
  7.2 0.7 all-gather.2.cloned.1.call-update
  7.9 0.8 broadcast_in_dim.8
  8.8 43.2 %all_to_all.25 = bf16[16,64,256]{2,1,0:T(8,128)(2,1)S(1)} all-to-all(bf16[16,64,256]{2,1,0:T(8,128)(2,1)S(1)} %broadcast_in_dim.8), channel_id=1, replica_groups=mesh['x'=4,'z'=16,'y'=4,'core'=2] {'z'}, dimensions={0} | all-to-all | bytes 1048576 | tf_op jit(solution)/shard_map/all_to_all | solution.py:95
  52.0 1.4 broadcast_in_dim.19
  53.4 4.3 %all-to-all-start.1 = ((bf16[4,1024,256]{2,1,0:T(8,128)(2,1)}), bf16[4,1024,256]{2,1,0:T(8,128)(2,1)S(1)}, u32[]{:S(2)}, u32[]{:S(2)}) async-start(bf16[4,1024,256]{2,1,0:T(8,128)(2,1)} %broadcast_in_dim.19), calls=%async_computation.1 | async-start | bytes 4194304 | tf_op jit(solution)/shard_map/all_to_all | solution.py:95
  57.7 0.1 mul.42
  57.9 0.9 broadcast_in_dim_reshape.5.t_ref
  58.8 0.1 convert_reduce_fusion
  58.9 0.8 fusion.6.b_ref
  59.7 4.8 %shard_map.94.gh_ref = f32[2,256,256]{2,1,0:T(8,128)} custom-call(bf16[8,512,512]{2,1,0:T(8,128)(2,1)} %all-gather.2.cloned.1.call-done.h_ref), custom_call_target="tpu_custom_call" | custom-call | flops 1073741824 | bytes 4194304 | tf_op jit(solution)/shard_map/pallas_call | solution.py:123
  64.5 15.6 %all-to-all-done.1 = bf16[4,1024,256]{2,1,0:T(8,128)(2,1)S(1)} async-done(((bf16[4,1024,256]{2,1,0:T(8,128)(2,1)}), bf16[4,1024,256]{2,1,0:T(8,128)(2,1)S(1)}, u32[]{:S(2)}, u32[]{:S(2)}) %all-to-all-start.1) | async-done | bytes 2097184 | tf_op jit(solution)/shard_map/all_to_all | solution.py:95
  80.1 1.3 copy-done.1
  81.4 5.9 %shard_map.95 = (bf16[512,256]{1,0:T(8,128)(2,1)}, f32[8,128]{1,0:T(8,128)}) custom-call(bf16[8,512,512]{2,1,0:T(8,128)(2,1)} %all-gather.2.cloned.1.call-done.h_ref, bf16[4096,256]{1,0:T(8,128)(2,1)} %bitcast.13, bf16[512,256]{1,0:T(8,128)(2,1)} %bitcast.17, f32[2,256]{1,0:T(2,128)} %fusion.6.b_ref, f32[512,1]{1,0:T(8,128)} %broadcast_in_dim_reshape.5.t_ref, ...), custom_call_target="tpu_custom_call" | custom-call | flops 1073741824 | bytes 6291456 | tf_op jit(solution)/shard_map/pallas_call | solution.py:134
  87.2 9.8 %all_to_all.26 = f32[8,1,128]{2,1,0:T(1,128)} all-to-all(f32[8,1,128]{2,1,0:T(1,128)} %bitcast.20), channel_id=1, replica_groups=mesh['x'=4,'z'=16,'y'=4,'core'=2] {'y','core'}, dimensions={0} | all-to-all | bytes 8192 | tf_op jit(solution)/shard_map/all_to_all | solution.py:159
  97.0 6.2 %shard_map.96 = f32[4096,256]{1,0:T(8,128)} custom-call(f32[8,128]{1,0:T(8,128)} %bitcast.18, bf16[8,512,512]{2,1,0:T(8,128)(2,1)} %all-gather.2.cloned.1.call-done.h_ref, bf16[512,256]{1,0:T(8,128)(2,1)} %get-tuple-element.6.g_ref), custom_call_target="tpu_custom_call" | custom-call | flops 1073741824 | bytes 6291456 | tf_op jit(solution)/shard_map/pallas_call | solution.py:162
  103.2 2.5 %convert_element_type.21 = f16[4096,256]{1,0:T(8,128)(2,1)S(1)} convert(f32[4096,256]{1,0:T(8,128)} %shard_map.96) | non-fusion elementwise | flops 1048576 | bytes 6291456 | tf_op jit(solution)/shard_map/convert_element_type | solution.py:176
  105.7 28.9 %all_to_all.27 = f16[4,1024,256]{2,1,0:T(8,128)(2,1)S(1)} all-to-all(f16[4,1024,256]{2,1,0:T(8,128)(2,1)S(1)} %bitcast.12), channel_id=1, replica_groups=mesh['x'=4,'z'=16,'y'=4,'core'=2] {'x'}, dimensions={0} | all-to-all | bytes 4194304 | tf_op jit(solution)/shard_map/all_to_all | solution.py:177
  134.6 0.7 fusion.1
  135.3 1.0 multiply_convert_fusion
  136.3 11.3 %all-to-all-start.4 = ((f16[16,64,256]{2,1,0:T(8,128)(2,1)}), f16[16,64,256]{2,1,0:T(8,128)(2,1)S(1)}, u32[]{:S(2)}, u32[]{:S(2)}) async-start(f16[16,64,256]{2,1,0:T(8,128)(2,1)} %multiply_convert_fusion), calls=%async_computation.4 | async-start | bytes 1048576 | tf_op jit(solution)/shard_map/all_to_all | solution.py:179
  147.7 0.5 sqrt.3
  148.2 26.9 %all-to-all-done.4 = f16[16,64,256]{2,1,0:T(8,128)(2,1)S(1)} async-done(((f16[16,64,256]{2,1,0:T(8,128)(2,1)}), f16[16,64,256]{2,1,0:T(8,128)(2,1)S(1)}, u32[]{:S(2)}, u32[]{:S(2)}) %all-to-all-start.4) | async-done | bytes 524320 | tf_op jit(solution)/shard_map/all_to_all | solution.py:179
  175.0 0.2 fusion.3
  175.2 0.7 add_multiply_fusion
  (18 shorter events, 0.2 us)
Async XLA Ops:
  7.2 51.8 %copy-start = (bf16[1024,256]{1,0:T(8,128)(2,1)S(1)}, bf16[1024,256]{1,0:T(8,128)(2,1)}, u32[]{:S(2)}) copy-start(bf16[1024,256]{1,0:T(8,128)(2,1)} %param.11) | copy-start | bytes 1572868
  7.2 52.5 %all-gather.2.cloned.1.call-start = ((), (), s32[]{:S(2)}) async-start(), calls=%async_computation.5 | async-start | bytes 4718592 | tf_op jit(solution)/shard_map/all_gather | solution.py:107
  7.9 49.8 %copy-start.6 = (f32[2,4]{1,0:T(2,128)S(1)}, f32[2,4]{1,0:T(2,128)}, u32[]{:S(2)}) copy-start(f32[2,4]{1,0:T(2,128)} %param.9) | copy-start | bytes 100
  8.7 50.1 %copy-start.5 = (s32[2,16]{1,0:T(2,128)S(1)}, s32[2,16]{1,0:T(2,128)}, u32[]{:S(2)}) copy-start(s32[2,16]{1,0:T(2,128)} %param.10) | copy-start | bytes 388
  53.4 26.6 %all-to-all-start.1 = ((bf16[4,1024,256]{2,1,0:T(8,128)(2,1)}), bf16[4,1024,256]{2,1,0:T(8,128)(2,1)S(1)}, u32[]{:S(2)}, u32[]{:S(2)}) async-start(bf16[4,1024,256]{2,1,0:T(8,128)(2,1)} %broadcast_in_dim.19), calls=%async_computation.1 | async-start | bytes 4194304 | tf_op jit(solution)/shard_map/all_to_all | solution.py:95
  80.1 1.3 copy-start.1
  105.7 42.0 %copy-start.4 = (f32[8,1,128]{2,1,0:T(1,128)S(1)}, f32[8,1,128]{2,1,0:T(1,128)}, u32[]{:S(2)}) copy-start(f32[8,1,128]{2,1,0:T(1,128)} %all_to_all.26) | copy-start | bytes 12292
  134.6 40.6 %copy-start.3 = (f32[64,256]{1,0:T(8,128)S(1)}, f32[64,256]{1,0:T(8,128)}, u32[]{:S(2)}) copy-start(f32[64,256]{1,0:T(8,128)} %param.13) | copy-start | bytes 196612
  136.3 38.7 %all-to-all-start.4 = ((f16[16,64,256]{2,1,0:T(8,128)(2,1)}), f16[16,64,256]{2,1,0:T(8,128)(2,1)S(1)}, u32[]{:S(2)}, u32[]{:S(2)}) async-start(f16[16,64,256]{2,1,0:T(8,128)(2,1)} %multiply_convert_fusion), calls=%async_computation.4 | async-start | bytes 1048576 | tf_op jit(solution)/shard_map/all_to_all | solution.py:179
  175.2 0.7 copy-start.2
Sparse Core Ops, SparseCore 0:
  10.2 43.9 all-gather.1

commit v3 on v2

--- a/solution.py
+++ b/solution.py
@@ -14,7 +14,8 @@
 BF16 = jnp.bfloat16
 F16 = jnp.float16
 SCALE = 256.0
-VMEM_LIMIT = 60 * 1024 * 1024
+TAIL = 16
+VMEM_LIMIT = 40 * 1024 * 1024
 
 
 def params(**kw):
@@ -67,18 +68,45 @@
         sq_ref[...] = out
 
 
-def sum_kernel(sq_ref, h_ref, g_ref, c_ref, *, bound, recs):
-    rows = g_ref.shape[0] // recs
-    feats = h_ref.shape[2]
+def pack_kernel(sq_ref, g_ref, o_ref, *, bound):
+    rows = g_ref.shape[0]
     norms = jnp.sqrt(jnp.sum(sq_ref[...], axis=0, keepdims=True))
     clip = bound / jnp.maximum(norms, bound)
+    high = clip.astype(BF16).astype(F32)
+    mid = (clip - high).astype(BF16).astype(F32)
+    low = clip - high - mid
+    shape = (TAIL, clip.shape[1])
+    row = lax.broadcasted_iota(jnp.int32, shape, 0)
+    tail = jnp.zeros(shape, F32)
+    for k, term in enumerate((high, mid, low)):
+        tail = jnp.where(row == k, jnp.broadcast_to(term, shape), tail)
+    tail = jnp.concatenate([tail] * (o_ref.shape[2] // clip.shape[1]), axis=1).astype(BF16)
+    for k in range(o_ref.shape[0]):
+        o_ref[k, 0:rows, :] = g_ref[...]
+        o_ref[k, rows : rows + TAIL, :] = tail
+
+
+def sum_kernel(h_ref, g_ref, c_ref, *, recs):
+    i = pl.program_id(0)
+    rows = (g_ref.shape[1] - TAIL) // recs
+    feats = h_ref.shape[2]
+    tail = g_ref[0, recs * rows : recs * rows + TAIL, :].astype(F32)
+    clip = jnp.sum(tail, axis=0, keepdims=True)
     for j in range(h_ref.shape[0]):
         total = None
         for r in range(recs):
             at = slice(r * rows, (r + 1) * rows)
-            block = dot(h_ref[j, at, :], g_ref[at, :], 0, 0) * clip[0:1, r : r + 1]
+            block = dot(h_ref[j, at, :], g_ref[0, at, :], 0, 0) * clip[0:1, r : r + 1]
             total = block if total is None else total + block
-        c_ref[j * feats : (j + 1) * feats, :] = root(total)
+        out = slice(j * feats, (j + 1) * feats)
+
+        @pl.when(i == 0)
+        def _():
+            c_ref[out, :] = total
+
+        @pl.when(i > 0)
+        def _():
+            c_ref[out, :] += total
 
 
 def root(v):
@@ -104,9 +132,14 @@
     nx, nz = lax.axis_size("x"), lax.axis_size("z")
     bound = 2.0 * math.sqrt(D * DO)
 
-    full = lax.all_gather(acts.reshape(recs * rows, feats), tensor, axis=0, tiled=False)
+    own = acts.reshape(recs * rows, feats)
+    full = lax.all_gather(own, tensor, axis=0, tiled=False)
+    swap = [(a * nx + b, b * nx + a) for a in range(nx) for b in range(nx)]
+    swapped = lax.ppermute(own, ("x", "y"), swap)
 
     wz = gather(weight, "z").reshape(nz * weight.shape[0], local_out)
+    swapped, wz = lax.optimization_barrier((swapped, wz))
+    mine = lax.all_gather(swapped, tensor, axis=0, tiled=False)
     wfull = gather(wz, "x").reshape(D, local_out)
 
     vocab_ids = lax.broadcasted_iota(jnp.int32, (1, 1, emb.shape[0]), 2)
@@ -159,23 +192,30 @@
     sq_all = lax.all_to_all(sq.reshape(nt, 1, 128), tensor, 0, 0).reshape(nt, 128)
     norms = jnp.sqrt(jnp.sum(sq_all[:, :recs], axis=0))
 
-    partial = pl.pallas_call(
-        functools.partial(sum_kernel, bound=bound, recs=recs),
-        grid=(grid,),
-        in_specs=[whole(nt, 128), h_spec, whole(recs * rows, local_out)],
-        out_specs=pl.BlockSpec((step * feats, local_out), lambda i: (i, 0)),
-        out_shape=jax.ShapeDtypeStruct((D, local_out), F32),
+    packed = pl.pallas_call(
+        functools.partial(pack_kernel, bound=bound),
+        out_shape=jax.ShapeDtypeStruct((nx, recs * rows + TAIL, local_out), BF16),
+        compiler_params=params(),
+    )(sq_all, grads)
+    packed = lax.all_to_all(packed, "x", 0, 0)
+    here = pl.pallas_call(
+        functools.partial(sum_kernel, recs=recs),
+        grid=(nx,),
+        in_specs=[
+            pl.BlockSpec((nt // nx, recs * rows, feats), lambda i: (i, 0, 0)),
+            pl.BlockSpec((1, recs * rows + TAIL, local_out), lambda i: (i, 0, 0)),
+        ],
+        out_specs=whole(D // nx, local_out),
+        out_shape=jax.ShapeDtypeStruct((D // nx, local_out), F32),
         compiler_params=params(),
         cost_estimate=pl.CostEstimate(
             flops=2 * recs * rows * local_out * D,
-            bytes_accessed=2 * recs * rows * D + 2 * D * local_out,
+            bytes_accessed=2 * recs * rows * (D + nx * local_out) + 4 * D // nx * local_out,
             transcendentals=0,
         ),
-    )(sq_all, full, grads)
-
-    sent = partial.astype(F16).reshape(nx, D // nx, local_out)
-    sum_x = jnp.sum(unroot(lax.all_to_all(sent, "x", 0, 0)), axis=0)
-    sent = root(sum_x).astype(F16).reshape(nz, D // nx // nz, local_out)
+    )(mine, packed)
+
+    sent = root(here).astype(F16).reshape(nz, D // nx // nz, local_out)
     clipped_sum = jnp.sum(unroot(lax.all_to_all(sent, "z", 0, 0)), axis=0)
     total_recs = recs * nx * nz
     update = (clipped_sum + bound * noise) / total_recs

time: 183 us -> 175 us (0.956)
  blocking collectives: 81.9 us -> 28.2 us
  waiting for transfers between devices: 43.1 us -> 75.8 us
  starting transfers between devices: 15.6 us -> 34.3 us
  Pallas kernels: 16.9 us -> 7.6 us
  local copies, waits for them, and re-layouts: 5.19 us -> 11.6 us
  other arithmetic: 5.16 us -> 1.97 us
    all_to_all x2 -> x1, blocking collectives: 72.1 us -> 18.2 us  [on_device(): packed = lax.all_to_all(packed, 'x', 0, 0)]
    all_to_all x1 -> x2, waiting for transfers between devices: 15.6 us -> 40.2 us  [gather(): return lax.all_to_all(jnp.broadcast_to(v[None], (n,) + v.shape), axis, 0, 0)]
    all_to_all x1 -> x2, starting transfers between devices: 4.29 us -> 21.6 us  [gather(): return lax.all_to_all(jnp.broadcast_to(v[None], (n,) + v.shape), axis, 0, 0)]
    all_gather x1 -> x2, waiting for transfers between devices: 0.01 us -> 7.49 us  [the longest x1 7.49 us: on_device(): full = lax.all_gather(own, tensor, axis=0, tiled=False)]
    unnamed x14 -> x22, local copies, waits for them, and re-layouts: 1.34 us -> 7.55 us
    pallas_call x1, Pallas kernels: 5.85 us -> 2.43 us  [on_device(): pl.pallas_call(grad_kernel, grid=(grid,), in_specs=[h_spec, pl.BlockSpec(...]
    pallas_call x1 -> x2, Pallas kernels: 6.24 us -> 3.21 us  [the longest x1 3.13 us: on_device(): pl.pallas_call(functools.partial(sum_kernel, recs=recs), grid=(nx,), in_s...]
    pallas_call x1, Pallas kernels: 4.79 us -> 1.96 us  [on_device(): pl.pallas_call(gram_kernel, grid=(grid,), in_specs=[h_spec], out_specs=wh...]
  transfers between devices with their start and end apart: 3 -> 6, of which waited for: 2 -> 4; matrix products, arithmetic and copies ran while one was open for 3% -> 2% of each run, Pallas kernels for 3% -> 3%
where the time goes in v3:
time: 175 us; the launch traced here: 174 us
  waiting for transfers between devices  75.8 us (43%)
  starting transfers between devices  34.3 us (20%)
  blocking collectives  28.2 us (16%)
  between operations  14.2 us (8%)
  local copies, waits for them, and re-layouts  11.6 us (7%)
  Pallas kernels  7.6 us (4%)
  other arithmetic  1.97 us (1%)
    all_to_all x2, waiting for transfers between devices, gather(): return lax.all_to_all(jnp.broadcast_to(v[None], (n,) + v.shape), axis, 0, 0)  40.2 us
    all_to_all x1, waiting for transfers between devices, on_device(): clipped_sum = jnp.sum(unroot(lax.all_to_all(sent, 'z', 0, 0)), axis=0)  27.4 us
    all_to_all x2, starting transfers between devices, gather(): return lax.all_to_all(jnp.broadcast_to(v[None], (n,) + v.shape), axis, 0, 0)  21.6 us
    all_to_all x1, blocking collectives, on_device(): packed = lax.all_to_all(packed, 'x', 0, 0)  18.2 us
    all_to_all x1, starting transfers between devices, on_device(): clipped_sum = jnp.sum(unroot(lax.all_to_all(sent, 'z', 0, 0)), axis=0)  12 us
    all_to_all x1, blocking collectives, on_device(): lax.all_to_all(sq.reshape(nt, 1, 128), tensor, 0, 0).reshape(nt, 128)  10.1 us
    unnamed x22, local copies, waits for them, and re-layouts  7.55 us
    all_gather x1, waiting for transfers between devices, on_device(): full = lax.all_gather(own, tensor, axis=0, tiled=False)  7.49 us
  transfers between devices with their start and end apart: 6, of which 4 were waited for; matrix products, arithmetic and copies ran while one was open for 2% of the time, Pallas kernels for 3%

profile of v3, /device:TPU:32, one launch (start us, length us, event | category | flops | bytes accessed | tf_op | source)
XLA Modules:
  0.0 173.9 jit_solution(16024832775332460001)
XLA Ops:
  7.2 0.7 all-gather.4.cloned.1.call-update
  7.9 1.6 broadcast_in_dim.6
  9.5 15.2 %all-to-all-start = ((bf16[16,64,256]{2,1,0:T(8,128)(2,1)}), bf16[16,64,256]{2,1,0:T(8,128)(2,1)S(1)}, u32[]{:S(2)}, u32[]{:S(2)}) async-start(bf16[16,64,256]{2,1,0:T(8,128)(2,1)} %broadcast_in_dim.6), calls=%async_computation | async-start | bytes 1048576 | tf_op jit(solution)/shard_map/all_to_all | solution.py:123
  24.8 0.7 collective-permute-start
  25.5 27.5 %all-to-all-done = bf16[16,64,256]{2,1,0:T(8,128)(2,1)S(1)} async-done(((bf16[16,64,256]{2,1,0:T(8,128)(2,1)}), bf16[16,64,256]{2,1,0:T(8,128)(2,1)S(1)}, u32[]{:S(2)}, u32[]{:S(2)}) %all-to-all-start) | async-done | bytes 524320 | tf_op jit(solution)/shard_map/all_to_all | solution.py:123
  53.0 1.5 broadcast_in_dim.7
  54.6 6.4 %all-to-all-start.1 = ((bf16[4,1024,256]{2,1,0:T(8,128)(2,1)}), bf16[4,1024,256]{2,1,0:T(8,128)(2,1)S(1)}, u32[]{:S(2)}, u32[]{:S(2)}) async-start(bf16[4,1024,256]{2,1,0:T(8,128)(2,1)} %broadcast_in_dim.7), calls=%async_computation.1 | async-start | bytes 4194304 | tf_op jit(solution)/shard_map/all_to_all | solution.py:123
  61.1 0.2 broadcast_in_dim_reshape.4.t_ref
  61.6 7.5 %all-gather.4.cloned.1.call-done.h_ref = bf16[8,512,512]{2,1,0:T(8,128)(2,1)} async-done(((bf16[1,512,512]{2,1,0:T(8,128)(2,1)}), bf16[8,512,512]{2,1,0:T(8,128)(2,1)}) %all-gather.4.cloned.1.call-update) | async-done | bytes 4194320 | tf_op jit(solution)/shard_map/all_gather | solution.py:136
  69.1 2.2 %copy-done.1 = bf16[8,512,512]{2,1,0:T(8,128)(2,1)S(1)} copy-done((bf16[8,512,512]{2,1,0:T(8,128)(2,1)S(1)}, bf16[8,512,512]{2,1,0:T(8,128)(2,1)}, u32[]{:S(2)}) %copy-start.1) | copy-done | bytes 4194328
  71.3 2.0 %shard_map.94.gh_ref = f32[2,256,256]{2,1,0:T(8,128)S(1)} custom-call(bf16[8,512,512]{2,1,0:T(8,128)(2,1)S(1)} %copy-done.1), custom_call_target="tpu_custom_call" | custom-call | flops 1073741824 | bytes 4194304 | tf_op jit(solution)/shard_map/pallas_call | solution.py:156
  73.2 12.7 %all-to-all-done.1 = bf16[4,1024,256]{2,1,0:T(8,128)(2,1)S(1)} async-done(((bf16[4,1024,256]{2,1,0:T(8,128)(2,1)}), bf16[4,1024,256]{2,1,0:T(8,128)(2,1)S(1)}, u32[]{:S(2)}, u32[]{:S(2)}) %all-to-all-start.1) | async-done | bytes 2097184 | tf_op jit(solution)/shard_map/all_to_all | solution.py:123
  86.0 2.2 %copy-done.2 = bf16[8,512,512]{2,1,0:T(8,128)(2,1)S(1)} copy-done((bf16[8,512,512]{2,1,0:T(8,128)(2,1)S(1)}, bf16[8,512,512]{2,1,0:T(8,128)(2,1)}, u32[]{:S(2)}) %copy-start.2) | copy-done | bytes 4194328
  88.2 0.9 copy-done.4
  89.1 2.4 %shard_map.95 = (bf16[512,256]{1,0:T(8,128)(2,1)S(1)}, f32[8,128]{1,0:T(8,128)S(1)}) custom-call(bf16[8,512,512]{2,1,0:T(8,128)(2,1)S(1)} %copy-done.2, bf16[4096,256]{1,0:T(8,128)(2,1)S(1)} %bitcast.13, bf16[512,256]{1,0:T(8,128)(2,1)S(1)} %bitcast.15, f32[2,256]{1,0:T(2,128)S(1)} %fusion.4.b_ref, f32[512,1]{1,0:T(8,128)S(1)} %broadcast_in_dim_reshape.4.t_ref, ...), custom_call_target="tpu_custom_call" | custom-call | flops 1073741824 | bytes 6291456 | tf_op jit(solution)/shard_map/pallas_call | solution.py:167
  91.6 10.1 %all_to_all.25 = f32[8,1,128]{2,1,0:T(1,128)S(1)} all-to-all(f32[8,1,128]{2,1,0:T(1,128)S(1)} %bitcast.18), channel_id=1, replica_groups=mesh['x'=4,'z'=16,'y'=4,'core'=2] {'y','core'}, dimensions={0} | all-to-all | bytes 8192 | tf_op jit(solution)/shard_map/all_to_all | solution.py:192
  101.7 18.2 %all_to_all.26.g_ref = bf16[4,528,256]{2,1,0:T(8,128)(2,1)S(1)} all-to-all(bf16[4,528,256]{2,1,0:T(8,128)(2,1)S(1)} %shard_map.96), channel_id=1, replica_groups=mesh['x'=4,'z'=16,'y'=4,'core'=2] {'x'}, dimensions={0} | all-to-all | bytes 2162688 | tf_op jit(solution)/shard_map/all_to_all | solution.py:200
  119.9 2.2 %copy-done.3 = bf16[4096,512]{1,0:T(8,128)(2,1)S(1)} copy-done((bf16[4096,512]{1,0:T(8,128)(2,1)S(1)}, bf16[4096,512]{1,0:T(8,128)(2,1)}, u32[]{:S(2)}) %copy-start.3) | copy-done | bytes 4194328
  122.1 3.1 %shard_map.97 = f32[1024,256]{1,0:T(8,128)S(1)} custom-call(bf16[8,512,512]{2,1,0:T(8,128)(2,1)S(1)} %bitcast.14, bf16[4,528,256]{2,1,0:T(8,128)(2,1)S(1)} %all_to_all.26.g_ref), custom_call_target="tpu_custom_call" | custom-call | flops 1073741824 | bytes 6291456 | tf_op jit(solution)/shard_map/pallas_call | solution.py:201
  125.2 1.0 multiply_convert_fusion
  126.2 12.0 %all-to-all-start.4 = ((f16[16,64,256]{2,1,0:T(8,128)(2,1)}), f16[16,64,256]{2,1,0:T(8,128)(2,1)S(1)}, u32[]{:S(2)}, u32[]{:S(2)}) async-start(f16[16,64,256]{2,1,0:T(8,128)(2,1)} %bitcast.9), calls=%async_computation.4 | async-start | bytes 1048576 | tf_op jit(solution)/shard_map/all_to_all | solution.py:219
  138.3 0.5 sqrt.3
  138.8 27.4 %all-to-all-done.4 = f16[16,64,256]{2,1,0:T(8,128)(2,1)S(1)} async-done(((f16[16,64,256]{2,1,0:T(8,128)(2,1)}), f16[16,64,256]{2,1,0:T(8,128)(2,1)S(1)}, u32[]{:S(2)}, u32[]{:S(2)}) %all-to-all-start.4) | async-done | bytes 524320 | tf_op jit(solution)/shard_map/all_to_all | solution.py:219
  166.4 0.6 add_multiply_fusion
  (31 shorter events, 0.8 us)
Async XLA Ops:
  7.2 54.2 %copy-start = (bf16[1024,256]{1,0:T(8,128)(2,1)S(1)}, bf16[1024,256]{1,0:T(8,128)(2,1)}, u32[]{:S(2)}) copy-start(bf16[1024,256]{1,0:T(8,128)(2,1)} %param.11) | copy-start | bytes 1572868
  7.2 17.6 %copy-start.5 = (bf16[2,4,64,512]{3,2,1,0:T(8,128)(2,1)S(1)}, bf16[2,4,64,512]{3,2,1,0:T(8,128)(2,1)}, u32[]{:S(2)}) copy-start(bf16[2,4,64,512]{3,2,1,0:T(8,128)(2,1)} %param.7) | copy-start | bytes 1572868
  7.2 61.9 %all-gather.4.cloned.1.call-start = ((), (), s32[]{:S(2)}) async-start(), calls=%async_computation.5 | async-start | bytes 4718592 | tf_op jit(solution)/shard_map/all_gather | solution.py:136
  9.5 43.5 %all-to-all-start = ((bf16[16,64,256]{2,1,0:T(8,128)(2,1)}), bf16[16,64,256]{2,1,0:T(8,128)(2,1)S(1)}, u32[]{:S(2)}, u32[]{:S(2)}) async-start(bf16[16,64,256]{2,1,0:T(8,128)(2,1)} %broadcast_in_dim.6), calls=%async_computation | async-start | bytes 1048576 | tf_op jit(solution)/shard_map/all_to_all | solution.py:123
  24.8 95.1 %all-gather.6.cloned.1.call-start = ((), (), s32[]{:S(2)}) async-start(), calls=%async_computation.6 | async-start | bytes 4718592 | tf_op jit(solution)/shard_map/all_gather | solution.py:142
  24.8 0.7 collective-permute-start
  25.5 27.5 %copy-start.6 = (bf16[512,512]{1,0:T(8,128)(2,1)}, bf16[512,512]{1,0:T(8,128)(2,1)S(1)}, u32[]{:S(2)}) copy-start(bf16[512,512]{1,0:T(8,128)(2,1)S(1)} %collective-permute-done) | copy-start | bytes 1572868
  54.5 6.4 %copy-start.10 = (f32[2,4]{1,0:T(2,128)S(1)}, f32[2,4]{1,0:T(2,128)}, u32[]{:S(2)}) copy-start(f32[2,4]{1,0:T(2,128)} %param.9) | copy-start | bytes 100
  54.6 6.7 %copy-start.9 = (s32[2,16]{1,0:T(2,128)S(1)}, s32[2,16]{1,0:T(2,128)}, u32[]{:S(2)}) copy-start(s32[2,16]{1,0:T(2,128)} %param.10) | copy-start | bytes 388
  54.6 31.4 %all-to-all-start.1 = ((bf16[4,1024,256]{2,1,0:T(8,128)(2,1)}), bf16[4,1024,256]{2,1,0:T(8,128)(2,1)S(1)}, u32[]{:S(2)}, u32[]{:S(2)}) async-start(bf16[4,1024,256]{2,1,0:T(8,128)(2,1)} %broadcast_in_dim.7), calls=%async_computation.1 | async-start | bytes 4194304 | tf_op jit(solution)/shard_map/all_to_all | solution.py:123
  69.1 2.2 %copy-start.1 = (bf16[8,512,512]{2,1,0:T(8,128)(2,1)S(1)}, bf16[8,512,512]{2,1,0:T(8,128)(2,1)}, u32[]{:S(2)}) copy-start(bf16[8,512,512]{2,1,0:T(8,128)(2,1)} %all-gather.4.cloned.1.call-done.h_ref) | copy-start | bytes 12582916
  86.0 2.2 %copy-start.2 = (bf16[8,512,512]{2,1,0:T(8,128)(2,1)S(1)}, bf16[8,512,512]{2,1,0:T(8,128)(2,1)}, u32[]{:S(2)}) copy-start(bf16[8,512,512]{2,1,0:T(8,128)(2,1)} %all-gather.4.cloned.1.call-done.h_ref) | copy-start | bytes 12582916
  88.2 0.9 copy-start.4
  119.9 2.2 %copy-start.3 = (bf16[4096,512]{1,0:T(8,128)(2,1)S(1)}, bf16[4096,512]{1,0:T(8,128)(2,1)}, u32[]{:S(2)}) copy-start(bf16[4096,512]{1,0:T(8,128)(2,1)} %all-gather.6.cloned.1.call-done) | copy-start | bytes 12582916
  125.2 41.1 %copy-start.8 = (f32[64,256]{1,0:T(8,128)S(1)}, f32[64,256]{1,0:T(8,128)}, u32[]{:S(2)}) copy-start(f32[64,256]{1,0:T(8,128)} %param.13) | copy-start | bytes 196612
  126.2 39.9 %all-to-all-start.4 = ((f16[16,64,256]{2,1,0:T(8,128)(2,1)}), f16[16,64,256]{2,1,0:T(8,128)(2,1)S(1)}, u32[]{:S(2)}, u32[]{:S(2)}) async-start(f16[16,64,256]{2,1,0:T(8,128)(2,1)} %bitcast.9), calls=%async_computation.4 | async-start | bytes 1048576 | tf_op jit(solution)/shard_map/all_to_all | solution.py:219
  166.4 0.7 copy-start.7
Sparse Core Ops, SparseCore 0:
  10.2 58.8 all-gather.3
  71.2 41.9 all-gather.5

commit v4 on v3

v4 whole, which is shorter than its diff:
```python
import functools
import math

import jax
import jax.numpy as jnp
from jax import lax
from jax.experimental import pallas as pl
from jax.experimental.pallas import tpu as pltpu
from jax.sharding import Mesh, PartitionSpec as P

D = 4096
DO = 2048
F32 = jnp.float32
BF16 = jnp.bfloat16
F16 = jnp.float16
SCALE = 256.0
TAIL = 16
MIB = 1024 * 1024


def params(mib=40):
    return pltpu.CompilerParams(vmem_limit_bytes=mib * MIB)


def dot(a, b, ca, cb):
    return lax.dot_general(a, b, (((ca,), (cb,)), ((), ())), preferred_element_type=F32)


def gram_kernel(h_ref, o_ref):
    @pl.when(pl.program_id(0) == 0)
    def _():
        o_ref[...] = jnp.zeros_like(o_ref)

    recs, rows, _ = o_ref.shape
    for j in range(h_ref.shape[0]):
        for r in range(recs):
            h = h_ref[j, r * rows : (r + 1) * rows, :]
            o_ref[r] += dot(h, h, 1, 1)


def fetch(src, dst, sems):
    copies = [pltpu.make_async_copy(src.at[j], dst.at[j], sems.at[j]) for j in range(dst.shape[0])]
    for copy in copies:
        copy.start()
    return copies


def grad_kernel(h_hbm, w_ref, n_hbm, b_ref, t_ref, gh_ref, g_ref, sq_ref, h_buf, n_buf, acc, h_sems, n_sems):
    blocks, _, feats = h_buf.shape
    h_copies = fetch(h_hbm, h_buf, h_sems)
    n_copies = fetch(n_hbm, n_buf, n_sems)
    for j in range(blocks):
        h_copies[j].wait()
        part = dot(h_buf[j], w_ref[j * feats : (j + 1) * feats, :], 1, 0)
        if j == 0:
            acc[...] = part
        else:
            acc[...] += part

    recs, rows, _ = gh_ref.shape
    lane = lax.broadcasted_iota(jnp.int32, sq_ref.shape, 1)
    out = jnp.zeros(sq_ref.shape, F32)
    for r in range(recs):
        at = slice(r * rows, (r + 1) * rows)
        n_copies[r].wait()
        pred = acc[at, :] + b_ref[r : r + 1, :]
        g = (t_ref[at, :] * (pred - n_buf[r].astype(F32))).astype(BF16)
        g_ref[at, :] = g
        out = jnp.where(lane == r, jnp.sum(gh_ref[r] * dot(g, g, 1, 1)), out)
    sq_ref[...] = out


def pack_kernel(sq_ref, g_ref, o_ref, *, bound):
    rows = g_ref.shape[0]
    norms = jnp.sqrt(jnp.sum(sq_ref[...], axis=0, keepdims=True))
    clip = bound / jnp.maximum(norms, bound)
    high = clip.astype(BF16).astype(F32)
    mid = (clip - high).astype(BF16).astype(F32)
    low = clip - high - mid
    shape = (TAIL, clip.shape[1])
    row = lax.broadcasted_iota(jnp.int32, shape, 0)
    tail = jnp.zeros(shape, F32)
    for k, term in enumerate((high, mid, low)):
        tail = jnp.where(row == k, jnp.broadcast_to(term, shape), tail)
    tail = jnp.concatenate([tail] * (o_ref.shape[2] // clip.shape[1]), axis=1).astype(BF16)
    for k in range(o_ref.shape[0]):
        o_ref[k, 0:rows, :] = g_ref[...]
        o_ref[k, rows : rows + TAIL, :] = tail


def sum_kernel(h_hbm, g_ref, c_ref, h_buf, acc, sems, *, recs):
    copies = fetch(h_hbm, h_buf, sems)
    blocks, total_rows, feats = h_buf.shape
    nx = g_ref.shape[0]
    rows = total_rows // recs
    per = blocks // nx
    for x in range(nx):
        tail = g_ref[x, total_rows : total_rows + TAIL, :].astype(F32)
        clip = jnp.sum(tail, axis=0, keepdims=True)
        for j in range(per):
            copies[x * per + j].wait()
            total = None
            for r in range(recs):
                at = slice(r * rows, (r + 1) * rows)
                block = dot(h_buf[x * per + j, at, :], g_ref[x, at, :], 0, 0) * clip[0:1, r : r + 1]
                total = block if total is None else total + block
            out = slice(j * feats, (j + 1) * feats)
            if x == 0:
                acc[out, :] = total
            else:
                acc[out, :] += total
    zl, zh, size, _ = c_ref.shape
    for b in range(zl):
        for a in range(zh):
            at = (a * zl + b) * size
            c_ref[b, a] = acc[at : at + size, :]


def root(v):
    return v * lax.rsqrt(jnp.maximum(jnp.abs(v), 1e-30)) * SCALE


def unroot(v):
    v = v.astype(F32)
    return v * jnp.abs(v) * (1.0 / (SCALE * SCALE))


def gather(v, axis):
    n = lax.axis_size(axis)
    return lax.all_to_all(jnp.broadcast_to(v[None], (n,) + v.shape), axis, 0, 0)


def on_device(acts, noise_draws, times, cond, emb, weight, noise):
    recs, draws, events, feats = acts.shape
    rows = draws * events
    local_out = weight.shape[1]
    tensor = ("y", "core")
    nt = lax.axis_size("y") * lax.axis_size("core")
    nx, nh, nl = lax.axis_size("x"), lax.axis_size("zh"), lax.axis_size("zl")
    nz = nh * nl
    bound = 2.0 * math.sqrt(D * DO)

    own = acts.reshape(recs * rows, feats)
    full = lax.all_gather(own, tensor, axis=0, tiled=False)
    swap = [(a * nx + b, b * nx + a) for a in range(nx) for b in range(nx)]
    swapped = lax.ppermute(own, ("x", "y"), swap)

    wz = lax.all_gather(weight, ("zh", "zl"), axis=0, tiled=True)
    swapped, wz = lax.optimization_barrier((swapped, wz))
    mine = lax.all_gather(swapped, tensor, axis=0, tiled=False)
    wfull = gather(wz, "x").reshape(D, local_out)

    vocab_ids = lax.broadcasted_iota(jnp.int32, (1, 1, emb.shape[0]), 2)
    counts = jnp.sum((cond[:, :, None] == vocab_ids).astype(F32), axis=1).astype(BF16)
    bias = jnp.dot(counts, emb, preferred_element_type=F32)
    wrow = jnp.repeat(
        (1.0 / (times + 0.25)).reshape(recs * draws) * (1.0 / math.sqrt(rows)), events
    )[:, None]

    step = 2
    grid = nt // step
    h_spec = pl.BlockSpec((step, recs * rows, feats), lambda i: (i, 0, 0))
    whole = lambda *shape: pl.BlockSpec(shape, lambda i: (0,) * len(shape))
    gram_h = pl.pallas_call(
        gram_kernel,
        grid=(grid,),
        in_specs=[h_spec],
        out_specs=whole(recs, rows, rows),
        out_shape=jax.ShapeDtypeStruct((recs, rows, rows), F32),
        compiler_params=params(),
        cost_estimate=pl.CostEstimate(
            flops=2 * recs * rows * rows * D, bytes_accessed=2 * recs * rows * D, transcendentals=0
        ),
    )(full)
    vmem = pl.BlockSpec(memory_space=pltpu.VMEM)
    hbm = pl.BlockSpec(memory_space=pltpu.HBM)
    grads, sq = pl.pallas_call(
        grad_kernel,
        in_specs=[hbm, vmem, hbm, vmem, vmem, vmem],
        out_specs=[vmem, vmem],
        out_shape=[
            jax.ShapeDtypeStruct((recs * rows, local_out), BF16),
            jax.ShapeDtypeStruct((nt, 128), F32),
        ],
        scratch_shapes=[
            pltpu.VMEM((nt, recs * rows, feats), BF16),
            pltpu.VMEM((recs, rows, local_out), BF16),
            pltpu.VMEM((recs * rows, local_out), F32),
            pltpu.SemaphoreType.DMA((nt,)),
            pltpu.SemaphoreType.DMA((recs,)),
        ],
        compiler_params=params(51),
        cost_estimate=pl.CostEstimate(
            flops=2 * recs * rows * local_out * D,
            bytes_accessed=2 * recs * rows * D + 2 * D * local_out,
            transcendentals=0,
        ),
    )(full, wfull, noise_draws.reshape(recs, rows, local_out), bias, wrow, gram_h)

    sq_all = lax.all_to_all(sq.reshape(nt, 1, 128), tensor, 0, 0).reshape(nt, 128)
    norms = jnp.sqrt(jnp.sum(sq_all[:, :recs], axis=0))

    packed = pl.pallas_call(
        functools.partial(pack_kernel, bound=bound),
        out_shape=jax.ShapeDtypeStruct((nx, recs * rows + TAIL, local_out), BF16),
        compiler_params=params(),
    )(sq_all, grads)
    packed = lax.all_to_all(packed, "x", 0, 0)
    block = weight.shape[0]
    here = pl.pallas_call(
        functools.partial(sum_kernel, recs=recs),
        in_specs=[hbm, vmem],
        out_specs=vmem,
        out_shape=jax.ShapeDtypeStruct((nl, nh, block, local_out), F32),
        scratch_shapes=[
            pltpu.VMEM((nt, recs * rows, feats), BF16),
            pltpu.VMEM((D // nx, local_out), F32),
            pltpu.SemaphoreType.DMA((nt,)),
        ],
        compiler_params=params(51),
        cost_estimate=pl.CostEstimate(
            flops=2 * recs * rows * local_out * D,
            bytes_accessed=2 * recs * rows * (D + nx * local_out) + 4 * D // nx * local_out,
            transcendentals=0,
        ),
    )(mine.reshape(nt, recs * rows, feats), packed)

    sent = root(here).astype(F16)
    sum_l = jnp.sum(unroot(lax.all_to_all(sent, "zl", 0, 0)), axis=0)
    sent = root(sum_l).astype(F16)
    clipped_sum = jnp.sum(unroot(lax.all_to_all(sent, "zh", 0, 0)), axis=0)
    total_recs = recs * nx * nz
    update = (clipped_sum + bound * noise) / total_recs
    return (clipped_sum, update, norms)


def solution(mesh):
    grid = Mesh(mesh.devices.reshape(4, 4, 4, 4, 2), ("x", "zh", "zl", "y", "core"))
    dp, tensor = ("x", "zh", "zl"), ("y", "core")
    in_specs = (
        P(dp, None, None, tensor),
        P(dp, None, None, tensor),
        P(dp, None),
        P(dp, None),
        P(None, tensor),
        P(dp, tensor),
        P(dp, tensor),
    )
    out_specs = (P(dp, tensor), P(dp, tensor), P(dp))
    return jax.shard_map(
        on_device, mesh=grid, in_specs=in_specs, out_specs=out_specs, check_vma=False
    )
```

time: 175 us -> 166 us (0.949)
  the two profiles are of different devices: /device:TPU:32 before, /device:TPU:1 now
where the time goes in v4:
time: 166 us; the launch traced here: 165 us
  blocking collectives  63.1 us (38%)
  waiting for transfers between devices  44.6 us (27%)
  starting transfers between devices  22.4 us (13%)
  between operations  14.2 us (9%)
  Pallas kernels  13.2 us (8%)
  local copies, waits for them, and re-layouts  5.39 us (3%)
  other arithmetic  1.94 us (1%)
    all_gather x1, blocking collectives, on_device(): wz = lax.all_gather(weight, ('zh', 'zl'), axis=0, tiled=True)  32.5 us
    all_to_all x1, blocking collectives, on_device(): sum_l = jnp.sum(unroot(lax.all_to_all(sent, 'zl', 0, 0)), axis=0)  16 us
    all_to_all x1, blocking collectives, on_device(): lax.all_to_all(sq.reshape(nt, 1, 128), tensor, 0, 0).reshape(nt, 128)  14.7 us
    all_to_all x1, waiting for transfers between devices, gather(): return lax.all_to_all(jnp.broadcast_to(v[None], (n,) + v.shape), axis, 0, 0)  14.1 us
    all_to_all x1, waiting for transfers between devices, on_device(): packed = lax.all_to_all(packed, 'x', 0, 0)  13.5 us
    all_to_all x1, waiting for transfers between devices, on_device(): clipped_sum = jnp.sum(unroot(lax.all_to_all(sent, 'zh', 0, 0)), axis=0)  12.9 us
    all_to_all x1, starting transfers between devices, gather(): return lax.all_to_all(jnp.broadcast_to(v[None], (n,) + v.shape), axis, 0, 0)  9.69 us
    all_to_all x1, starting transfers between devices, on_device(): clipped_sum = jnp.sum(unroot(lax.all_to_all(sent, 'zh', 0, 0)), axis=0)  7.39 us
  transfers between devices with their start and end apart: 6, of which 5 were waited for; matrix products, arithmetic and copies ran while one was open for 2% of the time, Pallas kernels for 6%

profile of v4, /device:TPU:1, one launch (start us, length us, event | category | flops | bytes accessed | tf_op | source)
XLA Modules:
  0.0 164.9 jit_solution(12801749893924793261)
XLA Ops:
  7.2 0.7 all-gather.4.cloned.1.call-update
  8.0 1.7 %collective-permute-start = (bf16[512,512]{1,0:T(8,128)(2,1)}, bf16[512,512]{1,0:T(8,128)(2,1)S(1)}, u32[]{:S(2)}, u32[]{:S(2)}) collective-permute-start(bf16[512,512]{1,0:T(8,128)(2,1)} %bitcast.17), channel_id=1, source_target_pairs={{0,0},{2,128},{4,256},{6,384},{128,2},{130,130},{132,258},{134,386... | collective-permute-start | bytes 1572872 | tf_op jit(solution)/shard_map/ppermute | solution.py:146
  9.7 32.5 %all_gather.12 = bf16[1024,256]{1,0:T(8,128)(2,1)S(1)} all-gather(bf16[64,256]{1,0:T(8,128)(2,1)} %param.12), channel_id=1, replica_groups=mesh['x'=4,'zh'=4,'zl'=4,'y'=4,'core'=2] {'zh','zl'}, dimensions={0}, use_global_device_ids=true | all-gather | bytes 557056 | tf_op jit(solution)/shard_map/all_gather | solution.py:148
  42.1 0.8 copy-done.3
  43.0 1.5 broadcast_in_dim.4
  44.4 9.7 %all-to-all-start = ((bf16[4,1024,256]{2,1,0:T(8,128)(2,1)}), bf16[4,1024,256]{2,1,0:T(8,128)(2,1)}, u32[]{:S(2)}, u32[]{:S(2)}) async-start(bf16[4,1024,256]{2,1,0:T(8,128)(2,1)} %broadcast_in_dim.4), calls=%async_computation | async-start | bytes 4194304 | tf_op jit(solution)/shard_map/all_to_all | solution.py:130
  54.8 1.9 %all-gather.4.cloned.1.call-done.h_ref.h_hbm = bf16[8,512,512]{2,1,0:T(8,128)(2,1)} async-done(((bf16[1,512,512]{2,1,0:T(8,128)(2,1)}), bf16[8,512,512]{2,1,0:T(8,128)(2,1)}) %all-gather.4.cloned.1.call-update) | async-done | bytes 4194320 | tf_op jit(solution)/shard_map/all_gather | solution.py:144
  56.7 2.2 %copy-done.1 = bf16[8,512,512]{2,1,0:T(8,128)(2,1)S(1)} copy-done((bf16[8,512,512]{2,1,0:T(8,128)(2,1)S(1)}, bf16[8,512,512]{2,1,0:T(8,128)(2,1)}, u32[]{:S(2)}) %copy-start.1) | copy-done | bytes 4194328
  58.9 2.0 %shard_map.94.gh_ref = f32[2,256,256]{2,1,0:T(8,128)S(1)} custom-call(bf16[8,512,512]{2,1,0:T(8,128)(2,1)S(1)} %copy-done.1), custom_call_target="tpu_custom_call" | custom-call | flops 1073741824 | bytes 4194304 | tf_op jit(solution)/shard_map/pallas_call | solution.py:164
  60.9 14.1 %all-to-all-done = bf16[4,1024,256]{2,1,0:T(8,128)(2,1)} async-done(((bf16[4,1024,256]{2,1,0:T(8,128)(2,1)}), bf16[4,1024,256]{2,1,0:T(8,128)(2,1)}, u32[]{:S(2)}, u32[]{:S(2)}) %all-to-all-start) | async-done | bytes 2097184 | tf_op jit(solution)/shard_map/all_to_all | solution.py:130
  75.0 6.2 %shard_map.95 = (bf16[512,256]{1,0:T(8,128)(2,1)S(1)}, f32[8,128]{1,0:T(8,128)S(1)}) custom-call(bf16[8,512,512]{2,1,0:T(8,128)(2,1)} %all-gather.4.cloned.1.call-done.h_ref.h_hbm, bf16[4096,256]{1,0:T(8,128)(2,1)} %bitcast.3.w_ref, bf16[2,256,256]{2,1,0:T(8,128)(2,1)S(1)} %bitcast.11, f32[2,256]{1,0:T(2,128)S(1)} %fusion.6.b_ref, ...), custom_call_target="tpu_custom_call" | custom-call | flops 1073741824 | bytes 6291456 | tf_op jit(solution)/shard_map/pallas_call | solution.py:177
  81.2 14.7 %all_to_all.25 = f32[8,1,128]{2,1,0:T(1,128)S(1)} all-to-all(f32[8,1,128]{2,1,0:T(1,128)S(1)} %bitcast.14), channel_id=1, replica_groups=mesh['x'=4,'zh'=4,'zl'=4,'y'=4,'core'=2] {'y','core'}, dimensions={0} | all-to-all | bytes 8192 | tf_op jit(solution)/shard_map/all_to_all | solution.py:200
  95.9 1.1 shard_map.96
  97.0 3.5 %all-to-all-start.2 = ((bf16[4,528,256]{2,1,0:T(8,128)(2,1)}), bf16[4,528,256]{2,1,0:T(8,128)(2,1)S(1)}, u32[]{:S(2)}, u32[]{:S(2)}) async-start(bf16[4,528,256]{2,1,0:T(8,128)(2,1)} %shard_map.96), calls=%async_computation.2 | async-start | bytes 2162688 | tf_op jit(solution)/shard_map/all_to_all | solution.py:208
  100.5 1.5 all-gather.6.cloned.1.call-done
  102.0 13.5 %all-to-all-done.2.g_ref = bf16[4,528,256]{2,1,0:T(8,128)(2,1)S(1)} async-done(((bf16[4,528,256]{2,1,0:T(8,128)(2,1)}), bf16[4,528,256]{2,1,0:T(8,128)(2,1)S(1)}, u32[]{:S(2)}, u32[]{:S(2)}) %all-to-all-start.2) | async-done | bytes 1081376 | tf_op jit(solution)/shard_map/all_to_all | solution.py:208
  115.4 3.9 %shard_map.97 = f32[4,4,64,256]{3,2,1,0:T(8,128)S(1)} custom-call(bf16[8,512,512]{2,1,0:T(8,128)(2,1)} %bitcast.15, bf16[4,528,256]{2,1,0:T(8,128)(2,1)S(1)} %all-to-all-done.2.g_ref), custom_call_target="tpu_custom_call" | custom-call | flops 1073741824 | bytes 6291456 | tf_op jit(solution)/shard_map/pallas_call | solution.py:210
  119.4 0.2 multiply_convert_fusion
  119.7 16.0 %all_to_all.26 = f16[4,4,64,256]{3,2,1,0:T(8,128)(2,1)S(1)} all-to-all(f16[4,4,64,256]{3,2,1,0:T(8,128)(2,1)S(1)} %multiply_convert_fusion), channel_id=1, replica_groups=mesh['x'=4,'zh'=4,'zl'=4,'y'=4,'core'=2] {'zl'}, dimensions={0} | all-to-all | bytes 1048576 | tf_op jit(solution)/shard_map/all_to_all | solution.py:229
  135.8 0.7 multiply_convert_fusion.1
  136.5 7.4 %all-to-all-start.4 = ((f16[4,64,256]{2,1,0:T(8,128)(2,1)}), f16[4,64,256]{2,1,0:T(8,128)(2,1)S(1)}, u32[]{:S(2)}, u32[]{:S(2)}) async-start(f16[4,64,256]{2,1,0:T(8,128)(2,1)} %multiply_convert_fusion.1), calls=%async_computation.4 | async-start | bytes 262144 | tf_op jit(solution)/shard_map/all_to_all | solution.py:231
  143.9 0.5 sqrt.3
  144.4 12.9 %all-to-all-done.4 = f16[4,64,256]{2,1,0:T(8,128)(2,1)S(1)} async-done(((f16[4,64,256]{2,1,0:T(8,128)(2,1)}), f16[4,64,256]{2,1,0:T(8,128)(2,1)S(1)}, u32[]{:S(2)}, u32[]{:S(2)}) %all-to-all-start.4) | async-done | bytes 131104 | tf_op jit(solution)/shard_map/all_to_all | solution.py:231
  157.4 0.7 add_multiply_fusion
  (27 shorter events, 1.0 us)
Async XLA Ops:
  7.2 47.5 %copy-start = (bf16[1024,256]{1,0:T(8,128)(2,1)S(1)}, bf16[1024,256]{1,0:T(8,128)(2,1)}, u32[]{:S(2)}) copy-start(bf16[1024,256]{1,0:T(8,128)(2,1)} %param.11) | copy-start | bytes 1572868
  7.2 49.5 %all-gather.4.cloned.1.call-start = ((), (), s32[]{:S(2)}) async-start(), calls=%async_computation.5 | async-start | bytes 4718592 | tf_op jit(solution)/shard_map/all_gather | solution.py:144
  7.9 94.1 %all-gather.6.cloned.1.call-start = ((), (), s32[]{:S(2)}) async-start(), calls=%async_computation.6 | async-start | bytes 4718592 | tf_op jit(solution)/shard_map/all_gather | solution.py:150
  8.0 34.2 %collective-permute-start = (bf16[512,512]{1,0:T(8,128)(2,1)}, bf16[512,512]{1,0:T(8,128)(2,1)S(1)}, u32[]{:S(2)}, u32[]{:S(2)}) collective-permute-start(bf16[512,512]{1,0:T(8,128)(2,1)} %bitcast.17), channel_id=1, source_target_pairs={{0,0},{2,128},{4,256},{6,384},{128,2},{130,130},{132,258},{134,386... | collective-permute-start | bytes 1572872 | tf_op jit(solution)/shard_map/ppermute | solution.py:146
  42.1 0.8 copy-start.3
  44.4 9.7 %copy-start.7 = (f32[2,4]{1,0:T(2,128)S(1)}, f32[2,4]{1,0:T(2,128)}, u32[]{:S(2)}) copy-start(f32[2,4]{1,0:T(2,128)} %param.9) | copy-start | bytes 100
  44.4 10.1 %copy-start.6 = (s32[2,16]{1,0:T(2,128)S(1)}, s32[2,16]{1,0:T(2,128)}, u32[]{:S(2)}) copy-start(s32[2,16]{1,0:T(2,128)} %param.10) | copy-start | bytes 388
  44.4 30.6 %all-to-all-start = ((bf16[4,1024,256]{2,1,0:T(8,128)(2,1)}), bf16[4,1024,256]{2,1,0:T(8,128)(2,1)}, u32[]{:S(2)}, u32[]{:S(2)}) async-start(bf16[4,1024,256]{2,1,0:T(8,128)(2,1)} %broadcast_in_dim.4), calls=%async_computation | async-start | bytes 4194304 | tf_op jit(solution)/shard_map/all_to_all | solution.py:130
  56.7 2.2 %copy-start.1 = (bf16[8,512,512]{2,1,0:T(8,128)(2,1)S(1)}, bf16[8,512,512]{2,1,0:T(8,128)(2,1)}, u32[]{:S(2)}) copy-start(bf16[8,512,512]{2,1,0:T(8,128)(2,1)} %all-gather.4.cloned.1.call-done.h_ref.h_hbm) | copy-start | bytes 12582916
  58.9 16.1 %copy-start.2 = (bf16[2,4,64,256]{3,2,1,0:T(8,128)(2,1)S(1)}, bf16[2,4,64,256]{3,2,1,0:T(8,128)(2,1)}, u32[]{:S(2)}) copy-start(bf16[2,4,64,256]{3,2,1,0:T(8,128)(2,1)} %param.8) | copy-start | bytes 786436
  97.0 18.4 %all-to-all-start.2 = ((bf16[4,528,256]{2,1,0:T(8,128)(2,1)}), bf16[4,528,256]{2,1,0:T(8,128)(2,1)S(1)}, u32[]{:S(2)}, u32[]{:S(2)}) async-start(bf16[4,528,256]{2,1,0:T(8,128)(2,1)} %shard_map.96), calls=%async_computation.2 | async-start | bytes 2162688 | tf_op jit(solution)/shard_map/all_to_all | solution.py:208
  119.4 38.0 %copy-start.5 = (f32[64,256]{1,0:T(8,128)S(1)}, f32[64,256]{1,0:T(8,128)}, u32[]{:S(2)}) copy-start(f32[64,256]{1,0:T(8,128)} %param.13) | copy-start | bytes 196612
  136.5 20.9 %all-to-all-start.4 = ((f16[4,64,256]{2,1,0:T(8,128)(2,1)}), f16[4,64,256]{2,1,0:T(8,128)(2,1)S(1)}, u32[]{:S(2)}, u32[]{:S(2)}) async-start(f16[4,64,256]{2,1,0:T(8,128)(2,1)} %multiply_convert_fusion.1), calls=%async_computation.4 | async-start | bytes 262144 | tf_op jit(solution)/shard_map/all_to_all | solution.py:231
  157.4 0.7 copy-start.4
Sparse Core Ops, SparseCore 0:
  10.2 46.4 all-gather.3
  58.9 43.0 all-gather.5

commit v5 on v4

v5 whole, which is shorter than its diff:
```python
import functools
import math

import jax
import jax.numpy as jnp
from jax import lax
from jax.experimental import pallas as pl
from jax.experimental.pallas import tpu as pltpu
from jax.sharding import Mesh, PartitionSpec as P

D = 4096
DO = 2048
F32 = jnp.float32
BF16 = jnp.bfloat16
F16 = jnp.float16
SCALE = 256.0
TAIL = 16
MIB = 1024 * 1024


def params(mib=40):
    return pltpu.CompilerParams(vmem_limit_bytes=mib * MIB)


def dot(a, b, ca, cb):
    return lax.dot_general(a, b, (((ca,), (cb,)), ((), ())), preferred_element_type=F32)


def fetch(src, dst, sems):
    copies = [pltpu.make_async_copy(src.at[j], dst.at[j], sems.at[j]) for j in range(dst.shape[0])]
    for copy in copies:
        copy.start()
    return copies


def grad_kernel(*refs):
    h_hbm, n_hbm, b_ref, t_ref = refs[:4]
    w_refs, (g_ref, sq_ref, h_buf, n_buf, h_sems, n_sems) = refs[4:-6], refs[-6:]
    total_rows, feats = h_buf.shape[1:]
    recs, rows, _ = n_buf.shape
    nx = len(w_refs) // 2
    h_copies = fetch(h_hbm, h_buf, h_sems)
    n_copies = fetch(n_hbm, n_buf, n_sems)
    for copy in h_copies:
        copy.wait()
    here = lax.axis_index("x")
    lane = lax.broadcasted_iota(jnp.int32, sq_ref.shape, 1)
    out = jnp.zeros(sq_ref.shape, F32)
    for r in range(recs):
        at = slice(r * rows, (r + 1) * rows)
        pred, gram = None, None
        for k, w_ref in enumerate(w_refs):
            h = h_buf[lax.rem(here + k // 2, nx) * 2 + k % 2, at, :]
            p, q = dot(h, w_ref[...], 1, 0), dot(h, h, 1, 1)
            pred = p if pred is None else pred + p
            gram = q if gram is None else gram + q
        n_copies[r].wait()
        pred = pred + b_ref[r : r + 1, :]
        g = (t_ref[at, :] * (pred - n_buf[r].astype(F32))).astype(BF16)
        g_ref[at, :] = g
        out = jnp.where(lane == r, jnp.sum(gram * dot(g, g, 1, 1)), out)
    sq_ref[...] = out


def pack_kernel(sq_ref, g_ref, o_ref, *, bound):
    rows = g_ref.shape[0]
    norms = jnp.sqrt(jnp.sum(sq_ref[...], axis=0, keepdims=True))
    clip = bound / jnp.maximum(norms, bound)
    high = clip.astype(BF16).astype(F32)
    mid = (clip - high).astype(BF16).astype(F32)
    low = clip - high - mid
    shape = (TAIL, clip.shape[1])
    row = lax.broadcasted_iota(jnp.int32, shape, 0)
    tail = jnp.zeros(shape, F32)
    for k, term in enumerate((high, mid, low)):
        tail = jnp.where(row == k, jnp.broadcast_to(term, shape), tail)
    tail = jnp.concatenate([tail] * (o_ref.shape[2] // clip.shape[1]), axis=1).astype(BF16)
    for k in range(o_ref.shape[0]):
        o_ref[k, 0:rows, :] = g_ref[...]
        o_ref[k, rows : rows + TAIL, :] = tail


def sum_kernel(h_hbm, g_ref, keep_ref, send_ref, h_buf, acc, sems, *, recs):
    copies = fetch(h_hbm, h_buf, sems)
    blocks, total_rows, feats = h_buf.shape
    nx = g_ref.shape[0]
    rows = total_rows // recs
    per = blocks // nx
    for x in range(nx):
        tail = g_ref[x, total_rows : total_rows + TAIL, :].astype(F32)
        clip = jnp.sum(tail, axis=0, keepdims=True)
        for j in range(per):
            copies[x * per + j].wait()
            total = None
            for r in range(recs):
                at = slice(r * rows, (r + 1) * rows)
                block = dot(h_buf[x * per + j, at, :], g_ref[x, at, :], 0, 0) * clip[0:1, r : r + 1]
                total = block if total is None else total + block
            out = slice(j * feats, (j + 1) * feats)
            if x == 0:
                acc[out, :] = total
            else:
                acc[out, :] += total
    groups, size, _ = keep_ref.shape
    odd = lax.axis_index("zp")
    for q in range(groups):
        keep_ref[q] = acc[pl.ds(pl.multiple_of((2 * q + odd) * size, size), size), :]
        send_ref[q] = acc[pl.ds(pl.multiple_of((2 * q + 1 - odd) * size, size), size), :]


def root(v):
    return v * lax.rsqrt(jnp.maximum(jnp.abs(v), 1e-30)) * SCALE


def unroot(v):
    v = v.astype(F32)
    return v * jnp.abs(v) * (1.0 / (SCALE * SCALE))


def ring_gather(v):
    up, down = [(i, (i + 1) % 4) for i in range(4)], [(i, (i + 3) % 4) for i in range(4)]
    half = v.shape[0] // 2
    a, b = v[:half], v[half:]
    a3, b1 = lax.ppermute(a, "x", up), lax.ppermute(b, "x", down)
    b3, a1 = lax.ppermute(b, "x", up), lax.ppermute(a, "x", down)
    a2, b2 = lax.ppermute(a3, "x", up), lax.ppermute(b1, "x", down)
    return [a, b, a1, b1, a2, b2, a3, b3]


def on_device(acts, noise_draws, times, cond, emb, weight, noise):
    recs, draws, events, feats = acts.shape
    rows = draws * events
    local_out = weight.shape[1]
    tensor = ("y", "core")
    nt = lax.axis_size("y") * lax.axis_size("core")
    nx, ng = lax.axis_size("x"), lax.axis_size("zg")
    nz = ng * lax.axis_size("zp")
    bound = 2.0 * math.sqrt(D * DO)

    own = acts.reshape(recs * rows, feats)
    full = lax.all_gather(own, tensor, axis=0, tiled=False)
    swap = [(a * nx + b, b * nx + a) for a in range(nx) for b in range(nx)]
    swapped = lax.ppermute(own, ("x", "y"), swap)

    wz = lax.all_gather(weight, ("zg", "zp"), axis=0, tiled=True)
    swapped, wz = lax.optimization_barrier((swapped, wz))
    mine = lax.all_gather(swapped, tensor, axis=0, tiled=False)
    w_blocks = ring_gather(wz)

    vocab_ids = lax.broadcasted_iota(jnp.int32, (1, 1, emb.shape[0]), 2)
    counts = jnp.sum((cond[:, :, None] == vocab_ids).astype(F32), axis=1).astype(BF16)
    bias = jnp.dot(counts, emb, preferred_element_type=F32)
    wrow = jnp.repeat(
        (1.0 / (times + 0.25)).reshape(recs * draws) * (1.0 / math.sqrt(rows)), events
    )[:, None]

    vmem = pl.BlockSpec(memory_space=pltpu.VMEM)
    hbm = pl.BlockSpec(memory_space=pltpu.HBM)
    grads, sq = pl.pallas_call(
        grad_kernel,
        in_specs=[hbm, hbm] + [vmem] * 10,
        out_specs=[vmem, vmem],
        out_shape=[
            jax.ShapeDtypeStruct((recs * rows, local_out), BF16),
            jax.ShapeDtypeStruct((nt, 128), F32),
        ],
        scratch_shapes=[
            pltpu.VMEM((nt, recs * rows, feats), BF16),
            pltpu.VMEM((recs, rows, local_out), BF16),
            pltpu.SemaphoreType.DMA((nt,)),
            pltpu.SemaphoreType.DMA((recs,)),
        ],
        compiler_params=params(51),
        cost_estimate=pl.CostEstimate(
            flops=2 * recs * rows * (local_out + rows) * D,
            bytes_accessed=2 * recs * rows * D + 2 * D * local_out,
            transcendentals=0,
        ),
    )(full, noise_draws.reshape(recs, rows, local_out), bias, wrow, *w_blocks)

    sq_all = lax.all_to_all(sq.reshape(nt, 1, 128), tensor, 0, 0).reshape(nt, 128)
    norms = jnp.sqrt(jnp.sum(sq_all[:, :recs], axis=0))

    packed = pl.pallas_call(
        functools.partial(pack_kernel, bound=bound),
        out_shape=jax.ShapeDtypeStruct((nx, recs * rows + TAIL, local_out), BF16),
        compiler_params=params(),
    )(sq_all, grads)
    packed = lax.all_to_all(packed, "x", 0, 0)
    block = weight.shape[0]
    keep, send = pl.pallas_call(
        functools.partial(sum_kernel, recs=recs),
        in_specs=[hbm, vmem],
        out_specs=[vmem, vmem],
        out_shape=[jax.ShapeDtypeStruct((ng, block, local_out), F32)] * 2,
        scratch_shapes=[
            pltpu.VMEM((nt, recs * rows, feats), BF16),
            pltpu.VMEM((D // nx, local_out), F32),
            pltpu.SemaphoreType.DMA((nt,)),
        ],
        compiler_params=params(51),
        cost_estimate=pl.CostEstimate(
            flops=2 * recs * rows * local_out * D,
            bytes_accessed=2 * recs * rows * (D + nx * local_out) + 4 * D // nx * local_out,
            transcendentals=0,
        ),
    )(mine.reshape(nt, recs * rows, feats), packed)

    got = lax.ppermute(root(send).astype(F16), "zp", [(0, 1), (1, 0)])
    sent = root(keep + unroot(got)).astype(F16)
    clipped_sum = jnp.sum(unroot(lax.all_to_all(sent, "zg", 0, 0)), axis=0)
    total_recs = recs * nx * nz
    update = (clipped_sum + bound * noise) / total_recs
    return (clipped_sum, update, norms)


def solution(mesh):
    grid = Mesh(mesh.devices.reshape(4, 8, 2, 4, 2), ("x", "zg", "zp", "y", "core"))
    dp, tensor = ("x", "zg", "zp"), ("y", "core")
    in_specs = (
        P(dp, None, None, tensor),
        P(dp, None, None, tensor),
        P(dp, None),
        P(dp, None),
        P(None, tensor),
        P(dp, tensor),
        P(dp, tensor),
    )
    out_specs = (P(dp, tensor), P(dp, tensor), P(dp))
    return jax.shard_map(
        on_device, mesh=grid, in_specs=in_specs, out_specs=out_specs, check_vma=False
    )
```

time: 166 us -> 161 us (0.970)
  the two profiles are of different devices: /device:TPU:1 before, /device:TPU:2 now
where the time goes in v5:
time: 161 us
  blocking collectives  47 us (29%)
  waiting for transfers between devices  45.4 us (28%)
  starting transfers between devices  36.9 us (23%)
  between operations  14.2 us (9%)
  Pallas kernels  11 us (7%)
  other arithmetic  3.25 us (2%)
  local copies, waits for them, and re-layouts  2.74 us (2%)
    all_gather x1, blocking collectives, on_device(): wz = lax.all_gather(weight, ('zg', 'zp'), axis=0, tiled=True)  38.8 us
    all_to_all x1, waiting for transfers between devices, on_device(): clipped_sum = jnp.sum(unroot(lax.all_to_all(sent, 'zg', 0, 0)), axis=0)  18.6 us
    all_to_all x1, waiting for transfers between devices, on_device(): packed = lax.all_to_all(packed, 'x', 0, 0)  12.7 us
    all_to_all x1, blocking collectives, on_device(): lax.all_to_all(sq.reshape(nt, 1, 128), tensor, 0, 0).reshape(nt, 128)  8.19 us
    ppermute x1, waiting for transfers between devices, on_device(): got = lax.ppermute(root(send).astype(F16), 'zp', [(0, 1), (1, 0)])  6.88 us
    ppermute x2, starting transfers between devices, ring_gather(): a3, b1 = (lax.ppermute(a, 'x', up), lax.ppermute(b, 'x', down))  6.7 us
    all_to_all x1, starting transfers between devices, on_device(): clipped_sum = jnp.sum(unroot(lax.all_to_all(sent, 'zg', 0, 0)), axis=0)  6.61 us
    all_to_all x1, starting transfers between devices, on_device(): packed = lax.all_to_all(packed, 'x', 0, 0)  6.5 us
  transfers between devices with their start and end apart: 12, of which 6 were waited for; matrix products, arithmetic and copies ran while one was open for 2% of the time, Pallas kernels for 4%

profile of v5, /device:TPU:2, one launch (start us, length us, event | category | flops | bytes accessed | tf_op | source)
XLA Modules:
  0.0 160.7 jit_solution(17336405149066372347)
XLA Ops:
  8.0 3.5 %collective-permute-start = (bf16[512,512]{1,0:T(8,128)(2,1)}, bf16[512,512]{1,0:T(8,128)(2,1)S(1)}, u32[]{:S(2)}, u32[]{:S(2)}) collective-permute-start(bf16[512,512]{1,0:T(8,128)(2,1)} %bitcast.16), channel_id=1, source_target_pairs={{0,0},{2,128},{4,256},{6,384},{128,2},{130,130},{132,258},{134,386... | collective-permute-start | bytes 1572872 | tf_op jit(solution)/shard_map/ppermute | solution.py:143
  11.4 38.8 %all_gather.12 = bf16[1024,256]{1,0:T(8,128)(2,1)S(1)} all-gather(bf16[64,256]{1,0:T(8,128)(2,1)} %param.12), channel_id=1, replica_groups=mesh['x'=4,'zg'=8,'zp'=2,'y'=4,'core'=2] {'zg','zp'}, dimensions={0}, use_global_device_ids=true | all-gather | bytes 557056 | tf_op jit(solution)/shard_map/all_gather | solution.py:145
  50.2 0.8 copy-done.2
  51.1 4.8 %collective-permute-start.3 = (bf16[512,256]{1,0:T(8,128)(2,1)S(1)}, bf16[512,256]{1,0:T(8,128)(2,1)S(1)}, u32[]{:S(2)}, u32[]{:S(2)}) collective-permute-start(bf16[512,256]{1,0:T(8,128)(2,1)S(1)} %get-tuple-element.16.refs_4_), channel_id=1, source_target_pairs={{0,128},{128,256},{256,384},{384,0},{1,129},{129,257},{257,385},{3... | collective-permute-start | bytes 786440 | tf_op jit(solution)/shard_map/ppermute | solution.py:124
  55.9 1.9 %collective-permute-start.2 = (bf16[512,256]{1,0:T(8,128)(2,1)S(1)}, bf16[512,256]{1,0:T(8,128)(2,1)S(1)}, u32[]{:S(2)}, u32[]{:S(2)}) collective-permute-start(bf16[512,256]{1,0:T(8,128)(2,1)S(1)} %get-tuple-element.15.refs_5_), channel_id=1, source_target_pairs={{0,384},{128,0},{256,128},{384,256},{1,385},{129,1},{257,129},{385... | collective-permute-start | bytes 786440 | tf_op jit(solution)/shard_map/ppermute | solution.py:124
  58.5 3.5 %collective-permute-start.1 = (bf16[512,256]{1,0:T(8,128)(2,1)S(1)}, bf16[512,256]{1,0:T(8,128)(2,1)S(1)}, u32[]{:S(2)}, u32[]{:S(2)}) collective-permute-start(bf16[512,256]{1,0:T(8,128)(2,1)S(1)} %get-tuple-element.16.refs_4_), channel_id=1, source_target_pairs={{0,384},{128,0},{256,128},{384,256},{1,385},{129,1},{257,129},{385... | collective-permute-start | bytes 786440 | tf_op jit(solution)/shard_map/ppermute | solution.py:125
  62.0 2.3 %collective-permute-start.6 = (bf16[512,256]{1,0:T(8,128)(2,1)S(1)}, bf16[512,256]{1,0:T(8,128)(2,1)S(1)}, u32[]{:S(2)}, u32[]{:S(2)}) collective-permute-start(bf16[512,256]{1,0:T(8,128)(2,1)S(1)} %get-tuple-element.15.refs_5_), channel_id=1, source_target_pairs={{0,128},{128,256},{256,384},{384,0},{1,129},{129,257},{257,385},{3... | collective-permute-start | bytes 786440 | tf_op jit(solution)/shard_map/ppermute | solution.py:125
  64.4 3.9 %collective-permute-start.4 = (bf16[512,256]{1,0:T(8,128)(2,1)S(1)}, bf16[512,256]{1,0:T(8,128)(2,1)S(1)}, u32[]{:S(2)}, u32[]{:S(2)}) collective-permute-start(bf16[512,256]{1,0:T(8,128)(2,1)S(1)} %collective-permute-done.3.refs_10_), channel_id=1, source_target_pairs={{0,128},{128,256},{256,384},{384,0},{1,129},{129,257},{257,385},{3... | collective-permute-start | bytes 786440 | tf_op jit(solution)/shard_map/ppermute | solution.py:126
  68.3 1.9 %collective-permute-start.5 = (bf16[512,256]{1,0:T(8,128)(2,1)S(1)}, bf16[512,256]{1,0:T(8,128)(2,1)S(1)}, u32[]{:S(2)}, u32[]{:S(2)}) collective-permute-start(bf16[512,256]{1,0:T(8,128)(2,1)S(1)} %collective-permute-done.2.refs_7_), channel_id=1, source_target_pairs={{0,384},{128,0},{256,128},{384,256},{1,385},{129,1},{257,129},{385... | collective-permute-start | bytes 786440 | tf_op jit(solution)/shard_map/ppermute | solution.py:126
  71.6 1.5 collective-permute-done.4.refs_8_
  73.1 3.7 %collective-permute-done.5.refs_9_ = bf16[512,256]{1,0:T(8,128)(2,1)S(1)} collective-permute-done((bf16[512,256]{1,0:T(8,128)(2,1)S(1)}, bf16[512,256]{1,0:T(8,128)(2,1)S(1)}, u32[]{:S(2)}, u32[]{:S(2)}) %collective-permute-start.5) | collective-permute-done | bytes 262176 | tf_op jit(solution)/shard_map/ppermute | solution.py:126
  76.8 1.0 copy-done.1
  77.7 5.8 %shard_map.94 = (bf16[512,256]{1,0:T(8,128)(2,1)S(1)}, f32[8,128]{1,0:T(8,128)S(1)}) custom-call(bf16[8,512,512]{2,1,0:T(8,128)(2,1)} %all-gather.4.cloned.1.call-done.refs_0_, bf16[2,256,256]{2,1,0:T(8,128)(2,1)S(1)} %bitcast.13, f32[2,256]{1,0:T(2,128)S(1)} %fusion.7.refs_2_, f32[512,1]{1,0:T(8,128)S(1)} %broadcast_in_dim_reshape.4.refs_3_, ...), custom_call_target="tpu_custom_call" | custom-call | flops 2147483648 | bytes 6291456 | tf_op jit(solution)/shard_map/pallas_call | solution.py:159
  83.6 8.2 %all_to_all.15 = f32[8,1,128]{2,1,0:T(1,128)S(1)} all-to-all(f32[8,1,128]{2,1,0:T(1,128)S(1)} %bitcast.12), channel_id=1, replica_groups=mesh['x'=4,'zg'=8,'zp'=2,'y'=4,'core'=2] {'y','core'}, dimensions={0} | all-to-all | bytes 8192 | tf_op jit(solution)/shard_map/all_to_all | solution.py:181
  91.8 1.1 shard_map.95
  92.9 6.5 %all-to-all-start.1 = ((bf16[4,528,256]{2,1,0:T(8,128)(2,1)}), bf16[4,528,256]{2,1,0:T(8,128)(2,1)S(1)}, u32[]{:S(2)}, u32[]{:S(2)}) async-start(bf16[4,528,256]{2,1,0:T(8,128)(2,1)} %shard_map.95), calls=%async_computation.1 | async-start | bytes 2162688 | tf_op jit(solution)/shard_map/all_to_all | solution.py:189
  99.4 1.3 all-gather.6.cloned.1.call-done
  100.7 12.7 %all-to-all-done.1.g_ref = bf16[4,528,256]{2,1,0:T(8,128)(2,1)S(1)} async-done(((bf16[4,528,256]{2,1,0:T(8,128)(2,1)}), bf16[4,528,256]{2,1,0:T(8,128)(2,1)S(1)}, u32[]{:S(2)}, u32[]{:S(2)}) %all-to-all-start.1) | async-done | bytes 1081376 | tf_op jit(solution)/shard_map/all_to_all | solution.py:189
  113.4 4.1 %shard_map.96 = (f32[8,64,256]{2,1,0:T(8,128)S(1)}, f32[8,64,256]{2,1,0:T(8,128)S(1)}) custom-call(bf16[8,512,512]{2,1,0:T(8,128)(2,1)} %bitcast.14, bf16[4,528,256]{2,1,0:T(8,128)(2,1)S(1)} %all-to-all-done.1.g_ref), custom_call_target="tpu_custom_call" | custom-call | flops 1073741824 | bytes 6291456 | tf_op jit(solution)/shard_map/pallas_call | solution.py:191
  117.7 1.9 %collective-permute-start.7 = (f16[8,64,256]{2,1,0:T(8,128)(2,1)S(1)}, f16[8,64,256]{2,1,0:T(8,128)(2,1)S(1)}, u32[]{:S(2)}, u32[]{:S(2)}) collective-permute-start(f16[8,64,256]{2,1,0:T(8,128)(2,1)S(1)} %multiply_convert_fusion.1), channel_id=1, source_target_pairs={{0,8},{8,0},{1,9},{9,1},{2,10},{10,2},{3,11},{11,3},{4,12},{12,4},... | collective-permute-start | bytes 786440 | tf_op jit(solution)/shard_map/ppermute | solution.py:209
  119.6 6.9 %collective-permute-done.7 = f16[8,64,256]{2,1,0:T(8,128)(2,1)S(1)} collective-permute-done((f16[8,64,256]{2,1,0:T(8,128)(2,1)S(1)}, f16[8,64,256]{2,1,0:T(8,128)(2,1)S(1)}, u32[]{:S(2)}, u32[]{:S(2)}) %collective-permute-start.7) | collective-permute-done | bytes 262176 | tf_op jit(solution)/shard_map/ppermute | solution.py:209
  126.5 0.9 multiply_convert_fusion
  127.4 6.6 %all-to-all-start.2 = ((f16[8,64,256]{2,1,0:T(8,128)(2,1)}), f16[8,64,256]{2,1,0:T(8,128)(2,1)S(1)}, u32[]{:S(2)}, u32[]{:S(2)}) async-start(f16[8,64,256]{2,1,0:T(8,128)(2,1)} %multiply_convert_fusion), calls=%async_computation.2 | async-start | bytes 524288 | tf_op jit(solution)/shard_map/all_to_all | solution.py:211
  134.5 18.6 %all-to-all-done.2 = f16[8,64,256]{2,1,0:T(8,128)(2,1)S(1)} async-done(((f16[8,64,256]{2,1,0:T(8,128)(2,1)}), f16[8,64,256]{2,1,0:T(8,128)(2,1)S(1)}, u32[]{:S(2)}, u32[]{:S(2)}) %all-to-all-start.2) | async-done | bytes 262176 | tf_op jit(solution)/shard_map/all_to_all | solution.py:211
  (30 shorter events, 4.3 us)
Async XLA Ops:
  7.2 64.2 %copy-start = (bf16[1024,256]{1,0:T(8,128)(2,1)S(1)}, bf16[1024,256]{1,0:T(8,128)(2,1)}, u32[]{:S(2)}) copy-start(bf16[1024,256]{1,0:T(8,128)(2,1)} %param.11) | copy-start | bytes 1572868
  7.2 69.6 %all-gather.4.cloned.1.call-start = ((), (), s32[]{:S(2)}) async-start(), calls=%async_computation.3 | async-start | bytes 4718592 | tf_op jit(solution)/shard_map/all_gather | solution.py:141
  7.9 92.8 %all-gather.6.cloned.1.call-start = ((), (), s32[]{:S(2)}) async-start(), calls=%async_computation.4 | async-start | bytes 4718592 | tf_op jit(solution)/shard_map/all_gather | solution.py:147
  8.0 42.2 %collective-permute-start = (bf16[512,512]{1,0:T(8,128)(2,1)}, bf16[512,512]{1,0:T(8,128)(2,1)S(1)}, u32[]{:S(2)}, u32[]{:S(2)}) collective-permute-start(bf16[512,512]{1,0:T(8,128)(2,1)} %bitcast.16), channel_id=1, source_target_pairs={{0,0},{2,128},{4,256},{6,384},{128,2},{130,130},{132,258},{134,386... | collective-permute-start | bytes 1572872 | tf_op jit(solution)/shard_map/ppermute | solution.py:143
  50.2 0.8 copy-start.2
  51.1 13.3 %collective-permute-start.3 = (bf16[512,256]{1,0:T(8,128)(2,1)S(1)}, bf16[512,256]{1,0:T(8,128)(2,1)S(1)}, u32[]{:S(2)}, u32[]{:S(2)}) collective-permute-start(bf16[512,256]{1,0:T(8,128)(2,1)S(1)} %get-tuple-element.16.refs_4_), channel_id=1, source_target_pairs={{0,128},{128,256},{256,384},{384,0},{1,129},{129,257},{257,385},{3... | collective-permute-start | bytes 786440 | tf_op jit(solution)/shard_map/ppermute | solution.py:124
  55.9 12.4 %collective-permute-start.2 = (bf16[512,256]{1,0:T(8,128)(2,1)S(1)}, bf16[512,256]{1,0:T(8,128)(2,1)S(1)}, u32[]{:S(2)}, u32[]{:S(2)}) collective-permute-start(bf16[512,256]{1,0:T(8,128)(2,1)S(1)} %get-tuple-element.15.refs_5_), channel_id=1, source_target_pairs={{0,384},{128,0},{256,128},{384,256},{1,385},{129,1},{257,129},{385... | collective-permute-start | bytes 786440 | tf_op jit(solution)/shard_map/ppermute | solution.py:124
  58.5 13.1 %collective-permute-start.1 = (bf16[512,256]{1,0:T(8,128)(2,1)S(1)}, bf16[512,256]{1,0:T(8,128)(2,1)S(1)}, u32[]{:S(2)}, u32[]{:S(2)}) collective-permute-start(bf16[512,256]{1,0:T(8,128)(2,1)S(1)} %get-tuple-element.16.refs_4_), channel_id=1, source_target_pairs={{0,384},{128,0},{256,128},{384,256},{1,385},{129,1},{257,129},{385... | collective-permute-start | bytes 786440 | tf_op jit(solution)/shard_map/ppermute | solution.py:125
  62.0 9.6 %collective-permute-start.6 = (bf16[512,256]{1,0:T(8,128)(2,1)S(1)}, bf16[512,256]{1,0:T(8,128)(2,1)S(1)}, u32[]{:S(2)}, u32[]{:S(2)}) collective-permute-start(bf16[512,256]{1,0:T(8,128)(2,1)S(1)} %get-tuple-element.15.refs_5_), channel_id=1, source_target_pairs={{0,128},{128,256},{256,384},{384,0},{1,129},{129,257},{257,385},{3... | collective-permute-start | bytes 786440 | tf_op jit(solution)/shard_map/ppermute | solution.py:125
  64.4 8.7 %collective-permute-start.4 = (bf16[512,256]{1,0:T(8,128)(2,1)S(1)}, bf16[512,256]{1,0:T(8,128)(2,1)S(1)}, u32[]{:S(2)}, u32[]{:S(2)}) collective-permute-start(bf16[512,256]{1,0:T(8,128)(2,1)S(1)} %collective-permute-done.3.refs_10_), channel_id=1, source_target_pairs={{0,128},{128,256},{256,384},{384,0},{1,129},{129,257},{257,385},{3... | collective-permute-start | bytes 786440 | tf_op jit(solution)/shard_map/ppermute | solution.py:126
  68.3 8.5 %collective-permute-start.5 = (bf16[512,256]{1,0:T(8,128)(2,1)S(1)}, bf16[512,256]{1,0:T(8,128)(2,1)S(1)}, u32[]{:S(2)}, u32[]{:S(2)}) collective-permute-start(bf16[512,256]{1,0:T(8,128)(2,1)S(1)} %collective-permute-done.2.refs_7_), channel_id=1, source_target_pairs={{0,384},{128,0},{256,128},{384,256},{1,385},{129,1},{257,129},{385... | collective-permute-start | bytes 786440 | tf_op jit(solution)/shard_map/ppermute | solution.py:126
  76.8 1.0 copy-start.1
  92.9 20.5 %all-to-all-start.1 = ((bf16[4,528,256]{2,1,0:T(8,128)(2,1)}), bf16[4,528,256]{2,1,0:T(8,128)(2,1)S(1)}, u32[]{:S(2)}, u32[]{:S(2)}) async-start(bf16[4,528,256]{2,1,0:T(8,128)(2,1)} %shard_map.95), calls=%async_computation.1 | async-start | bytes 2162688 | tf_op jit(solution)/shard_map/all_to_all | solution.py:189
  99.4 53.9 %copy-start.4 = (f32[64,256]{1,0:T(8,128)S(1)}, f32[64,256]{1,0:T(8,128)}, u32[]{:S(2)}) copy-start(f32[64,256]{1,0:T(8,128)} %param.13) | copy-start | bytes 196612
  117.7 8.8 %collective-permute-start.7 = (f16[8,64,256]{2,1,0:T(8,128)(2,1)S(1)}, f16[8,64,256]{2,1,0:T(8,128)(2,1)S(1)}, u32[]{:S(2)}, u32[]{:S(2)}) collective-permute-start(f16[8,64,256]{2,1,0:T(8,128)(2,1)S(1)} %multiply_convert_fusion.1), channel_id=1, source_target_pairs={{0,8},{8,0},{1,9},{9,1},{2,10},{10,2},{3,11},{11,3},{4,12},{12,4},... | collective-permute-start | bytes 786440 | tf_op jit(solution)/shard_map/ppermute | solution.py:209
  127.4 25.8 %all-to-all-start.2 = ((f16[8,64,256]{2,1,0:T(8,128)(2,1)}), f16[8,64,256]{2,1,0:T(8,128)(2,1)S(1)}, u32[]{:S(2)}, u32[]{:S(2)}) async-start(f16[8,64,256]{2,1,0:T(8,128)(2,1)} %multiply_convert_fusion), calls=%async_computation.2 | async-start | bytes 524288 | tf_op jit(solution)/shard_map/all_to_all | solution.py:211
  153.2 0.7 copy-start.3
Sparse Core Ops, SparseCore 0:
  10.2 44.2 all-gather.3
  56.6 44.0 all-gather.5

commit v6 on v5

--- a/solution.py
+++ b/solution.py
@@ -14,7 +14,6 @@
 BF16 = jnp.bfloat16
 F16 = jnp.float16
 SCALE = 256.0
-TAIL = 16
 MIB = 1024 * 1024
 
 
@@ -26,8 +25,11 @@
     return lax.dot_general(a, b, (((ca,), (cb,)), ((), ())), preferred_element_type=F32)
 
 
-def fetch(src, dst, sems):
-    copies = [pltpu.make_async_copy(src.at[j], dst.at[j], sems.at[j]) for j in range(dst.shape[0])]
+def fetch(src, dst, sems, order=None):
+    copies = [
+        pltpu.make_async_copy(src.at[order[j] if order else j], dst.at[j], sems.at[j])
+        for j in range(dst.shape[0])
+    ]
     for copy in copies:
         copy.start()
     return copies
@@ -39,18 +41,19 @@
     total_rows, feats = h_buf.shape[1:]
     recs, rows, _ = n_buf.shape
     nx = len(w_refs) // 2
-    h_copies = fetch(h_hbm, h_buf, h_sems)
+    here = lax.axis_index("x")
+    order = [lax.rem(here + k // 2, nx) * 2 + k % 2 for k in range(2 * nx)]
+    h_copies = fetch(h_hbm, h_buf, h_sems, order)
     n_copies = fetch(n_hbm, n_buf, n_sems)
-    for copy in h_copies:
-        copy.wait()
-    here = lax.axis_index("x")
     lane = lax.broadcasted_iota(jnp.int32, sq_ref.shape, 1)
     out = jnp.zeros(sq_ref.shape, F32)
     for r in range(recs):
         at = slice(r * rows, (r + 1) * rows)
         pred, gram = None, None
         for k, w_ref in enumerate(w_refs):
-            h = h_buf[lax.rem(here + k // 2, nx) * 2 + k % 2, at, :]
+            if r == 0:
+                h_copies[k].wait()
+            h = h_buf[k, at, :]
             p, q = dot(h, w_ref[...], 1, 0), dot(h, h, 1, 1)
             pred = p if pred is None else pred + p
             gram = q if gram is None else gram + q
@@ -62,33 +65,14 @@
     sq_ref[...] = out
 
 
-def pack_kernel(sq_ref, g_ref, o_ref, *, bound):
-    rows = g_ref.shape[0]
-    norms = jnp.sqrt(jnp.sum(sq_ref[...], axis=0, keepdims=True))
-    clip = bound / jnp.maximum(norms, bound)
-    high = clip.astype(BF16).astype(F32)
-    mid = (clip - high).astype(BF16).astype(F32)
-    low = clip - high - mid
-    shape = (TAIL, clip.shape[1])
-    row = lax.broadcasted_iota(jnp.int32, shape, 0)
-    tail = jnp.zeros(shape, F32)
-    for k, term in enumerate((high, mid, low)):
-        tail = jnp.where(row == k, jnp.broadcast_to(term, shape), tail)
-    tail = jnp.concatenate([tail] * (o_ref.shape[2] // clip.shape[1]), axis=1).astype(BF16)
-    for k in range(o_ref.shape[0]):
-        o_ref[k, 0:rows, :] = g_ref[...]
-        o_ref[k, rows : rows + TAIL, :] = tail
-
-
-def sum_kernel(h_hbm, g_ref, keep_ref, send_ref, h_buf, acc, sems, *, recs):
+def sum_kernel(h_hbm, g_ref, sq_ref, keep_ref, send_ref, h_buf, acc, sems, *, recs, bound):
     copies = fetch(h_hbm, h_buf, sems)
     blocks, total_rows, feats = h_buf.shape
     nx = g_ref.shape[0]
     rows = total_rows // recs
     per = blocks // nx
     for x in range(nx):
-        tail = g_ref[x, total_rows : total_rows + TAIL, :].astype(F32)
-        clip = jnp.sum(tail, axis=0, keepdims=True)
+        clip = bound / jnp.maximum(jnp.sqrt(sq_ref[x, 0:1, :]), bound)
         for j in range(per):
             copies[x * per + j].wait()
             total = None
@@ -178,19 +162,17 @@
         ),
     )(full, noise_draws.reshape(recs, rows, local_out), bias, wrow, *w_blocks)
 
-    sq_all = lax.all_to_all(sq.reshape(nt, 1, 128), tensor, 0, 0).reshape(nt, 128)
-    norms = jnp.sqrt(jnp.sum(sq_all[:, :recs], axis=0))
-
-    packed = pl.pallas_call(
-        functools.partial(pack_kernel, bound=bound),
-        out_shape=jax.ShapeDtypeStruct((nx, recs * rows + TAIL, local_out), BF16),
-        compiler_params=params(),
-    )(sq_all, grads)
-    packed = lax.all_to_all(packed, "x", 0, 0)
+    all_grads = lax.all_to_all(
+        jnp.broadcast_to(grads[None], (nx, recs * rows, local_out)), "x", 0, 0
+    )
+    sq = lax.psum(sq + lax.ppermute(sq, "core", [(0, 1), (1, 0)]), "y")
+    norms = jnp.sqrt(sq[0, :recs])
+    all_sq = lax.all_gather(sq, "x", axis=0, tiled=False)
+
     block = weight.shape[0]
     keep, send = pl.pallas_call(
-        functools.partial(sum_kernel, recs=recs),
-        in_specs=[hbm, vmem],
+        functools.partial(sum_kernel, recs=recs, bound=bound),
+        in_specs=[hbm, vmem, vmem],
         out_specs=[vmem, vmem],
         out_shape=[jax.ShapeDtypeStruct((ng, block, local_out), F32)] * 2,
         scratch_shapes=[
@@ -204,7 +186,7 @@
             bytes_accessed=2 * recs * rows * (D + nx * local_out) + 4 * D // nx * local_out,
             transcendentals=0,
         ),
-    )(mine.reshape(nt, recs * rows, feats), packed)
+    )(mine.reshape(nt, recs * rows, feats), all_grads, all_sq)
 
     got = lax.ppermute(root(send).astype(F16), "zp", [(0, 1), (1, 0)])
     sent = root(keep + unroot(got)).astype(F16)

time: 161 us -> 160 us (level)
  waiting for transfers between devices: 45.4 us -> 29.5 us
  blocking collectives: 47 us -> 61.3 us
  Pallas kernels: 11 us -> 9.13 us
    all_to_all x1, waiting for transfers between devices: 12.7 us -> 0.01 us  [on_device(): lax.all_to_all(jnp.broadcast_to(grads[None], (nx, recs * rows, local_out)...]
    all_gather x0 -> x1, blocking collectives: none -> 11.9 us  [on_device(): all_sq = lax.all_gather(sq, 'x', axis=0, tiled=False)]
    psum x0 -> x1, blocking collectives: none -> 10.6 us  [on_device(): sq = lax.psum(sq + lax.ppermute(sq, 'core', [(0, 1), (1, 0)]), 'y')]
    all_to_all x1 -> x0, blocking collectives: 8.19 us -> none  [on_device(): lax.all_to_all(sq.reshape(nt, 1, 128), tensor, 0, 0).reshape(nt, 128)]
    all_to_all x1, waiting for transfers between devices: 18.6 us -> 16.1 us  [on_device(): clipped_sum = jnp.sum(unroot(lax.all_to_all(sent, 'zg', 0, 0)), axis=0)]
    ppermute x0 -> x1, starting transfers between devices: none -> 2.04 us  [on_device(): sq = lax.psum(sq + lax.ppermute(sq, 'core', [(0, 1), (1, 0)]), 'y')]
    pallas_call x2 -> x1, Pallas kernels: 5.21 us -> 4.17 us  [on_device(): pl.pallas_call(functools.partial(sum_kernel, recs=recs, bound=bound), in_...]
  transfers between devices with their start and end apart: 12 -> 13, of which waited for: 6 -> 5; matrix products, arithmetic and copies ran while one was open for 2% -> 2% of each run, Pallas kernels for 4% -> 3%
where the time goes in v6:
time: 160 us; the launch traced here: 159 us
  blocking collectives  61.3 us (38%)
  starting transfers between devices  37.8 us (24%)
  waiting for transfers between devices  29.5 us (18%)
  between operations  14.2 us (9%)
  Pallas kernels  9.13 us (6%)
  local copies, waits for them, and re-layouts  3.78 us (2%)
  other arithmetic  3.25 us (2%)
    all_gather x1, blocking collectives, on_device(): wz = lax.all_gather(weight, ('zg', 'zp'), axis=0, tiled=True)  38.8 us
    all_to_all x1, waiting for transfers between devices, on_device(): clipped_sum = jnp.sum(unroot(lax.all_to_all(sent, 'zg', 0, 0)), axis=0)  16.1 us
    all_gather x1, blocking collectives, on_device(): all_sq = lax.all_gather(sq, 'x', axis=0, tiled=False)  11.9 us
    psum x1, blocking collectives, on_device(): sq = lax.psum(sq + lax.ppermute(sq, 'core', [(0, 1), (1, 0)]), 'y')  10.6 us
    ppermute x2, starting transfers between devices, ring_gather(): a3, b1 = (lax.ppermute(a, 'x', up), lax.ppermute(b, 'x', down))  6.7 us
    all_to_all x1, starting transfers between devices, on_device(): clipped_sum = jnp.sum(unroot(lax.all_to_all(sent, 'zg', 0, 0)), axis=0)  6.62 us
    ppermute x1, waiting for transfers between devices, on_device(): got = lax.ppermute(root(send).astype(F16), 'zp', [(0, 1), (1, 0)])  6.34 us
    ppermute x2, starting transfers between devices, ring_gather(): a2, b2 = (lax.ppermute(a3, 'x', up), lax.ppermute(b1, 'x', down))  5.84 us
  transfers between devices with their start and end apart: 13, of which 5 were waited for; matrix products, arithmetic and copies ran while one was open for 2% of the time, Pallas kernels for 3%

profile of v6, /device:TPU:2, one launch (start us, length us, event | category | flops | bytes accessed | tf_op | source)
XLA Modules:
  0.0 159.2 jit_solution(2733455483690494884)
XLA Ops:
  8.0 3.5 %collective-permute-start = (bf16[512,512]{1,0:T(8,128)(2,1)}, bf16[512,512]{1,0:T(8,128)(2,1)S(1)}, u32[]{:S(2)}, u32[]{:S(2)}) collective-permute-start(bf16[512,512]{1,0:T(8,128)(2,1)} %bitcast.13), channel_id=1, source_target_pairs={{0,0},{2,128},{4,256},{6,384},{128,2},{130,130},{132,258},{134,386... | collective-permute-start | bytes 1572872 | tf_op jit(solution)/shard_map/ppermute | solution.py:127
  11.4 38.8 %all_gather.18 = bf16[1024,256]{1,0:T(8,128)(2,1)S(1)} all-gather(bf16[64,256]{1,0:T(8,128)(2,1)} %param.12), channel_id=1, replica_groups=mesh['x'=4,'zg'=8,'zp'=2,'y'=4,'core'=2] {'zg','zp'}, dimensions={0}, use_global_device_ids=true | all-gather | bytes 557056 | tf_op jit(solution)/shard_map/all_gather | solution.py:129
  51.1 4.8 %collective-permute-start.3 = (bf16[512,256]{1,0:T(8,128)(2,1)S(1)}, bf16[512,256]{1,0:T(8,128)(2,1)S(1)}, u32[]{:S(2)}, u32[]{:S(2)}) collective-permute-start(bf16[512,256]{1,0:T(8,128)(2,1)S(1)} %get-tuple-element.16.refs_4_), channel_id=1, source_target_pairs={{0,128},{128,256},{256,384},{384,0},{1,129},{129,257},{257,385},{3... | collective-permute-start | bytes 786440 | tf_op jit(solution)/shard_map/ppermute | solution.py:108
  55.9 1.9 %collective-permute-start.2 = (bf16[512,256]{1,0:T(8,128)(2,1)S(1)}, bf16[512,256]{1,0:T(8,128)(2,1)S(1)}, u32[]{:S(2)}, u32[]{:S(2)}) collective-permute-start(bf16[512,256]{1,0:T(8,128)(2,1)S(1)} %get-tuple-element.15.refs_5_), channel_id=1, source_target_pairs={{0,384},{128,0},{256,128},{384,256},{1,385},{129,1},{257,129},{385... | collective-permute-start | bytes 786440 | tf_op jit(solution)/shard_map/ppermute | solution.py:108
  58.5 3.5 %collective-permute-start.1 = (bf16[512,256]{1,0:T(8,128)(2,1)S(1)}, bf16[512,256]{1,0:T(8,128)(2,1)S(1)}, u32[]{:S(2)}, u32[]{:S(2)}) collective-permute-start(bf16[512,256]{1,0:T(8,128)(2,1)S(1)} %get-tuple-element.16.refs_4_), channel_id=1, source_target_pairs={{0,384},{128,0},{256,128},{384,256},{1,385},{129,1},{257,129},{385... | collective-permute-start | bytes 786440 | tf_op jit(solution)/shard_map/ppermute | solution.py:109
  62.0 2.3 %collective-permute-start.6 = (bf16[512,256]{1,0:T(8,128)(2,1)S(1)}, bf16[512,256]{1,0:T(8,128)(2,1)S(1)}, u32[]{:S(2)}, u32[]{:S(2)}) collective-permute-start(bf16[512,256]{1,0:T(8,128)(2,1)S(1)} %get-tuple-element.15.refs_5_), channel_id=1, source_target_pairs={{0,128},{128,256},{256,384},{384,0},{1,129},{129,257},{257,385},{3... | collective-permute-start | bytes 786440 | tf_op jit(solution)/shard_map/ppermute | solution.py:109
  64.4 3.9 %collective-permute-start.4 = (bf16[512,256]{1,0:T(8,128)(2,1)S(1)}, bf16[512,256]{1,0:T(8,128)(2,1)S(1)}, u32[]{:S(2)}, u32[]{:S(2)}) collective-permute-start(bf16[512,256]{1,0:T(8,128)(2,1)S(1)} %collective-permute-done.3.refs_10_), channel_id=1, source_target_pairs={{0,128},{128,256},{256,384},{384,0},{1,129},{129,257},{257,385},{3... | collective-permute-start | bytes 786440 | tf_op jit(solution)/shard_map/ppermute | solution.py:110
  68.3 1.9 %collective-permute-start.5 = (bf16[512,256]{1,0:T(8,128)(2,1)S(1)}, bf16[512,256]{1,0:T(8,128)(2,1)S(1)}, u32[]{:S(2)}, u32[]{:S(2)}) collective-permute-start(bf16[512,256]{1,0:T(8,128)(2,1)S(1)} %collective-permute-done.2.refs_7_), channel_id=1, source_target_pairs={{0,384},{128,0},{256,128},{384,256},{1,385},{129,1},{257,129},{385... | collective-permute-start | bytes 786440 | tf_op jit(solution)/shard_map/ppermute | solution.py:110
  71.6 1.5 collective-permute-done.4.refs_8_
  73.1 3.7 %collective-permute-done.5.refs_9_ = bf16[512,256]{1,0:T(8,128)(2,1)S(1)} collective-permute-done((bf16[512,256]{1,0:T(8,128)(2,1)S(1)}, bf16[512,256]{1,0:T(8,128)(2,1)S(1)}, u32[]{:S(2)}, u32[]{:S(2)}) %collective-permute-start.5) | collective-permute-done | bytes 262176 | tf_op jit(solution)/shard_map/ppermute | solution.py:110
  76.8 1.0 copy-done.1
  77.7 5.0 %shard_map.94 = (bf16[512,256]{1,0:T(8,128)(2,1)S(1)}, f32[8,128]{1,0:T(8,128)S(1)}) custom-call(bf16[8,512,512]{2,1,0:T(8,128)(2,1)} %all-gather.5.cloned.1.call-done.refs_0_, bf16[2,256,256]{2,1,0:T(8,128)(2,1)S(1)} %bitcast.10, f32[2,256]{1,0:T(2,128)S(1)} %fusion.7.refs_2_, f32[512,1]{1,0:T(8,128)S(1)} %broadcast_in_dim_reshape.4.refs_3_, ...), custom_call_target="tpu_custom_call" | custom-call | flops 2147483648 | bytes 6291456 | tf_op jit(solution)/shard_map/pallas_call | solution.py:143
  82.7 1.0 broadcast_in_dim.5
  83.7 5.4 %all-to-all-start = ((bf16[4,512,256]{2,1,0:T(8,128)(2,1)}), bf16[4,512,256]{2,1,0:T(8,128)(2,1)S(1)}, u32[]{:S(2)}, u32[]{:S(2)}) async-start(bf16[4,512,256]{2,1,0:T(8,128)(2,1)} %broadcast_in_dim.5), calls=%async_computation | async-start | bytes 2097152 | tf_op jit(solution)/shard_map/all_to_all | solution.py:165
  89.1 2.0 %collective-permute-start.7 = (f32[8,128]{1,0:T(8,128)S(1)}, f32[8,128]{1,0:T(8,128)S(1)}, u32[]{:S(2)}, u32[]{:S(2)}) collective-permute-start(f32[8,128]{1,0:T(8,128)S(1)} %get-tuple-element.12), channel_id=1, source_target_pairs={{0,1},{1,0},{2,3},{3,2},{4,5},{5,4},{6,7},{7,6},{8,9},{9,8},{10,11... | collective-permute-start | bytes 12296 | tf_op jit(solution)/shard_map/ppermute | solution.py:168
  91.2 1.1 collective-permute-done.7
  92.3 10.6 %psum.7 = f32[8,128]{1,0:T(8,128)S(1)} all-reduce(f32[8,128]{1,0:T(8,128)S(1)} %add.15), channel_id=1, replica_groups=mesh['x'=4,'zg'=8,'zp'=2,'y'=4,'core'=2] {'y'}, use_global_device_ids=true, to_apply=%region_1.0 | all-reduce | flops 1024 | bytes 8192 | tf_op jit(solution)/shard_map/psum | solution.py:168
  102.9 11.9 %all-gather.1 = f32[32,128]{1,0:T(8,128)S(1)} all-gather(f32[8,128]{1,0:T(8,128)S(1)} %psum.7), channel_id=3, replica_groups=mesh['x'=4,'zg'=8,'zp'=2,'y'=4,'core'=2] {'x'}, dimensions={0}, use_global_device_ids=true | all-gather | bytes 20480 | tf_op jit(solution)/shard_map/all_gather | solution.py:170
  114.8 4.2 %shard_map.95 = (f32[8,64,256]{2,1,0:T(8,128)S(1)}, f32[8,64,256]{2,1,0:T(8,128)S(1)}) custom-call(bf16[8,512,512]{2,1,0:T(8,128)(2,1)} %bitcast.11, bf16[4,512,256]{2,1,0:T(8,128)(2,1)S(1)} %all-to-all-done.g_ref, f32[4,8,128]{2,1,0:T(8,128)S(1)} %bitcast.9), custom_call_target="tpu_custom_call" | custom-call | flops 1073741824 | bytes 6291456 | tf_op jit(solution)/shard_map/pallas_call | solution.py:173
  119.1 1.9 %collective-permute-start.8 = (f16[8,64,256]{2,1,0:T(8,128)(2,1)S(1)}, f16[8,64,256]{2,1,0:T(8,128)(2,1)S(1)}, u32[]{:S(2)}, u32[]{:S(2)}) collective-permute-start(f16[8,64,256]{2,1,0:T(8,128)(2,1)S(1)} %multiply_convert_fusion.1), channel_id=1, source_target_pairs={{0,8},{8,0},{1,9},{9,1},{2,10},{10,2},{3,11},{11,3},{4,12},{12,4},... | collective-permute-start | bytes 786440 | tf_op jit(solution)/shard_map/ppermute | solution.py:191
  121.1 6.3 %collective-permute-done.8 = f16[8,64,256]{2,1,0:T(8,128)(2,1)S(1)} collective-permute-done((f16[8,64,256]{2,1,0:T(8,128)(2,1)S(1)}, f16[8,64,256]{2,1,0:T(8,128)(2,1)S(1)}, u32[]{:S(2)}, u32[]{:S(2)}) %collective-permute-start.8) | collective-permute-done | bytes 262176 | tf_op jit(solution)/shard_map/ppermute | solution.py:191
  127.4 0.9 multiply_convert_fusion
  128.3 6.6 %all-to-all-start.1 = ((f16[8,64,256]{2,1,0:T(8,128)(2,1)}), f16[8,64,256]{2,1,0:T(8,128)(2,1)S(1)}, u32[]{:S(2)}, u32[]{:S(2)}) async-start(f16[8,64,256]{2,1,0:T(8,128)(2,1)} %multiply_convert_fusion), calls=%async_computation.1 | async-start | bytes 524288 | tf_op jit(solution)/shard_map/all_to_all | solution.py:193
  135.5 16.1 %all-to-all-done.1 = f16[8,64,256]{2,1,0:T(8,128)(2,1)S(1)} async-done(((f16[8,64,256]{2,1,0:T(8,128)(2,1)}), f16[8,64,256]{2,1,0:T(8,128)(2,1)S(1)}, u32[]{:S(2)}, u32[]{:S(2)}) %all-to-all-start.1) | async-done | bytes 262176 | tf_op jit(solution)/shard_map/all_to_all | solution.py:193
  (33 shorter events, 5.1 us)
Async XLA Ops:
  7.2 64.2 %copy-start = (bf16[1024,256]{1,0:T(8,128)(2,1)S(1)}, bf16[1024,256]{1,0:T(8,128)(2,1)}, u32[]{:S(2)}) copy-start(bf16[1024,256]{1,0:T(8,128)(2,1)} %param.11) | copy-start | bytes 1572868
  7.2 69.6 %all-gather.5.cloned.1.call-start = ((), (), s32[]{:S(2)}) async-start(), calls=%async_computation.2 | async-start | bytes 4718592 | tf_op jit(solution)/shard_map/all_gather | solution.py:125
  7.9 106.9 %all-gather.7.cloned.1.call-start = ((), (), s32[]{:S(2)}) async-start(), calls=%async_computation.3 | async-start | bytes 4718592 | tf_op jit(solution)/shard_map/all_gather | solution.py:131
  8.0 42.2 %collective-permute-start = (bf16[512,512]{1,0:T(8,128)(2,1)}, bf16[512,512]{1,0:T(8,128)(2,1)S(1)}, u32[]{:S(2)}, u32[]{:S(2)}) collective-permute-start(bf16[512,512]{1,0:T(8,128)(2,1)} %bitcast.13), channel_id=1, source_target_pairs={{0,0},{2,128},{4,256},{6,384},{128,2},{130,130},{132,258},{134,386... | collective-permute-start | bytes 1572872 | tf_op jit(solution)/shard_map/ppermute | solution.py:127
  50.2 0.8 copy-start.2
  51.1 13.3 %collective-permute-start.3 = (bf16[512,256]{1,0:T(8,128)(2,1)S(1)}, bf16[512,256]{1,0:T(8,128)(2,1)S(1)}, u32[]{:S(2)}, u32[]{:S(2)}) collective-permute-start(bf16[512,256]{1,0:T(8,128)(2,1)S(1)} %get-tuple-element.16.refs_4_), channel_id=1, source_target_pairs={{0,128},{128,256},{256,384},{384,0},{1,129},{129,257},{257,385},{3... | collective-permute-start | bytes 786440 | tf_op jit(solution)/shard_map/ppermute | solution.py:108
  55.9 12.4 %collective-permute-start.2 = (bf16[512,256]{1,0:T(8,128)(2,1)S(1)}, bf16[512,256]{1,0:T(8,128)(2,1)S(1)}, u32[]{:S(2)}, u32[]{:S(2)}) collective-permute-start(bf16[512,256]{1,0:T(8,128)(2,1)S(1)} %get-tuple-element.15.refs_5_), channel_id=1, source_target_pairs={{0,384},{128,0},{256,128},{384,256},{1,385},{129,1},{257,129},{385... | collective-permute-start | bytes 786440 | tf_op jit(solution)/shard_map/ppermute | solution.py:108
  58.5 13.1 %collective-permute-start.1 = (bf16[512,256]{1,0:T(8,128)(2,1)S(1)}, bf16[512,256]{1,0:T(8,128)(2,1)S(1)}, u32[]{:S(2)}, u32[]{:S(2)}) collective-permute-start(bf16[512,256]{1,0:T(8,128)(2,1)S(1)} %get-tuple-element.16.refs_4_), channel_id=1, source_target_pairs={{0,384},{128,0},{256,128},{384,256},{1,385},{129,1},{257,129},{385... | collective-permute-start | bytes 786440 | tf_op jit(solution)/shard_map/ppermute | solution.py:109
  62.0 9.6 %collective-permute-start.6 = (bf16[512,256]{1,0:T(8,128)(2,1)S(1)}, bf16[512,256]{1,0:T(8,128)(2,1)S(1)}, u32[]{:S(2)}, u32[]{:S(2)}) collective-permute-start(bf16[512,256]{1,0:T(8,128)(2,1)S(1)} %get-tuple-element.15.refs_5_), channel_id=1, source_target_pairs={{0,128},{128,256},{256,384},{384,0},{1,129},{129,257},{257,385},{3... | collective-permute-start | bytes 786440 | tf_op jit(solution)/shard_map/ppermute | solution.py:109
  64.4 8.7 %collective-permute-start.4 = (bf16[512,256]{1,0:T(8,128)(2,1)S(1)}, bf16[512,256]{1,0:T(8,128)(2,1)S(1)}, u32[]{:S(2)}, u32[]{:S(2)}) collective-permute-start(bf16[512,256]{1,0:T(8,128)(2,1)S(1)} %collective-permute-done.3.refs_10_), channel_id=1, source_target_pairs={{0,128},{128,256},{256,384},{384,0},{1,129},{129,257},{257,385},{3... | collective-permute-start | bytes 786440 | tf_op jit(solution)/shard_map/ppermute | solution.py:110
  68.3 8.5 %collective-permute-start.5 = (bf16[512,256]{1,0:T(8,128)(2,1)S(1)}, bf16[512,256]{1,0:T(8,128)(2,1)S(1)}, u32[]{:S(2)}, u32[]{:S(2)}) collective-permute-start(bf16[512,256]{1,0:T(8,128)(2,1)S(1)} %collective-permute-done.2.refs_7_), channel_id=1, source_target_pairs={{0,384},{128,0},{256,128},{384,256},{1,385},{129,1},{257,129},{385... | collective-permute-start | bytes 786440 | tf_op jit(solution)/shard_map/ppermute | solution.py:110
  76.8 1.0 copy-start.1
  83.7 31.1 %all-to-all-start = ((bf16[4,512,256]{2,1,0:T(8,128)(2,1)}), bf16[4,512,256]{2,1,0:T(8,128)(2,1)S(1)}, u32[]{:S(2)}, u32[]{:S(2)}) async-start(bf16[4,512,256]{2,1,0:T(8,128)(2,1)} %broadcast_in_dim.5), calls=%async_computation | async-start | bytes 2097152 | tf_op jit(solution)/shard_map/all_to_all | solution.py:165
  89.1 62.6 %copy-start.4 = (f32[64,256]{1,0:T(8,128)S(1)}, f32[64,256]{1,0:T(8,128)}, u32[]{:S(2)}) copy-start(f32[64,256]{1,0:T(8,128)} %param.13) | copy-start | bytes 196612
  89.1 3.2 %collective-permute-start.7 = (f32[8,128]{1,0:T(8,128)S(1)}, f32[8,128]{1,0:T(8,128)S(1)}, u32[]{:S(2)}, u32[]{:S(2)}) collective-permute-start(f32[8,128]{1,0:T(8,128)S(1)} %get-tuple-element.12), channel_id=1, source_target_pairs={{0,1},{1,0},{2,3},{3,2},{4,5},{5,4},{6,7},{7,6},{8,9},{9,8},{10,11... | collective-permute-start | bytes 12296 | tf_op jit(solution)/shard_map/ppermute | solution.py:168
  119.1 8.3 %collective-permute-start.8 = (f16[8,64,256]{2,1,0:T(8,128)(2,1)S(1)}, f16[8,64,256]{2,1,0:T(8,128)(2,1)S(1)}, u32[]{:S(2)}, u32[]{:S(2)}) collective-permute-start(f16[8,64,256]{2,1,0:T(8,128)(2,1)S(1)} %multiply_convert_fusion.1), channel_id=1, source_target_pairs={{0,8},{8,0},{1,9},{9,1},{2,10},{10,2},{3,11},{11,3},{4,12},{12,4},... | collective-permute-start | bytes 786440 | tf_op jit(solution)/shard_map/ppermute | solution.py:191
  128.3 23.3 %all-to-all-start.1 = ((f16[8,64,256]{2,1,0:T(8,128)(2,1)}), f16[8,64,256]{2,1,0:T(8,128)(2,1)S(1)}, u32[]{:S(2)}, u32[]{:S(2)}) async-start(f16[8,64,256]{2,1,0:T(8,128)(2,1)} %multiply_convert_fusion), calls=%async_computation.1 | async-start | bytes 524288 | tf_op jit(solution)/shard_map/all_to_all | solution.py:193
  151.7 0.7 copy-start.3
Sparse Core Ops, SparseCore 0:
  10.2 44.2 all-gather.4
  56.6 44.0 all-gather.6

commit v7 on v6

--- a/solution.py
+++ b/solution.py
@@ -14,6 +14,7 @@
 BF16 = jnp.bfloat16
 F16 = jnp.float16
 SCALE = 256.0
+AFTER = 6
 MIB = 1024 * 1024
 
 
@@ -35,34 +36,51 @@
     return copies
 
 
+def gram_kernel(h_hbm, n_hbm, after, h_ref, n_ref, gram_ref, h_sems, n_sems):
+    recs, rows, _ = gram_ref.shape
+    blocks = h_ref.shape[0]
+    nx = blocks // 2
+    here = lax.axis_index("x")
+    order = [lax.rem(here + k // 2, nx) * 2 + k % 2 for k in range(blocks)]
+    h_copies = fetch(h_hbm, h_ref, h_sems, order)
+    n_copies = fetch(n_hbm, n_ref, n_sems)
+    for r in range(recs):
+        total = None
+        for k in range(blocks):
+            if r == 0:
+                h_copies[k].wait()
+            h = h_ref[k, r * rows : (r + 1) * rows, :]
+            q = dot(h, h, 1, 1)
+            total = q if total is None else total + q
+        gram_ref[r] = total
+    for copy in n_copies:
+        copy.wait()
+
+
 def grad_kernel(*refs):
-    h_hbm, n_hbm, b_ref, t_ref = refs[:4]
-    w_refs, (g_ref, sq_ref, h_buf, n_buf, h_sems, n_sems) = refs[4:-6], refs[-6:]
-    total_rows, feats = h_buf.shape[1:]
-    recs, rows, _ = n_buf.shape
-    nx = len(w_refs) // 2
-    here = lax.axis_index("x")
-    order = [lax.rem(here + k // 2, nx) * 2 + k % 2 for k in range(2 * nx)]
-    h_copies = fetch(h_hbm, h_buf, h_sems, order)
-    n_copies = fetch(n_hbm, n_buf, n_sems)
+    h_ref, n_ref, gram_ref, b_ref, t_ref = refs[:5]
+    w_refs, (g_ref, sq_ref) = refs[5:-2], refs[-2:]
+    recs, rows, _ = gram_ref.shape
+    events = rows // t_ref.shape[1]
+    row = lax.broadcasted_iota(jnp.int32, sq_ref.shape, 0)
     lane = lax.broadcasted_iota(jnp.int32, sq_ref.shape, 1)
     out = jnp.zeros(sq_ref.shape, F32)
     for r in range(recs):
         at = slice(r * rows, (r + 1) * rows)
-        pred, gram = None, None
+        pred = None
         for k, w_ref in enumerate(w_refs):
-            if r == 0:
-                h_copies[k].wait()
-            h = h_buf[k, at, :]
-            p, q = dot(h, w_ref[...], 1, 0), dot(h, h, 1, 1)
+            p = dot(h_ref[k, at, :], w_ref[...], 1, 0)
             pred = p if pred is None else pred + p
-            gram = q if gram is None else gram + q
-        n_copies[r].wait()
-        pred = pred + b_ref[r : r + 1, :]
-        g = (t_ref[at, :] * (pred - n_buf[r].astype(F32))).astype(BF16)
-        g_ref[at, :] = g
-        out = jnp.where(lane == r, jnp.sum(gram * dot(g, g, 1, 1)), out)
-    sq_ref[...] = out
+        diff = pred + b_ref[r : r + 1, :] - n_ref[r].astype(F32)
+        parts = []
+        for a in range(t_ref.shape[1]):
+            wgt = 1.0 / (t_ref[r : r + 1, a : a + 1] + 0.25)
+            parts.append(wgt * diff[a * events : (a + 1) * events, :])
+        g = (jnp.concatenate(parts, axis=0) * (1.0 / math.sqrt(rows))).astype(BF16)
+        for k in range(g_ref.shape[0]):
+            g_ref[k, at, :] = g
+        out = jnp.where(lane == r, jnp.sum(gram_ref[r] * dot(g, g, 1, 1)), out)
+    sq_ref[...] = jnp.where(row == lax.axis_index("x"), out, 0.0)
 
 
 def sum_kernel(h_hbm, g_ref, sq_ref, keep_ref, send_ref, h_buf, acc, sems, *, recs, bound):
@@ -72,7 +90,7 @@
     rows = total_rows // recs
     per = blocks // nx
     for x in range(nx):
-        clip = bound / jnp.maximum(jnp.sqrt(sq_ref[x, 0:1, :]), bound)
+        clip = bound / jnp.maximum(jnp.sqrt(sq_ref[x : x + 1, :]), bound)
         for j in range(per):
             copies[x * per + j].wait()
             total = None
@@ -134,40 +152,46 @@
     vocab_ids = lax.broadcasted_iota(jnp.int32, (1, 1, emb.shape[0]), 2)
     counts = jnp.sum((cond[:, :, None] == vocab_ids).astype(F32), axis=1).astype(BF16)
     bias = jnp.dot(counts, emb, preferred_element_type=F32)
-    wrow = jnp.repeat(
-        (1.0 / (times + 0.25)).reshape(recs * draws) * (1.0 / math.sqrt(rows)), events
-    )[:, None]
 
     vmem = pl.BlockSpec(memory_space=pltpu.VMEM)
     hbm = pl.BlockSpec(memory_space=pltpu.HBM)
+    h, n, gram = pl.pallas_call(
+        gram_kernel,
+        in_specs=[hbm, hbm, pl.BlockSpec(memory_space=pl.ANY)],
+        out_specs=[vmem, vmem, vmem],
+        out_shape=[
+            jax.ShapeDtypeStruct((nt, recs * rows, feats), BF16),
+            jax.ShapeDtypeStruct((recs, rows, local_out), BF16),
+            jax.ShapeDtypeStruct((recs, rows, rows), F32),
+        ],
+        scratch_shapes=[pltpu.SemaphoreType.DMA((nt,)), pltpu.SemaphoreType.DMA((recs,))],
+        compiler_params=params(48),
+        cost_estimate=pl.CostEstimate(
+            flops=2 * recs * rows * rows * D, bytes_accessed=4 * recs * rows * D, transcendentals=0
+        ),
+    )(full, noise_draws.reshape(recs, rows, local_out), w_blocks[AFTER])
     grads, sq = pl.pallas_call(
         grad_kernel,
-        in_specs=[hbm, hbm] + [vmem] * 10,
+        in_specs=[vmem] * 13,
         out_specs=[vmem, vmem],
         out_shape=[
-            jax.ShapeDtypeStruct((recs * rows, local_out), BF16),
-            jax.ShapeDtypeStruct((nt, 128), F32),
+            jax.ShapeDtypeStruct((nx, recs * rows, local_out), BF16),
+            jax.ShapeDtypeStruct((8, 128), F32),
         ],
-        scratch_shapes=[
-            pltpu.VMEM((nt, recs * rows, feats), BF16),
-            pltpu.VMEM((recs, rows, local_out), BF16),
-            pltpu.SemaphoreType.DMA((nt,)),
-            pltpu.SemaphoreType.DMA((recs,)),
-        ],
-        compiler_params=params(51),
+        compiler_params=params(),
         cost_estimate=pl.CostEstimate(
-            flops=2 * recs * rows * (local_out + rows) * D,
+            flops=2 * recs * rows * local_out * D,
             bytes_accessed=2 * recs * rows * D + 2 * D * local_out,
             transcendentals=0,
         ),
-    )(full, noise_draws.reshape(recs, rows, local_out), bias, wrow, *w_blocks)
-
-    all_grads = lax.all_to_all(
-        jnp.broadcast_to(grads[None], (nx, recs * rows, local_out)), "x", 0, 0
-    )
-    sq = lax.psum(sq + lax.ppermute(sq, "core", [(0, 1), (1, 0)]), "y")
-    norms = jnp.sqrt(sq[0, :recs])
-    all_sq = lax.all_gather(sq, "x", axis=0, tiled=False)
+    )(h, n, gram, bias, times, *w_blocks)
+
+    all_grads = lax.all_to_all(grads, "x", 0, 0)
+    sq = sq + lax.ppermute(sq, "core", [(0, 1), (1, 0)])
+    for axis in ("y", "x"):
+        for pairs in ((1, 0, 3, 2), (3, 2, 1, 0)):
+            sq = sq + lax.ppermute(sq, axis, list(enumerate(pairs)))
+    norms = jnp.sqrt(lax.dynamic_index_in_dim(sq, lax.axis_index("x"), 0, False)[:recs])
 
     block = weight.shape[0]
     keep, send = pl.pallas_call(
@@ -186,7 +210,7 @@
             bytes_accessed=2 * recs * rows * (D + nx * local_out) + 4 * D // nx * local_out,
             transcendentals=0,
         ),
-    )(mine.reshape(nt, recs * rows, feats), all_grads, all_sq)
+    )(mine.reshape(nt, recs * rows, feats), all_grads, sq)
 
     got = lax.ppermute(root(send).astype(F16), "zp", [(0, 1), (1, 0)])
     sent = root(keep + unroot(got)).astype(F16)

time: 160 us -> 159 us (level)
  the two profiles are of different devices: /device:TPU:2 before, /device:TPU:30 now
where the time goes in v7:
time: 159 us; the launch traced here: 158 us
  starting transfers between devices  46.7 us (29%)
  waiting for transfers between devices  41.7 us (26%)
  blocking collectives  38.9 us (24%)
  between operations  14.3 us (9%)
  Pallas kernels  11.6 us (7%)
  other arithmetic  2.56 us (2%)
  local copies, waits for them, and re-layouts  2.41 us (2%)
    all_gather x1, blocking collectives, on_device(): wz = lax.all_gather(weight, ('zg', 'zp'), axis=0, tiled=True)  38.9 us
    all_to_all x1, waiting for transfers between devices, on_device(): clipped_sum = jnp.sum(unroot(lax.all_to_all(sent, 'zg', 0, 0)), axis=0)  16.7 us
    ppermute x4, waiting for transfers between devices, on_device(): sq = sq + lax.ppermute(sq, axis, list(enumerate(pairs)))  14.3 us
    ppermute x4, starting transfers between devices, on_device(): sq = sq + lax.ppermute(sq, axis, list(enumerate(pairs)))  10.1 us
    ppermute x2, starting transfers between devices, ring_gather(): b3, a1 = (lax.ppermute(b, 'x', up), lax.ppermute(a, 'x', down))  7.05 us
    all_to_all x1, starting transfers between devices, on_device(): clipped_sum = jnp.sum(unroot(lax.all_to_all(sent, 'zg', 0, 0)), axis=0)  6.84 us
    ppermute x2, starting transfers between devices, ring_gather(): a3, b1 = (lax.ppermute(a, 'x', up), lax.ppermute(b, 'x', down))  6.65 us
    ppermute x1, waiting for transfers between devices, on_device(): got = lax.ppermute(root(send).astype(F16), 'zp', [(0, 1), (1, 0)])  6.34 us
  transfers between devices with their start and end apart: 17, of which 8 were waited for; matrix products, arithmetic and copies ran while one was open for 1% of the time, Pallas kernels for 5%

profile of v7, /device:TPU:30, one launch (start us, length us, event | category | flops | bytes accessed | tf_op | source)
XLA Modules:
  0.0 158.3 jit_solution(13065885929316373313)
XLA Ops:
  9.7 38.9 %all_gather.12 = bf16[1024,256]{1,0:T(8,128)(2,1)S(1)} all-gather(bf16[64,256]{1,0:T(8,128)(2,1)} %param.12), channel_id=1, replica_groups=mesh['x'=4,'zg'=8,'zp'=2,'y'=4,'core'=2] {'zg','zp'}, dimensions={0}, use_global_device_ids=true | all-gather | bytes 557056 | tf_op jit(solution)/shard_map/all_gather | solution.py:147
  49.5 4.7 %collective-permute-start.1 = (bf16[512,256]{1,0:T(8,128)(2,1)S(1)}, bf16[512,256]{1,0:T(8,128)(2,1)S(1)}, u32[]{:S(2)}, u32[]{:S(2)}) collective-permute-start(bf16[512,256]{1,0:T(8,128)(2,1)S(1)} %get-tuple-element.22.refs_5_), channel_id=1, source_target_pairs={{0,128},{128,256},{256,384},{384,0},{1,129},{129,257},{257,385},{3... | collective-permute-start | bytes 786440 | tf_op jit(solution)/shard_map/ppermute | solution.py:126
  54.2 1.9 %collective-permute-start.3 = (bf16[512,256]{1,0:T(8,128)(2,1)S(1)}, bf16[512,256]{1,0:T(8,128)(2,1)S(1)}, u32[]{:S(2)}, u32[]{:S(2)}) collective-permute-start(bf16[512,256]{1,0:T(8,128)(2,1)S(1)} %get-tuple-element.21.refs_6_), channel_id=1, source_target_pairs={{0,384},{128,0},{256,128},{384,256},{1,385},{129,1},{257,129},{385... | collective-permute-start | bytes 786440 | tf_op jit(solution)/shard_map/ppermute | solution.py:126
  56.9 3.4 %collective-permute-start.2 = (bf16[512,256]{1,0:T(8,128)(2,1)S(1)}, bf16[512,256]{1,0:T(8,128)(2,1)S(1)}, u32[]{:S(2)}, u32[]{:S(2)}) collective-permute-start(bf16[512,256]{1,0:T(8,128)(2,1)S(1)} %get-tuple-element.22.refs_5_), channel_id=1, source_target_pairs={{0,384},{128,0},{256,128},{384,256},{1,385},{129,1},{257,129},{385... | collective-permute-start | bytes 786440 | tf_op jit(solution)/shard_map/ppermute | solution.py:127
  60.4 3.6 %collective-permute-start.6 = (bf16[512,256]{1,0:T(8,128)(2,1)S(1)}, bf16[512,256]{1,0:T(8,128)(2,1)S(1)}, u32[]{:S(2)}, u32[]{:S(2)}) collective-permute-start(bf16[512,256]{1,0:T(8,128)(2,1)S(1)} %get-tuple-element.21.refs_6_), channel_id=1, source_target_pairs={{0,128},{128,256},{256,384},{384,0},{1,129},{129,257},{257,385},{3... | collective-permute-start | bytes 786440 | tf_op jit(solution)/shard_map/ppermute | solution.py:127
  64.0 3.9 %collective-permute-start.4 = (bf16[512,256]{1,0:T(8,128)(2,1)S(1)}, bf16[512,256]{1,0:T(8,128)(2,1)S(1)}, u32[]{:S(2)}, u32[]{:S(2)}) collective-permute-start(bf16[512,256]{1,0:T(8,128)(2,1)S(1)} %collective-permute-done.1.after.refs_11_), channel_id=1, source_target_pairs={{0,128},{128,256},{256,384},{384,0},{1,129},{129,257},{257,385},{3... | collective-permute-start | bytes 786440 | tf_op jit(solution)/shard_map/ppermute | solution.py:128
  67.9 1.9 %collective-permute-start.5 = (bf16[512,256]{1,0:T(8,128)(2,1)S(1)}, bf16[512,256]{1,0:T(8,128)(2,1)S(1)}, u32[]{:S(2)}, u32[]{:S(2)}) collective-permute-start(bf16[512,256]{1,0:T(8,128)(2,1)S(1)} %collective-permute-done.3.refs_8_), channel_id=1, source_target_pairs={{0,384},{128,0},{256,128},{384,256},{1,385},{129,1},{257,129},{385... | collective-permute-start | bytes 786440 | tf_op jit(solution)/shard_map/ppermute | solution.py:128
  71.0 3.9 %shard_map.94 = (bf16[8,512,512]{2,1,0:T(8,128)(2,1)S(1)}, bf16[2,256,256]{2,1,0:T(8,128)(2,1)S(1)}, f32[2,256,256]{2,1,0:T(8,128)S(1)}) custom-call(bf16[8,512,512]{2,1,0:T(8,128)(2,1)} %all-gather.4.cloned.1.call-done.h_hbm, bf16[2,256,256]{2,1,0:T(8,128)(2,1)S(1)} %bitcast.8, bf16[512,256]{1,0:T(8,128)(2,1)S(1)} %collective-permute-done.1.after.refs_11_), custom_call_target="tpu_custom_call" | custom-call | flops 1073741824 | bytes 8388608 | tf_op jit(solution)/shard_map/pallas_call | solution.py:158
  75.0 2.5 %collective-permute-done.5.refs_10_ = bf16[512,256]{1,0:T(8,128)(2,1)S(1)} collective-permute-done((bf16[512,256]{1,0:T(8,128)(2,1)S(1)}, bf16[512,256]{1,0:T(8,128)(2,1)S(1)}, u32[]{:S(2)}, u32[]{:S(2)}) %collective-permute-start.5) | collective-permute-done | bytes 262176 | tf_op jit(solution)/shard_map/ppermute | solution.py:128
  77.4 3.5 %shard_map.95 = (bf16[4,512,256]{2,1,0:T(8,128)(2,1)}, f32[8,128]{1,0:T(8,128)S(1)}) custom-call(bf16[8,512,512]{2,1,0:T(8,128)(2,1)S(1)} %get-tuple-element.14.refs_0_, bf16[2,256,256]{2,1,0:T(8,128)(2,1)S(1)} %get-tuple-element.15.refs_1_, f32[2,256,256]{2,1,0:T(8,128)S(1)} %get-tuple-element.16.refs_2_, f32[2,256]{1,0:T(2,128)S(1)} %fusion.7.refs_3_, ...), custom_call_target="tpu_custom_call" | custom-call | flops 1073741824 | bytes 6291456 | tf_op jit(solution)/shard_map/pallas_call | solution.py:173
  81.0 4.5 %all-to-all-start = ((bf16[4,512,256]{2,1,0:T(8,128)(2,1)}), bf16[4,512,256]{2,1,0:T(8,128)(2,1)S(1)}, u32[]{:S(2)}, u32[]{:S(2)}) async-start(bf16[4,512,256]{2,1,0:T(8,128)(2,1)} %get-tuple-element.17), calls=%async_computation | async-start | bytes 2097152 | tf_op jit(solution)/shard_map/all_to_all | solution.py:189
  85.5 2.0 %collective-permute-start.7 = (f32[8,128]{1,0:T(8,128)S(1)}, f32[8,128]{1,0:T(8,128)S(1)}, u32[]{:S(2)}, u32[]{:S(2)}) collective-permute-start(f32[8,128]{1,0:T(8,128)S(1)} %get-tuple-element.18), channel_id=1, source_target_pairs={{0,1},{1,0},{2,3},{3,2},{4,5},{5,4},{6,7},{7,6},{8,9},{9,8},{10,11... | collective-permute-start | bytes 12296 | tf_op jit(solution)/shard_map/ppermute | solution.py:190
  88.6 3.0 %collective-permute-start.8 = (f32[8,128]{1,0:T(8,128)S(1)}, f32[8,128]{1,0:T(8,128)S(1)}, u32[]{:S(2)}, u32[]{:S(2)}) collective-permute-start(f32[8,128]{1,0:T(8,128)S(1)} %add.25), channel_id=1, source_target_pairs={{0,2},{2,0},{4,6},{6,4},{1,3},{3,1},{5,7},{7,5},{8,10},{10,8},{12,... | collective-permute-start | bytes 12296 | tf_op jit(solution)/shard_map/ppermute | solution.py:193
  91.7 2.5 %collective-permute-done.8 = f32[8,128]{1,0:T(8,128)S(1)} collective-permute-done((f32[8,128]{1,0:T(8,128)S(1)}, f32[8,128]{1,0:T(8,128)S(1)}, u32[]{:S(2)}, u32[]{:S(2)}) %collective-permute-start.8) | collective-permute-done | bytes 4128 | tf_op jit(solution)/shard_map/ppermute | solution.py:193
  94.2 2.4 %collective-permute-start.9 = (f32[8,128]{1,0:T(8,128)S(1)}, f32[8,128]{1,0:T(8,128)S(1)}, u32[]{:S(2)}, u32[]{:S(2)}) collective-permute-start(f32[8,128]{1,0:T(8,128)S(1)} %add.26), channel_id=1, source_target_pairs={{0,6},{2,4},{4,2},{6,0},{1,7},{3,5},{5,3},{7,1},{8,14},{10,12},{12... | collective-permute-start | bytes 12296 | tf_op jit(solution)/shard_map/ppermute | solution.py:193
  96.6 4.3 %collective-permute-done.9 = f32[8,128]{1,0:T(8,128)S(1)} collective-permute-done((f32[8,128]{1,0:T(8,128)S(1)}, f32[8,128]{1,0:T(8,128)S(1)}, u32[]{:S(2)}, u32[]{:S(2)}) %collective-permute-start.9) | collective-permute-done | bytes 4128 | tf_op jit(solution)/shard_map/ppermute | solution.py:193
  100.9 2.8 %collective-permute-start.10 = (f32[8,128]{1,0:T(8,128)S(1)}, f32[8,128]{1,0:T(8,128)S(1)}, u32[]{:S(2)}, u32[]{:S(2)}) collective-permute-start(f32[8,128]{1,0:T(8,128)S(1)} %add.27), channel_id=1, source_target_pairs={{0,128},{128,0},{256,384},{384,256},{1,129},{129,1},{257,385},{385... | collective-permute-start | bytes 12296 | tf_op jit(solution)/shard_map/ppermute | solution.py:193
  103.7 2.7 %collective-permute-done.10 = f32[8,128]{1,0:T(8,128)S(1)} collective-permute-done((f32[8,128]{1,0:T(8,128)S(1)}, f32[8,128]{1,0:T(8,128)S(1)}, u32[]{:S(2)}, u32[]{:S(2)}) %collective-permute-start.10) | collective-permute-done | bytes 4128 | tf_op jit(solution)/shard_map/ppermute | solution.py:193
  108.3 4.8 %collective-permute-done.11 = f32[8,128]{1,0:T(8,128)S(1)} collective-permute-done((f32[8,128]{1,0:T(8,128)S(1)}, f32[8,128]{1,0:T(8,128)S(1)}, u32[]{:S(2)}, u32[]{:S(2)}) %collective-permute-start.11) | collective-permute-done | bytes 4128 | tf_op jit(solution)/shard_map/ppermute | solution.py:193
  113.1 4.2 %shard_map.96 = (f32[8,64,256]{2,1,0:T(8,128)S(1)}, f32[8,64,256]{2,1,0:T(8,128)S(1)}) custom-call(bf16[8,512,512]{2,1,0:T(8,128)(2,1)} %bitcast.9, bf16[4,512,256]{2,1,0:T(8,128)(2,1)S(1)} %all-to-all-done.g_ref, f32[8,128]{1,0:T(8,128)S(1)} %add.29.sq_ref), custom_call_target="tpu_custom_call" | custom-call | flops 1073741824 | bytes 6291456 | tf_op jit(solution)/shard_map/pallas_call | solution.py:197
  117.4 1.9 %collective-permute-start.12 = (f16[8,64,256]{2,1,0:T(8,128)(2,1)S(1)}, f16[8,64,256]{2,1,0:T(8,128)(2,1)S(1)}, u32[]{:S(2)}, u32[]{:S(2)}) collective-permute-start(f16[8,64,256]{2,1,0:T(8,128)(2,1)S(1)} %multiply_convert_fusion.1), channel_id=1, source_target_pairs={{0,8},{8,0},{1,9},{9,1},{2,10},{10,2},{3,11},{11,3},{4,12},{12,4},... | collective-permute-start | bytes 786440 | tf_op jit(solution)/shard_map/ppermute | solution.py:215
  119.3 6.3 %collective-permute-done.12 = f16[8,64,256]{2,1,0:T(8,128)(2,1)S(1)} collective-permute-done((f16[8,64,256]{2,1,0:T(8,128)(2,1)S(1)}, f16[8,64,256]{2,1,0:T(8,128)(2,1)S(1)}, u32[]{:S(2)}, u32[]{:S(2)}) %collective-permute-start.12) | collective-permute-done | bytes 262176 | tf_op jit(solution)/shard_map/ppermute | solution.py:215
  126.6 6.8 %all-to-all-start.1 = ((f16[8,64,256]{2,1,0:T(8,128)(2,1)}), f16[8,64,256]{2,1,0:T(8,128)(2,1)S(1)}, u32[]{:S(2)}, u32[]{:S(2)}) async-start(f16[8,64,256]{2,1,0:T(8,128)(2,1)} %multiply_convert_fusion), calls=%async_computation.1 | async-start | bytes 524288 | tf_op jit(solution)/shard_map/all_to_all | solution.py:217
  133.9 16.7 %all-to-all-done.1 = f16[8,64,256]{2,1,0:T(8,128)(2,1)S(1)} async-done(((f16[8,64,256]{2,1,0:T(8,128)(2,1)}), f16[8,64,256]{2,1,0:T(8,128)(2,1)S(1)}, u32[]{:S(2)}, u32[]{:S(2)}) %all-to-all-start.1) | async-done | bytes 262176 | tf_op jit(solution)/shard_map/all_to_all | solution.py:217
  (42 shorter events, 10.7 us)
Async XLA Ops:
  7.2 62.7 %copy-start = (bf16[1024,256]{1,0:T(8,128)(2,1)S(1)}, bf16[1024,256]{1,0:T(8,128)(2,1)}, u32[]{:S(2)}) copy-start(bf16[1024,256]{1,0:T(8,128)(2,1)} %param.11) | copy-start | bytes 1572868
  7.2 70.2 %copy-start.2 = (f32[2,4]{1,0:T(2,128)S(1)}, f32[2,4]{1,0:T(2,128)}, u32[]{:S(2)}) copy-start(f32[2,4]{1,0:T(2,128)} %refs_4_.1) | copy-start | bytes 100
  7.2 62.9 %all-gather.4.cloned.1.call-start = ((), (), s32[]{:S(2)}) async-start(), calls=%async_computation.2 | async-start | bytes 4718592 | tf_op jit(solution)/shard_map/all_gather | solution.py:143
  7.9 105.2 %all-gather.6.cloned.1.call-start = ((), (), s32[]{:S(2)}) async-start(), calls=%async_computation.3 | async-start | bytes 4718592 | tf_op jit(solution)/shard_map/all_gather | solution.py:149
  8.0 40.6 %collective-permute-start = (bf16[512,512]{1,0:T(8,128)(2,1)}, bf16[512,512]{1,0:T(8,128)(2,1)S(1)}, u32[]{:S(2)}, u32[]{:S(2)}) collective-permute-start(bf16[512,512]{1,0:T(8,128)(2,1)} %bitcast.11), channel_id=1, source_target_pairs={{0,0},{2,128},{4,256},{6,384},{128,2},{130,130},{132,258},{134,386... | collective-permute-start | bytes 1572872 | tf_op jit(solution)/shard_map/ppermute | solution.py:145
  48.5 0.9 copy-start.3
  49.5 14.5 %collective-permute-start.1 = (bf16[512,256]{1,0:T(8,128)(2,1)S(1)}, bf16[512,256]{1,0:T(8,128)(2,1)S(1)}, u32[]{:S(2)}, u32[]{:S(2)}) collective-permute-start(bf16[512,256]{1,0:T(8,128)(2,1)S(1)} %get-tuple-element.22.refs_5_), channel_id=1, source_target_pairs={{0,128},{128,256},{256,384},{384,0},{1,129},{129,257},{257,385},{3... | collective-permute-start | bytes 786440 | tf_op jit(solution)/shard_map/ppermute | solution.py:126
  54.2 13.7 %collective-permute-start.3 = (bf16[512,256]{1,0:T(8,128)(2,1)S(1)}, bf16[512,256]{1,0:T(8,128)(2,1)S(1)}, u32[]{:S(2)}, u32[]{:S(2)}) collective-permute-start(bf16[512,256]{1,0:T(8,128)(2,1)S(1)} %get-tuple-element.21.refs_6_), channel_id=1, source_target_pairs={{0,384},{128,0},{256,128},{384,256},{1,385},{129,1},{257,129},{385... | collective-permute-start | bytes 786440 | tf_op jit(solution)/shard_map/ppermute | solution.py:126
  56.9 18.0 %collective-permute-start.2 = (bf16[512,256]{1,0:T(8,128)(2,1)S(1)}, bf16[512,256]{1,0:T(8,128)(2,1)S(1)}, u32[]{:S(2)}, u32[]{:S(2)}) collective-permute-start(bf16[512,256]{1,0:T(8,128)(2,1)S(1)} %get-tuple-element.22.refs_5_), channel_id=1, source_target_pairs={{0,384},{128,0},{256,128},{384,256},{1,385},{129,1},{257,129},{385... | collective-permute-start | bytes 786440 | tf_op jit(solution)/shard_map/ppermute | solution.py:127
  60.4 14.6 %collective-permute-start.6 = (bf16[512,256]{1,0:T(8,128)(2,1)S(1)}, bf16[512,256]{1,0:T(8,128)(2,1)S(1)}, u32[]{:S(2)}, u32[]{:S(2)}) collective-permute-start(bf16[512,256]{1,0:T(8,128)(2,1)S(1)} %get-tuple-element.21.refs_6_), channel_id=1, source_target_pairs={{0,128},{128,256},{256,384},{384,0},{1,129},{129,257},{257,385},{3... | collective-permute-start | bytes 786440 | tf_op jit(solution)/shard_map/ppermute | solution.py:127
  64.0 11.0 %collective-permute-start.4 = (bf16[512,256]{1,0:T(8,128)(2,1)S(1)}, bf16[512,256]{1,0:T(8,128)(2,1)S(1)}, u32[]{:S(2)}, u32[]{:S(2)}) collective-permute-start(bf16[512,256]{1,0:T(8,128)(2,1)S(1)} %collective-permute-done.1.after.refs_11_), channel_id=1, source_target_pairs={{0,128},{128,256},{256,384},{384,0},{1,129},{129,257},{257,385},{3... | collective-permute-start | bytes 786440 | tf_op jit(solution)/shard_map/ppermute | solution.py:128
  67.9 9.5 %collective-permute-start.5 = (bf16[512,256]{1,0:T(8,128)(2,1)S(1)}, bf16[512,256]{1,0:T(8,128)(2,1)S(1)}, u32[]{:S(2)}, u32[]{:S(2)}) collective-permute-start(bf16[512,256]{1,0:T(8,128)(2,1)S(1)} %collective-permute-done.3.refs_8_), channel_id=1, source_target_pairs={{0,384},{128,0},{256,128},{384,256},{1,385},{129,1},{257,129},{385... | collective-permute-start | bytes 786440 | tf_op jit(solution)/shard_map/ppermute | solution.py:128
  70.1 1.0 copy-start.1
  81.0 32.1 %all-to-all-start = ((bf16[4,512,256]{2,1,0:T(8,128)(2,1)}), bf16[4,512,256]{2,1,0:T(8,128)(2,1)S(1)}, u32[]{:S(2)}, u32[]{:S(2)}) async-start(bf16[4,512,256]{2,1,0:T(8,128)(2,1)} %get-tuple-element.17), calls=%async_computation | async-start | bytes 2097152 | tf_op jit(solution)/shard_map/all_to_all | solution.py:189
  85.5 65.3 %copy-start.5 = (f32[64,256]{1,0:T(8,128)S(1)}, f32[64,256]{1,0:T(8,128)}, u32[]{:S(2)}) copy-start(f32[64,256]{1,0:T(8,128)} %param.13) | copy-start | bytes 196612
  85.5 3.2 %collective-permute-start.7 = (f32[8,128]{1,0:T(8,128)S(1)}, f32[8,128]{1,0:T(8,128)S(1)}, u32[]{:S(2)}, u32[]{:S(2)}) collective-permute-start(f32[8,128]{1,0:T(8,128)S(1)} %get-tuple-element.18), channel_id=1, source_target_pairs={{0,1},{1,0},{2,3},{3,2},{4,5},{5,4},{6,7},{7,6},{8,9},{9,8},{10,11... | collective-permute-start | bytes 12296 | tf_op jit(solution)/shard_map/ppermute | solution.py:190
  88.6 5.5 %collective-permute-start.8 = (f32[8,128]{1,0:T(8,128)S(1)}, f32[8,128]{1,0:T(8,128)S(1)}, u32[]{:S(2)}, u32[]{:S(2)}) collective-permute-start(f32[8,128]{1,0:T(8,128)S(1)} %add.25), channel_id=1, source_target_pairs={{0,2},{2,0},{4,6},{6,4},{1,3},{3,1},{5,7},{7,5},{8,10},{10,8},{12,... | collective-permute-start | bytes 12296 | tf_op jit(solution)/shard_map/ppermute | solution.py:193
  94.2 6.7 %collective-permute-start.9 = (f32[8,128]{1,0:T(8,128)S(1)}, f32[8,128]{1,0:T(8,128)S(1)}, u32[]{:S(2)}, u32[]{:S(2)}) collective-permute-start(f32[8,128]{1,0:T(8,128)S(1)} %add.26), channel_id=1, source_target_pairs={{0,6},{2,4},{4,2},{6,0},{1,7},{3,5},{5,3},{7,1},{8,14},{10,12},{12... | collective-permute-start | bytes 12296 | tf_op jit(solution)/shard_map/ppermute | solution.py:193
  100.9 5.5 %collective-permute-start.10 = (f32[8,128]{1,0:T(8,128)S(1)}, f32[8,128]{1,0:T(8,128)S(1)}, u32[]{:S(2)}, u32[]{:S(2)}) collective-permute-start(f32[8,128]{1,0:T(8,128)S(1)} %add.27), channel_id=1, source_target_pairs={{0,128},{128,0},{256,384},{384,256},{1,129},{129,1},{257,385},{385... | collective-permute-start | bytes 12296 | tf_op jit(solution)/shard_map/ppermute | solution.py:193
  106.4 6.7 %collective-permute-start.11 = (f32[8,128]{1,0:T(8,128)S(1)}, f32[8,128]{1,0:T(8,128)S(1)}, u32[]{:S(2)}, u32[]{:S(2)}) collective-permute-start(f32[8,128]{1,0:T(8,128)S(1)} %add.28), channel_id=1, source_target_pairs={{0,384},{128,256},{256,128},{384,0},{1,385},{129,257},{257,129},{3... | collective-permute-start | bytes 12296 | tf_op jit(solution)/shard_map/ppermute | solution.py:193
  117.4 8.3 %collective-permute-start.12 = (f16[8,64,256]{2,1,0:T(8,128)(2,1)S(1)}, f16[8,64,256]{2,1,0:T(8,128)(2,1)S(1)}, u32[]{:S(2)}, u32[]{:S(2)}) collective-permute-start(f16[8,64,256]{2,1,0:T(8,128)(2,1)S(1)} %multiply_convert_fusion.1), channel_id=1, source_target_pairs={{0,8},{8,0},{1,9},{9,1},{2,10},{10,2},{3,11},{11,3},{4,12},{12,4},... | collective-permute-start | bytes 786440 | tf_op jit(solution)/shard_map/ppermute | solution.py:215
  126.6 24.1 %all-to-all-start.1 = ((f16[8,64,256]{2,1,0:T(8,128)(2,1)}), f16[8,64,256]{2,1,0:T(8,128)(2,1)S(1)}, u32[]{:S(2)}, u32[]{:S(2)}) async-start(f16[8,64,256]{2,1,0:T(8,128)(2,1)} %multiply_convert_fusion), calls=%async_computation.1 | async-start | bytes 524288 | tf_op jit(solution)/shard_map/all_to_all | solution.py:217
  150.8 0.7 copy-start.4
Sparse Core Ops, SparseCore 0:
  10.2 43.8 all-gather.3
  56.2 42.2 all-gather.5

commit v8 on v7

--- a/solution.py
+++ b/solution.py
@@ -15,6 +15,7 @@
 F16 = jnp.float16
 SCALE = 256.0
 AFTER = 6
+TAIL = 16
 MIB = 1024 * 1024
 
 
@@ -62,7 +63,6 @@
     w_refs, (g_ref, sq_ref) = refs[5:-2], refs[-2:]
     recs, rows, _ = gram_ref.shape
     events = rows // t_ref.shape[1]
-    row = lax.broadcasted_iota(jnp.int32, sq_ref.shape, 0)
     lane = lax.broadcasted_iota(jnp.int32, sq_ref.shape, 1)
     out = jnp.zeros(sq_ref.shape, F32)
     for r in range(recs):
@@ -77,20 +77,38 @@
             wgt = 1.0 / (t_ref[r : r + 1, a : a + 1] + 0.25)
             parts.append(wgt * diff[a * events : (a + 1) * events, :])
         g = (jnp.concatenate(parts, axis=0) * (1.0 / math.sqrt(rows))).astype(BF16)
-        for k in range(g_ref.shape[0]):
-            g_ref[k, at, :] = g
+        g_ref[at, :] = g
         out = jnp.where(lane == r, jnp.sum(gram_ref[r] * dot(g, g, 1, 1)), out)
-    sq_ref[...] = jnp.where(row == lax.axis_index("x"), out, 0.0)
-
-
-def sum_kernel(h_hbm, g_ref, sq_ref, keep_ref, send_ref, h_buf, acc, sems, *, recs, bound):
+    sq_ref[...] = out
+
+
+def pack_kernel(sq_ref, g_ref, o_ref, *, bound):
+    rows = g_ref.shape[0]
+    norms = jnp.sqrt(jnp.sum(sq_ref[...], axis=0, keepdims=True))
+    clip = bound / jnp.maximum(norms, bound)
+    high = clip.astype(BF16).astype(F32)
+    mid = (clip - high).astype(BF16).astype(F32)
+    low = clip - high - mid
+    shape = (TAIL, clip.shape[1])
+    row = lax.broadcasted_iota(jnp.int32, shape, 0)
+    tail = jnp.zeros(shape, F32)
+    for k, term in enumerate((high, mid, low)):
+        tail = jnp.where(row == k, jnp.broadcast_to(term, shape), tail)
+    tail = jnp.concatenate([tail] * (o_ref.shape[2] // clip.shape[1]), axis=1).astype(BF16)
+    for k in range(o_ref.shape[0]):
+        o_ref[k, 0:rows, :] = g_ref[...]
+        o_ref[k, rows : rows + TAIL, :] = tail
+
+
+def sum_kernel(h_hbm, g_ref, keep_ref, send_ref, h_buf, acc, sems, *, recs):
     copies = fetch(h_hbm, h_buf, sems)
     blocks, total_rows, feats = h_buf.shape
     nx = g_ref.shape[0]
     rows = total_rows // recs
     per = blocks // nx
     for x in range(nx):
-        clip = bound / jnp.maximum(jnp.sqrt(sq_ref[x : x + 1, :]), bound)
+        tail = g_ref[x, total_rows : total_rows + TAIL, :].astype(F32)
+        clip = jnp.sum(tail, axis=0, keepdims=True)
         for j in range(per):
             copies[x * per + j].wait()
             total = None
@@ -175,8 +193,8 @@
         in_specs=[vmem] * 13,
         out_specs=[vmem, vmem],
         out_shape=[
-            jax.ShapeDtypeStruct((nx, recs * rows, local_out), BF16),
-            jax.ShapeDtypeStruct((8, 128), F32),
+            jax.ShapeDtypeStruct((recs * rows, local_out), BF16),
+            jax.ShapeDtypeStruct((nt, 128), F32),
         ],
         compiler_params=params(),
         cost_estimate=pl.CostEstimate(
@@ -186,17 +204,19 @@
         ),
     )(h, n, gram, bias, times, *w_blocks)
 
-    all_grads = lax.all_to_all(grads, "x", 0, 0)
-    sq = sq + lax.ppermute(sq, "core", [(0, 1), (1, 0)])
-    for axis in ("y", "x"):
-        for pairs in ((1, 0, 3, 2), (3, 2, 1, 0)):
-            sq = sq + lax.ppermute(sq, axis, list(enumerate(pairs)))
-    norms = jnp.sqrt(lax.dynamic_index_in_dim(sq, lax.axis_index("x"), 0, False)[:recs])
-
+    sq_all = lax.all_to_all(sq.reshape(nt, 1, 128), tensor, 0, 0).reshape(nt, 128)
+    norms = jnp.sqrt(jnp.sum(sq_all[:, :recs], axis=0))
+
+    packed = pl.pallas_call(
+        functools.partial(pack_kernel, bound=bound),
+        out_shape=jax.ShapeDtypeStruct((nx, recs * rows + TAIL, local_out), BF16),
+        compiler_params=params(),
+    )(sq_all, grads)
+    packed = lax.all_to_all(packed, "x", 0, 0)
     block = weight.shape[0]
     keep, send = pl.pallas_call(
-        functools.partial(sum_kernel, recs=recs, bound=bound),
-        in_specs=[hbm, vmem, vmem],
+        functools.partial(sum_kernel, recs=recs),
+        in_specs=[hbm, vmem],
         out_specs=[vmem, vmem],
         out_shape=[jax.ShapeDtypeStruct((ng, block, local_out), F32)] * 2,
         scratch_shapes=[
@@ -210,7 +230,7 @@
             bytes_accessed=2 * recs * rows * (D + nx * local_out) + 4 * D // nx * local_out,
             transcendentals=0,
         ),
-    )(mine.reshape(nt, recs * rows, feats), all_grads, sq)
+    )(mine.reshape(nt, recs * rows, feats), packed)
 
     got = lax.ppermute(root(send).astype(F16), "zp", [(0, 1), (1, 0)])
     sent = root(keep + unroot(got)).astype(F16)

time: 159 us -> 158 us (level)
  the two profiles are of different devices: /device:TPU:30 before, /device:TPU:2 now
where the time goes in v8:
time: 158 us
  blocking collectives  47.2 us (30%)
  waiting for transfers between devices  41.9 us (27%)
  starting transfers between devices  37.2 us (24%)
  between operations  14.2 us (9%)
  Pallas kernels  11.9 us (8%)
  other arithmetic  2.56 us (2%)
  local copies, waits for them, and re-layouts  2.38 us (2%)
    all_gather x1, blocking collectives, on_device(): wz = lax.all_gather(weight, ('zg', 'zp'), axis=0, tiled=True)  38.8 us
    all_to_all x1, waiting for transfers between devices, on_device(): clipped_sum = jnp.sum(unroot(lax.all_to_all(sent, 'zg', 0, 0)), axis=0)  18.7 us
    all_to_all x1, waiting for transfers between devices, on_device(): packed = lax.all_to_all(packed, 'x', 0, 0)  9.07 us
    all_to_all x1, blocking collectives, on_device(): lax.all_to_all(sq.reshape(nt, 1, 128), tensor, 0, 0).reshape(nt, 128)  8.38 us
    ppermute x1, waiting for transfers between devices, on_device(): got = lax.ppermute(root(send).astype(F16), 'zp', [(0, 1), (1, 0)])  6.96 us
    all_to_all x1, starting transfers between devices, on_device(): clipped_sum = jnp.sum(unroot(lax.all_to_all(sent, 'zg', 0, 0)), axis=0)  6.77 us
    ppermute x2, starting transfers between devices, ring_gather(): a3, b1 = (lax.ppermute(a, 'x', up), lax.ppermute(b, 'x', down))  6.7 us
    all_to_all x1, starting transfers between devices, on_device(): packed = lax.all_to_all(packed, 'x', 0, 0)  6.61 us
  transfers between devices with their start and end apart: 12, of which 5 were waited for; matrix products, arithmetic and copies ran while one was open for 1% of the time, Pallas kernels for 5%

profile of v8, /device:TPU:2, one launch (start us, length us, event | category | flops | bytes accessed | tf_op | source)
XLA Modules:
  0.0 157.5 jit_solution(12811321339306259834)
XLA Ops:
  8.0 3.5 %collective-permute-start = (bf16[512,512]{1,0:T(8,128)(2,1)}, bf16[512,512]{1,0:T(8,128)(2,1)S(1)}, u32[]{:S(2)}, u32[]{:S(2)}) collective-permute-start(bf16[512,512]{1,0:T(8,128)(2,1)} %bitcast.16), channel_id=1, source_target_pairs={{0,0},{2,128},{4,256},{6,384},{128,2},{130,130},{132,258},{134,386... | collective-permute-start | bytes 1572872 | tf_op jit(solution)/shard_map/ppermute | solution.py:163
  11.4 38.8 %all_gather.12 = bf16[1024,256]{1,0:T(8,128)(2,1)S(1)} all-gather(bf16[64,256]{1,0:T(8,128)(2,1)} %param.12), channel_id=1, replica_groups=mesh['x'=4,'zg'=8,'zp'=2,'y'=4,'core'=2] {'zg','zp'}, dimensions={0}, use_global_device_ids=true | all-gather | bytes 557056 | tf_op jit(solution)/shard_map/all_gather | solution.py:165
  50.2 0.8 copy-done.3
  51.1 4.8 %collective-permute-start.1 = (bf16[512,256]{1,0:T(8,128)(2,1)S(1)}, bf16[512,256]{1,0:T(8,128)(2,1)S(1)}, u32[]{:S(2)}, u32[]{:S(2)}) collective-permute-start(bf16[512,256]{1,0:T(8,128)(2,1)S(1)} %get-tuple-element.22.refs_5_), channel_id=1, source_target_pairs={{0,128},{128,256},{256,384},{384,0},{1,129},{129,257},{257,385},{3... | collective-permute-start | bytes 786440 | tf_op jit(solution)/shard_map/ppermute | solution.py:144
  55.9 1.9 %collective-permute-start.3 = (bf16[512,256]{1,0:T(8,128)(2,1)S(1)}, bf16[512,256]{1,0:T(8,128)(2,1)S(1)}, u32[]{:S(2)}, u32[]{:S(2)}) collective-permute-start(bf16[512,256]{1,0:T(8,128)(2,1)S(1)} %get-tuple-element.21.refs_6_), channel_id=1, source_target_pairs={{0,384},{128,0},{256,128},{384,256},{1,385},{129,1},{257,129},{385... | collective-permute-start | bytes 786440 | tf_op jit(solution)/shard_map/ppermute | solution.py:144
  58.6 3.5 %collective-permute-start.2 = (bf16[512,256]{1,0:T(8,128)(2,1)S(1)}, bf16[512,256]{1,0:T(8,128)(2,1)S(1)}, u32[]{:S(2)}, u32[]{:S(2)}) collective-permute-start(bf16[512,256]{1,0:T(8,128)(2,1)S(1)} %get-tuple-element.22.refs_5_), channel_id=1, source_target_pairs={{0,384},{128,0},{256,128},{384,256},{1,385},{129,1},{257,129},{385... | collective-permute-start | bytes 786440 | tf_op jit(solution)/shard_map/ppermute | solution.py:145
  62.1 2.3 %collective-permute-start.6 = (bf16[512,256]{1,0:T(8,128)(2,1)S(1)}, bf16[512,256]{1,0:T(8,128)(2,1)S(1)}, u32[]{:S(2)}, u32[]{:S(2)}) collective-permute-start(bf16[512,256]{1,0:T(8,128)(2,1)S(1)} %get-tuple-element.21.refs_6_), channel_id=1, source_target_pairs={{0,128},{128,256},{256,384},{384,0},{1,129},{129,257},{257,385},{3... | collective-permute-start | bytes 786440 | tf_op jit(solution)/shard_map/ppermute | solution.py:145
  64.5 3.9 %collective-permute-start.4 = (bf16[512,256]{1,0:T(8,128)(2,1)S(1)}, bf16[512,256]{1,0:T(8,128)(2,1)S(1)}, u32[]{:S(2)}, u32[]{:S(2)}) collective-permute-start(bf16[512,256]{1,0:T(8,128)(2,1)S(1)} %collective-permute-done.1.after.refs_11_), channel_id=1, source_target_pairs={{0,128},{128,256},{256,384},{384,0},{1,129},{129,257},{257,385},{3... | collective-permute-start | bytes 786440 | tf_op jit(solution)/shard_map/ppermute | solution.py:146
  68.4 1.9 %collective-permute-start.5 = (bf16[512,256]{1,0:T(8,128)(2,1)S(1)}, bf16[512,256]{1,0:T(8,128)(2,1)S(1)}, u32[]{:S(2)}, u32[]{:S(2)}) collective-permute-start(bf16[512,256]{1,0:T(8,128)(2,1)S(1)} %collective-permute-done.3.refs_8_), channel_id=1, source_target_pairs={{0,384},{128,0},{256,128},{384,256},{1,385},{129,1},{257,129},{385... | collective-permute-start | bytes 786440 | tf_op jit(solution)/shard_map/ppermute | solution.py:146
  70.6 1.0 copy-done.1
  71.5 3.9 %shard_map.94 = (bf16[8,512,512]{2,1,0:T(8,128)(2,1)S(1)}, bf16[2,256,256]{2,1,0:T(8,128)(2,1)S(1)}, f32[2,256,256]{2,1,0:T(8,128)S(1)}) custom-call(bf16[8,512,512]{2,1,0:T(8,128)(2,1)} %all-gather.4.cloned.1.call-done.h_hbm, bf16[2,256,256]{2,1,0:T(8,128)(2,1)S(1)} %bitcast.10, bf16[512,256]{1,0:T(8,128)(2,1)S(1)} %collective-permute-done.1.after.refs_11_), custom_call_target="tpu_custom_call" | custom-call | flops 1073741824 | bytes 8388608 | tf_op jit(solution)/shard_map/pallas_call | solution.py:176
  75.5 1.4 collective-permute-done.5.refs_10_
  76.9 2.8 %shard_map.95 = (bf16[512,256]{1,0:T(8,128)(2,1)S(1)}, f32[8,128]{1,0:T(8,128)S(1)}) custom-call(bf16[8,512,512]{2,1,0:T(8,128)(2,1)S(1)} %get-tuple-element.14.refs_0_, bf16[2,256,256]{2,1,0:T(8,128)(2,1)S(1)} %get-tuple-element.15.refs_1_, f32[2,256,256]{2,1,0:T(8,128)S(1)} %get-tuple-element.16.refs_2_, f32[2,256]{1,0:T(2,128)S(1)} %fusion.7.refs_3_, ...), custom_call_target="tpu_custom_call" | custom-call | flops 1073741824 | bytes 6291456 | tf_op jit(solution)/shard_map/pallas_call | solution.py:191
  79.7 8.4 %all_to_all.15 = f32[8,1,128]{2,1,0:T(1,128)S(1)} all-to-all(f32[8,1,128]{2,1,0:T(1,128)S(1)} %bitcast.13), channel_id=1, replica_groups=mesh['x'=4,'zg'=8,'zp'=2,'y'=4,'core'=2] {'y','core'}, dimensions={0} | all-to-all | bytes 8192 | tf_op jit(solution)/shard_map/all_to_all | solution.py:207
  88.1 1.1 shard_map.96
  89.2 6.6 %all-to-all-start.1 = ((bf16[4,528,256]{2,1,0:T(8,128)(2,1)}), bf16[4,528,256]{2,1,0:T(8,128)(2,1)S(1)}, u32[]{:S(2)}, u32[]{:S(2)}) async-start(bf16[4,528,256]{2,1,0:T(8,128)(2,1)} %shard_map.96), calls=%async_computation.1 | async-start | bytes 2162688 | tf_op jit(solution)/shard_map/all_to_all | solution.py:215
  95.8 5.0 %all-gather.6.cloned.1.call-done = bf16[4096,512]{1,0:T(8,128)(2,1)} async-done(((bf16[512,512]{1,0:T(8,128)(2,1)}), bf16[4096,512]{1,0:T(8,128)(2,1)}) %all-gather.6.cloned.1.call-update) | async-done | bytes 4194320 | tf_op jit(solution)/shard_map/all_gather | solution.py:167
  100.8 9.1 %all-to-all-done.1.g_ref = bf16[4,528,256]{2,1,0:T(8,128)(2,1)S(1)} async-done(((bf16[4,528,256]{2,1,0:T(8,128)(2,1)}), bf16[4,528,256]{2,1,0:T(8,128)(2,1)S(1)}, u32[]{:S(2)}, u32[]{:S(2)}) %all-to-all-start.1) | async-done | bytes 1081376 | tf_op jit(solution)/shard_map/all_to_all | solution.py:215
  109.9 4.1 %shard_map.97 = (f32[8,64,256]{2,1,0:T(8,128)S(1)}, f32[8,64,256]{2,1,0:T(8,128)S(1)}) custom-call(bf16[8,512,512]{2,1,0:T(8,128)(2,1)} %bitcast.14, bf16[4,528,256]{2,1,0:T(8,128)(2,1)S(1)} %all-to-all-done.1.g_ref), custom_call_target="tpu_custom_call" | custom-call | flops 1073741824 | bytes 6291456 | tf_op jit(solution)/shard_map/pallas_call | solution.py:217
  114.2 1.9 %collective-permute-start.7 = (f16[8,64,256]{2,1,0:T(8,128)(2,1)S(1)}, f16[8,64,256]{2,1,0:T(8,128)(2,1)S(1)}, u32[]{:S(2)}, u32[]{:S(2)}) collective-permute-start(f16[8,64,256]{2,1,0:T(8,128)(2,1)S(1)} %multiply_convert_fusion.1), channel_id=1, source_target_pairs={{0,8},{8,0},{1,9},{9,1},{2,10},{10,2},{3,11},{11,3},{4,12},{12,4},... | collective-permute-start | bytes 786440 | tf_op jit(solution)/shard_map/ppermute | solution.py:235
  116.1 7.0 %collective-permute-done.7 = f16[8,64,256]{2,1,0:T(8,128)(2,1)S(1)} collective-permute-done((f16[8,64,256]{2,1,0:T(8,128)(2,1)S(1)}, f16[8,64,256]{2,1,0:T(8,128)(2,1)S(1)}, u32[]{:S(2)}, u32[]{:S(2)}) %collective-permute-start.7) | collective-permute-done | bytes 262176 | tf_op jit(solution)/shard_map/ppermute | solution.py:235
  123.1 0.9 multiply_convert_fusion
  124.0 6.8 %all-to-all-start.2 = ((f16[8,64,256]{2,1,0:T(8,128)(2,1)}), f16[8,64,256]{2,1,0:T(8,128)(2,1)S(1)}, u32[]{:S(2)}, u32[]{:S(2)}) async-start(f16[8,64,256]{2,1,0:T(8,128)(2,1)} %multiply_convert_fusion), calls=%async_computation.2 | async-start | bytes 524288 | tf_op jit(solution)/shard_map/all_to_all | solution.py:237
  131.3 18.7 %all-to-all-done.2 = f16[8,64,256]{2,1,0:T(8,128)(2,1)S(1)} async-done(((f16[8,64,256]{2,1,0:T(8,128)(2,1)}), f16[8,64,256]{2,1,0:T(8,128)(2,1)S(1)}, u32[]{:S(2)}, u32[]{:S(2)}) %all-to-all-start.2) | async-done | bytes 262176 | tf_op jit(solution)/shard_map/all_to_all | solution.py:237
  (29 shorter events, 3.2 us)
Async XLA Ops:
  7.2 63.2 %copy-start = (bf16[1024,256]{1,0:T(8,128)(2,1)S(1)}, bf16[1024,256]{1,0:T(8,128)(2,1)}, u32[]{:S(2)}) copy-start(bf16[1024,256]{1,0:T(8,128)(2,1)} %param.11) | copy-start | bytes 1572868
  7.2 69.7 %copy-start.2 = (f32[2,4]{1,0:T(2,128)S(1)}, f32[2,4]{1,0:T(2,128)}, u32[]{:S(2)}) copy-start(f32[2,4]{1,0:T(2,128)} %refs_4_.1) | copy-start | bytes 100
  7.2 63.4 %all-gather.4.cloned.1.call-start = ((), (), s32[]{:S(2)}) async-start(), calls=%async_computation.3 | async-start | bytes 4718592 | tf_op jit(solution)/shard_map/all_gather | solution.py:161
  7.9 92.9 %all-gather.6.cloned.1.call-start = ((), (), s32[]{:S(2)}) async-start(), calls=%async_computation.4 | async-start | bytes 4718592 | tf_op jit(solution)/shard_map/all_gather | solution.py:167
  8.0 42.2 %collective-permute-start = (bf16[512,512]{1,0:T(8,128)(2,1)}, bf16[512,512]{1,0:T(8,128)(2,1)S(1)}, u32[]{:S(2)}, u32[]{:S(2)}) collective-permute-start(bf16[512,512]{1,0:T(8,128)(2,1)} %bitcast.16), channel_id=1, source_target_pairs={{0,0},{2,128},{4,256},{6,384},{128,2},{130,130},{132,258},{134,386... | collective-permute-start | bytes 1572872 | tf_op jit(solution)/shard_map/ppermute | solution.py:163
  50.2 0.8 copy-start.3
  51.1 13.4 %collective-permute-start.1 = (bf16[512,256]{1,0:T(8,128)(2,1)S(1)}, bf16[512,256]{1,0:T(8,128)(2,1)S(1)}, u32[]{:S(2)}, u32[]{:S(2)}) collective-permute-start(bf16[512,256]{1,0:T(8,128)(2,1)S(1)} %get-tuple-element.22.refs_5_), channel_id=1, source_target_pairs={{0,128},{128,256},{256,384},{384,0},{1,129},{129,257},{257,385},{3... | collective-permute-start | bytes 786440 | tf_op jit(solution)/shard_map/ppermute | solution.py:144
  55.9 12.5 %collective-permute-start.3 = (bf16[512,256]{1,0:T(8,128)(2,1)S(1)}, bf16[512,256]{1,0:T(8,128)(2,1)S(1)}, u32[]{:S(2)}, u32[]{:S(2)}) collective-permute-start(bf16[512,256]{1,0:T(8,128)(2,1)S(1)} %get-tuple-element.21.refs_6_), channel_id=1, source_target_pairs={{0,384},{128,0},{256,128},{384,256},{1,385},{129,1},{257,129},{385... | collective-permute-start | bytes 786440 | tf_op jit(solution)/shard_map/ppermute | solution.py:144
  58.6 16.8 %collective-permute-start.2 = (bf16[512,256]{1,0:T(8,128)(2,1)S(1)}, bf16[512,256]{1,0:T(8,128)(2,1)S(1)}, u32[]{:S(2)}, u32[]{:S(2)}) collective-permute-start(bf16[512,256]{1,0:T(8,128)(2,1)S(1)} %get-tuple-element.22.refs_5_), channel_id=1, source_target_pairs={{0,384},{128,0},{256,128},{384,256},{1,385},{129,1},{257,129},{385... | collective-permute-start | bytes 786440 | tf_op jit(solution)/shard_map/ppermute | solution.py:145
  62.1 13.3 %collective-permute-start.6 = (bf16[512,256]{1,0:T(8,128)(2,1)S(1)}, bf16[512,256]{1,0:T(8,128)(2,1)S(1)}, u32[]{:S(2)}, u32[]{:S(2)}) collective-permute-start(bf16[512,256]{1,0:T(8,128)(2,1)S(1)} %get-tuple-element.21.refs_6_), channel_id=1, source_target_pairs={{0,128},{128,256},{256,384},{384,0},{1,129},{129,257},{257,385},{3... | collective-permute-start | bytes 786440 | tf_op jit(solution)/shard_map/ppermute | solution.py:145
  64.5 11.0 %collective-permute-start.4 = (bf16[512,256]{1,0:T(8,128)(2,1)S(1)}, bf16[512,256]{1,0:T(8,128)(2,1)S(1)}, u32[]{:S(2)}, u32[]{:S(2)}) collective-permute-start(bf16[512,256]{1,0:T(8,128)(2,1)S(1)} %collective-permute-done.1.after.refs_11_), channel_id=1, source_target_pairs={{0,128},{128,256},{256,384},{384,0},{1,129},{129,257},{257,385},{3... | collective-permute-start | bytes 786440 | tf_op jit(solution)/shard_map/ppermute | solution.py:146
  68.4 8.5 %collective-permute-start.5 = (bf16[512,256]{1,0:T(8,128)(2,1)S(1)}, bf16[512,256]{1,0:T(8,128)(2,1)S(1)}, u32[]{:S(2)}, u32[]{:S(2)}) collective-permute-start(bf16[512,256]{1,0:T(8,128)(2,1)S(1)} %collective-permute-done.3.refs_8_), channel_id=1, source_target_pairs={{0,384},{128,0},{256,128},{384,256},{1,385},{129,1},{257,129},{385... | collective-permute-start | bytes 786440 | tf_op jit(solution)/shard_map/ppermute | solution.py:146
  70.6 1.0 copy-start.1
  89.2 20.7 %all-to-all-start.1 = ((bf16[4,528,256]{2,1,0:T(8,128)(2,1)}), bf16[4,528,256]{2,1,0:T(8,128)(2,1)S(1)}, u32[]{:S(2)}, u32[]{:S(2)}) async-start(bf16[4,528,256]{2,1,0:T(8,128)(2,1)} %shard_map.96), calls=%async_computation.1 | async-start | bytes 2162688 | tf_op jit(solution)/shard_map/all_to_all | solution.py:215
  95.8 54.2 %copy-start.5 = (f32[64,256]{1,0:T(8,128)S(1)}, f32[64,256]{1,0:T(8,128)}, u32[]{:S(2)}) copy-start(f32[64,256]{1,0:T(8,128)} %param.13) | copy-start | bytes 196612
  114.2 8.9 %collective-permute-start.7 = (f16[8,64,256]{2,1,0:T(8,128)(2,1)S(1)}, f16[8,64,256]{2,1,0:T(8,128)(2,1)S(1)}, u32[]{:S(2)}, u32[]{:S(2)}) collective-permute-start(f16[8,64,256]{2,1,0:T(8,128)(2,1)S(1)} %multiply_convert_fusion.1), channel_id=1, source_target_pairs={{0,8},{8,0},{1,9},{9,1},{2,10},{10,2},{3,11},{11,3},{4,12},{12,4},... | collective-permute-start | bytes 786440 | tf_op jit(solution)/shard_map/ppermute | solution.py:235
  124.0 26.0 %all-to-all-start.2 = ((f16[8,64,256]{2,1,0:T(8,128)(2,1)}), f16[8,64,256]{2,1,0:T(8,128)(2,1)S(1)}, u32[]{:S(2)}, u32[]{:S(2)}) async-start(f16[8,64,256]{2,1,0:T(8,128)(2,1)} %multiply_convert_fusion), calls=%async_computation.2 | async-start | bytes 524288 | tf_op jit(solution)/shard_map/all_to_all | solution.py:237
  150.0 0.7 copy-start.4
Sparse Core Ops, SparseCore 0:
  10.2 44.2 all-gather.3
  56.6 44.1 all-gather.5

commit v9 on v8

--- a/solution.py
+++ b/solution.py
@@ -162,7 +162,10 @@
     swap = [(a * nx + b, b * nx + a) for a in range(nx) for b in range(nx)]
     swapped = lax.ppermute(own, ("x", "y"), swap)
 
-    wz = lax.all_gather(weight, ("zg", "zp"), axis=0, tiled=True)
+    other = lax.ppermute(weight, "zp", [(0, 1), (1, 0)])
+    odd = lax.axis_index("zp") == 1
+    pair = jnp.concatenate([jnp.where(odd, other, weight), jnp.where(odd, weight, other)], axis=0)
+    wz = lax.all_gather(pair, "zg", axis=0, tiled=True)
     swapped, wz = lax.optimization_barrier((swapped, wz))
     mine = lax.all_gather(swapped, tensor, axis=0, tiled=False)
     w_blocks = ring_gather(wz)

time: 158 us -> 162 us (1.025)
  starting transfers between devices: 37.2 us -> 42.9 us
  blocking collectives: 47.2 us -> 44.4 us
    ppermute x0 -> x1, starting transfers between devices: none -> 3.83 us  [on_device(): other = lax.ppermute(weight, 'zp', [(0, 1), (1, 0)])]
    all_gather x1, blocking collectives: 38.8 us -> 36.5 us  [on_device(): wz = lax.all_gather(pair, 'zg', axis=0, tiled=True)]
  transfers between devices with their start and end apart: 12 -> 13, of which waited for: 5 -> 5; matrix products, arithmetic and copies ran while one was open for 1% -> 1% of each run, Pallas kernels for 5% -> 5%
where the time goes in v9:
time: 162 us; the launch traced here: 161 us
  blocking collectives  44.4 us (27%)
  starting transfers between devices  42.9 us (26%)
  waiting for transfers between devices  41.5 us (26%)
  between operations  14.3 us (9%)
  Pallas kernels  12 us (7%)
  other arithmetic  3.34 us (2%)
  local copies, waits for them, and re-layouts  2.39 us (1%)
    all_gather x1, blocking collectives, on_device(): wz = lax.all_gather(pair, 'zg', axis=0, tiled=True)  36.5 us
    all_to_all x1, waiting for transfers between devices, on_device(): clipped_sum = jnp.sum(unroot(lax.all_to_all(sent, 'zg', 0, 0)), axis=0)  18.9 us
    all_to_all x1, waiting for transfers between devices, on_device(): packed = lax.all_to_all(packed, 'x', 0, 0)  9.16 us
    all_to_all x1, blocking collectives, on_device(): lax.all_to_all(sq.reshape(nt, 1, 128), tensor, 0, 0).reshape(nt, 128)  7.92 us
    all_to_all x1, starting transfers between devices, on_device(): clipped_sum = jnp.sum(unroot(lax.all_to_all(sent, 'zg', 0, 0)), axis=0)  7.23 us
    ppermute x2, starting transfers between devices, ring_gather(): a3, b1 = (lax.ppermute(a, 'x', up), lax.ppermute(b, 'x', down))  7.02 us
    all_to_all x1, starting transfers between devices, on_device(): packed = lax.all_to_all(packed, 'x', 0, 0)  6.94 us
    ppermute x1, waiting for transfers between devices, on_device(): got = lax.ppermute(root(send).astype(F16), 'zp', [(0, 1), (1, 0)])  6.22 us
  transfers between devices with their start and end apart: 13, of which 5 were waited for; matrix products, arithmetic and copies ran while one was open for 1% of the time, Pallas kernels for 5%

profile of v9, /device:TPU:2, one launch (start us, length us, event | category | flops | bytes accessed | tf_op | source)
XLA Modules:
  0.0 160.9 jit_solution(8159899117447194304)
XLA Ops:
  8.0 3.8 %collective-permute-start.1 = (bf16[64,256]{1,0:T(8,128)(2,1)}, bf16[64,256]{1,0:T(8,128)(2,1)S(1)}, u32[]{:S(2)}, u32[]{:S(2)}) collective-permute-start(bf16[64,256]{1,0:T(8,128)(2,1)} %param.12), channel_id=1, source_target_pairs={{0,8},{8,0},{1,9},{9,1},{2,10},{10,2},{3,11},{11,3},{4,12},{12,4},... | collective-permute-start | bytes 98312 | tf_op jit(solution)/shard_map/ppermute | solution.py:165
  11.8 3.5 %collective-permute-start = (bf16[512,512]{1,0:T(8,128)(2,1)}, bf16[512,512]{1,0:T(8,128)(2,1)S(1)}, u32[]{:S(2)}, u32[]{:S(2)}) collective-permute-start(bf16[512,512]{1,0:T(8,128)(2,1)} %bitcast.16), channel_id=1, source_target_pairs={{0,0},{2,128},{4,256},{6,384},{128,2},{130,130},{132,258},{134,386... | collective-permute-start | bytes 1572872 | tf_op jit(solution)/shard_map/ppermute | solution.py:163
  16.1 36.5 %all_gather.12 = bf16[1024,256]{1,0:T(8,128)(2,1)S(1)} all-gather(bf16[128,256]{1,0:T(8,128)(2,1)S(1)} %pad_maximum_fusion), channel_id=1, replica_groups=mesh['x'=4,'zg'=8,'zp'=2,'y'=4,'core'=2] {'zg'}, dimensions={0}, use_global_device_ids=true | all-gather | bytes 589824 | tf_op jit(solution)/shard_map/all_gather | solution.py:168
  53.5 5.1 %collective-permute-start.2 = (bf16[512,256]{1,0:T(8,128)(2,1)S(1)}, bf16[512,256]{1,0:T(8,128)(2,1)S(1)}, u32[]{:S(2)}, u32[]{:S(2)}) collective-permute-start(bf16[512,256]{1,0:T(8,128)(2,1)S(1)} %get-tuple-element.22.refs_5_), channel_id=1, source_target_pairs={{0,128},{128,256},{256,384},{384,0},{1,129},{129,257},{257,385},{3... | collective-permute-start | bytes 786440 | tf_op jit(solution)/shard_map/ppermute | solution.py:144
  58.6 1.9 %collective-permute-start.4 = (bf16[512,256]{1,0:T(8,128)(2,1)S(1)}, bf16[512,256]{1,0:T(8,128)(2,1)S(1)}, u32[]{:S(2)}, u32[]{:S(2)}) collective-permute-start(bf16[512,256]{1,0:T(8,128)(2,1)S(1)} %get-tuple-element.21.refs_6_), channel_id=1, source_target_pairs={{0,384},{128,0},{256,128},{384,256},{1,385},{129,1},{257,129},{385... | collective-permute-start | bytes 786440 | tf_op jit(solution)/shard_map/ppermute | solution.py:144
  61.3 3.6 %collective-permute-start.3 = (bf16[512,256]{1,0:T(8,128)(2,1)S(1)}, bf16[512,256]{1,0:T(8,128)(2,1)S(1)}, u32[]{:S(2)}, u32[]{:S(2)}) collective-permute-start(bf16[512,256]{1,0:T(8,128)(2,1)S(1)} %get-tuple-element.22.refs_5_), channel_id=1, source_target_pairs={{0,384},{128,0},{256,128},{384,256},{1,385},{129,1},{257,129},{385... | collective-permute-start | bytes 786440 | tf_op jit(solution)/shard_map/ppermute | solution.py:145
  64.9 2.3 %collective-permute-start.7 = (bf16[512,256]{1,0:T(8,128)(2,1)S(1)}, bf16[512,256]{1,0:T(8,128)(2,1)S(1)}, u32[]{:S(2)}, u32[]{:S(2)}) collective-permute-start(bf16[512,256]{1,0:T(8,128)(2,1)S(1)} %get-tuple-element.21.refs_6_), channel_id=1, source_target_pairs={{0,128},{128,256},{256,384},{384,0},{1,129},{129,257},{257,385},{3... | collective-permute-start | bytes 786440 | tf_op jit(solution)/shard_map/ppermute | solution.py:145
  67.2 3.9 %collective-permute-start.5 = (bf16[512,256]{1,0:T(8,128)(2,1)S(1)}, bf16[512,256]{1,0:T(8,128)(2,1)S(1)}, u32[]{:S(2)}, u32[]{:S(2)}) collective-permute-start(bf16[512,256]{1,0:T(8,128)(2,1)S(1)} %collective-permute-done.2.after.refs_11_), channel_id=1, source_target_pairs={{0,128},{128,256},{256,384},{384,0},{1,129},{129,257},{257,385},{3... | collective-permute-start | bytes 786440 | tf_op jit(solution)/shard_map/ppermute | solution.py:146
  71.1 1.9 %collective-permute-start.6 = (bf16[512,256]{1,0:T(8,128)(2,1)S(1)}, bf16[512,256]{1,0:T(8,128)(2,1)S(1)}, u32[]{:S(2)}, u32[]{:S(2)}) collective-permute-start(bf16[512,256]{1,0:T(8,128)(2,1)S(1)} %collective-permute-done.4.refs_8_), channel_id=1, source_target_pairs={{0,384},{128,0},{256,128},{384,256},{1,385},{129,1},{257,129},{385... | collective-permute-start | bytes 786440 | tf_op jit(solution)/shard_map/ppermute | solution.py:146
  73.2 1.0 copy-done.1
  74.2 3.9 %shard_map.94 = (bf16[8,512,512]{2,1,0:T(8,128)(2,1)S(1)}, bf16[2,256,256]{2,1,0:T(8,128)(2,1)S(1)}, f32[2,256,256]{2,1,0:T(8,128)S(1)}) custom-call(bf16[8,512,512]{2,1,0:T(8,128)(2,1)} %all-gather.4.cloned.1.call-done.h_hbm, bf16[2,256,256]{2,1,0:T(8,128)(2,1)S(1)} %bitcast.10, bf16[512,256]{1,0:T(8,128)(2,1)S(1)} %collective-permute-done.2.after.refs_11_), custom_call_target="tpu_custom_call" | custom-call | flops 1073741824 | bytes 8388608 | tf_op jit(solution)/shard_map/pallas_call | solution.py:179
  78.1 1.5 collective-permute-done.6.refs_10_
  79.6 2.8 %shard_map.95 = (bf16[512,256]{1,0:T(8,128)(2,1)S(1)}, f32[8,128]{1,0:T(8,128)S(1)}) custom-call(bf16[8,512,512]{2,1,0:T(8,128)(2,1)S(1)} %get-tuple-element.14.refs_0_, bf16[2,256,256]{2,1,0:T(8,128)(2,1)S(1)} %get-tuple-element.15.refs_1_, f32[2,256,256]{2,1,0:T(8,128)S(1)} %get-tuple-element.16.refs_2_, f32[2,256]{1,0:T(2,128)S(1)} %fusion.7.refs_3_, ...), custom_call_target="tpu_custom_call" | custom-call | flops 1073741824 | bytes 6291456 | tf_op jit(solution)/shard_map/pallas_call | solution.py:194
  82.5 7.9 %all_to_all.15 = f32[8,1,128]{2,1,0:T(1,128)S(1)} all-to-all(f32[8,1,128]{2,1,0:T(1,128)S(1)} %bitcast.13), channel_id=1, replica_groups=mesh['x'=4,'zg'=8,'zp'=2,'y'=4,'core'=2] {'y','core'}, dimensions={0} | all-to-all | bytes 8192 | tf_op jit(solution)/shard_map/all_to_all | solution.py:210
  90.4 1.1 shard_map.96
  91.5 6.9 %all-to-all-start.1 = ((bf16[4,528,256]{2,1,0:T(8,128)(2,1)}), bf16[4,528,256]{2,1,0:T(8,128)(2,1)S(1)}, u32[]{:S(2)}, u32[]{:S(2)}) async-start(bf16[4,528,256]{2,1,0:T(8,128)(2,1)} %shard_map.96), calls=%async_computation.1 | async-start | bytes 2162688 | tf_op jit(solution)/shard_map/all_to_all | solution.py:218
  98.4 4.9 %all-gather.6.cloned.1.call-done = bf16[4096,512]{1,0:T(8,128)(2,1)} async-done(((bf16[512,512]{1,0:T(8,128)(2,1)}), bf16[4096,512]{1,0:T(8,128)(2,1)}) %all-gather.6.cloned.1.call-update) | async-done | bytes 4194320 | tf_op jit(solution)/shard_map/all_gather | solution.py:170
  103.4 9.2 %all-to-all-done.1.g_ref = bf16[4,528,256]{2,1,0:T(8,128)(2,1)S(1)} async-done(((bf16[4,528,256]{2,1,0:T(8,128)(2,1)}), bf16[4,528,256]{2,1,0:T(8,128)(2,1)S(1)}, u32[]{:S(2)}, u32[]{:S(2)}) %all-to-all-start.1) | async-done | bytes 1081376 | tf_op jit(solution)/shard_map/all_to_all | solution.py:218
  112.5 4.1 %shard_map.97 = (f32[8,64,256]{2,1,0:T(8,128)S(1)}, f32[8,64,256]{2,1,0:T(8,128)S(1)}) custom-call(bf16[8,512,512]{2,1,0:T(8,128)(2,1)} %bitcast.14, bf16[4,528,256]{2,1,0:T(8,128)(2,1)S(1)} %all-to-all-done.1.g_ref), custom_call_target="tpu_custom_call" | custom-call | flops 1073741824 | bytes 6291456 | tf_op jit(solution)/shard_map/pallas_call | solution.py:220
  116.8 2.7 %collective-permute-start.8 = (f16[8,64,256]{2,1,0:T(8,128)(2,1)S(1)}, f16[8,64,256]{2,1,0:T(8,128)(2,1)S(1)}, u32[]{:S(2)}, u32[]{:S(2)}) collective-permute-start(f16[8,64,256]{2,1,0:T(8,128)(2,1)S(1)} %multiply_convert_fusion.1), channel_id=1, source_target_pairs={{0,8},{8,0},{1,9},{9,1},{2,10},{10,2},{3,11},{11,3},{4,12},{12,4},... | collective-permute-start | bytes 786440 | tf_op jit(solution)/shard_map/ppermute | solution.py:238
  119.5 6.2 %collective-permute-done.8 = f16[8,64,256]{2,1,0:T(8,128)(2,1)S(1)} collective-permute-done((f16[8,64,256]{2,1,0:T(8,128)(2,1)S(1)}, f16[8,64,256]{2,1,0:T(8,128)(2,1)S(1)}, u32[]{:S(2)}, u32[]{:S(2)}) %collective-permute-start.8) | collective-permute-done | bytes 262176 | tf_op jit(solution)/shard_map/ppermute | solution.py:238
  125.7 0.9 multiply_convert_fusion
  126.6 7.2 %all-to-all-start.2 = ((f16[8,64,256]{2,1,0:T(8,128)(2,1)}), f16[8,64,256]{2,1,0:T(8,128)(2,1)S(1)}, u32[]{:S(2)}, u32[]{:S(2)}) async-start(f16[8,64,256]{2,1,0:T(8,128)(2,1)} %multiply_convert_fusion), calls=%async_computation.2 | async-start | bytes 524288 | tf_op jit(solution)/shard_map/all_to_all | solution.py:240
  134.4 18.9 %all-to-all-done.2 = f16[8,64,256]{2,1,0:T(8,128)(2,1)S(1)} async-done(((f16[8,64,256]{2,1,0:T(8,128)(2,1)}), f16[8,64,256]{2,1,0:T(8,128)(2,1)S(1)}, u32[]{:S(2)}, u32[]{:S(2)}) %all-to-all-start.2) | async-done | bytes 262176 | tf_op jit(solution)/shard_map/all_to_all | solution.py:240
  (33 shorter events, 4.8 us)
Async XLA Ops:
  7.2 65.9 %copy-start = (bf16[1024,256]{1,0:T(8,128)(2,1)S(1)}, bf16[1024,256]{1,0:T(8,128)(2,1)}, u32[]{:S(2)}) copy-start(bf16[1024,256]{1,0:T(8,128)(2,1)} %param.11) | copy-start | bytes 1572868
  7.2 72.5 %copy-start.2 = (f32[2,4]{1,0:T(2,128)S(1)}, f32[2,4]{1,0:T(2,128)}, u32[]{:S(2)}) copy-start(f32[2,4]{1,0:T(2,128)} %refs_4_.1) | copy-start | bytes 100
  7.2 66.0 %all-gather.4.cloned.1.call-start = ((), (), s32[]{:S(2)}) async-start(), calls=%async_computation.3 | async-start | bytes 4718592 | tf_op jit(solution)/shard_map/all_gather | solution.py:161
  7.9 95.5 %all-gather.6.cloned.1.call-start = ((), (), s32[]{:S(2)}) async-start(), calls=%async_computation.4 | async-start | bytes 4718592 | tf_op jit(solution)/shard_map/all_gather | solution.py:170
  8.0 7.3 %collective-permute-start.1 = (bf16[64,256]{1,0:T(8,128)(2,1)}, bf16[64,256]{1,0:T(8,128)(2,1)S(1)}, u32[]{:S(2)}, u32[]{:S(2)}) collective-permute-start(bf16[64,256]{1,0:T(8,128)(2,1)} %param.12), channel_id=1, source_target_pairs={{0,8},{8,0},{1,9},{9,1},{2,10},{10,2},{3,11},{11,3},{4,12},{12,4},... | collective-permute-start | bytes 98312 | tf_op jit(solution)/shard_map/ppermute | solution.py:165
  11.8 40.8 %collective-permute-start = (bf16[512,512]{1,0:T(8,128)(2,1)}, bf16[512,512]{1,0:T(8,128)(2,1)S(1)}, u32[]{:S(2)}, u32[]{:S(2)}) collective-permute-start(bf16[512,512]{1,0:T(8,128)(2,1)} %bitcast.16), channel_id=1, source_target_pairs={{0,0},{2,128},{4,256},{6,384},{128,2},{130,130},{132,258},{134,386... | collective-permute-start | bytes 1572872 | tf_op jit(solution)/shard_map/ppermute | solution.py:163
  52.6 0.9 copy-start.3
  53.5 13.7 %collective-permute-start.2 = (bf16[512,256]{1,0:T(8,128)(2,1)S(1)}, bf16[512,256]{1,0:T(8,128)(2,1)S(1)}, u32[]{:S(2)}, u32[]{:S(2)}) collective-permute-start(bf16[512,256]{1,0:T(8,128)(2,1)S(1)} %get-tuple-element.22.refs_5_), channel_id=1, source_target_pairs={{0,128},{128,256},{256,384},{384,0},{1,129},{129,257},{257,385},{3... | collective-permute-start | bytes 786440 | tf_op jit(solution)/shard_map/ppermute | solution.py:144
  58.6 12.5 %collective-permute-start.4 = (bf16[512,256]{1,0:T(8,128)(2,1)S(1)}, bf16[512,256]{1,0:T(8,128)(2,1)S(1)}, u32[]{:S(2)}, u32[]{:S(2)}) collective-permute-start(bf16[512,256]{1,0:T(8,128)(2,1)S(1)} %get-tuple-element.21.refs_6_), channel_id=1, source_target_pairs={{0,384},{128,0},{256,128},{384,256},{1,385},{129,1},{257,129},{385... | collective-permute-start | bytes 786440 | tf_op jit(solution)/shard_map/ppermute | solution.py:144
  61.3 16.8 %collective-permute-start.3 = (bf16[512,256]{1,0:T(8,128)(2,1)S(1)}, bf16[512,256]{1,0:T(8,128)(2,1)S(1)}, u32[]{:S(2)}, u32[]{:S(2)}) collective-permute-start(bf16[512,256]{1,0:T(8,128)(2,1)S(1)} %get-tuple-element.22.refs_5_), channel_id=1, source_target_pairs={{0,384},{128,0},{256,128},{384,256},{1,385},{129,1},{257,129},{385... | collective-permute-start | bytes 786440 | tf_op jit(solution)/shard_map/ppermute | solution.py:145
  64.9 13.2 %collective-permute-start.7 = (bf16[512,256]{1,0:T(8,128)(2,1)S(1)}, bf16[512,256]{1,0:T(8,128)(2,1)S(1)}, u32[]{:S(2)}, u32[]{:S(2)}) collective-permute-start(bf16[512,256]{1,0:T(8,128)(2,1)S(1)} %get-tuple-element.21.refs_6_), channel_id=1, source_target_pairs={{0,128},{128,256},{256,384},{384,0},{1,129},{129,257},{257,385},{3... | collective-permute-start | bytes 786440 | tf_op jit(solution)/shard_map/ppermute | solution.py:145
  67.2 11.0 %collective-permute-start.5 = (bf16[512,256]{1,0:T(8,128)(2,1)S(1)}, bf16[512,256]{1,0:T(8,128)(2,1)S(1)}, u32[]{:S(2)}, u32[]{:S(2)}) collective-permute-start(bf16[512,256]{1,0:T(8,128)(2,1)S(1)} %collective-permute-done.2.after.refs_11_), channel_id=1, source_target_pairs={{0,128},{128,256},{256,384},{384,0},{1,129},{129,257},{257,385},{3... | collective-permute-start | bytes 786440 | tf_op jit(solution)/shard_map/ppermute | solution.py:146
  71.1 8.5 %collective-permute-start.6 = (bf16[512,256]{1,0:T(8,128)(2,1)S(1)}, bf16[512,256]{1,0:T(8,128)(2,1)S(1)}, u32[]{:S(2)}, u32[]{:S(2)}) collective-permute-start(bf16[512,256]{1,0:T(8,128)(2,1)S(1)} %collective-permute-done.4.refs_8_), channel_id=1, source_target_pairs={{0,384},{128,0},{256,128},{384,256},{1,385},{129,1},{257,129},{385... | collective-permute-start | bytes 786440 | tf_op jit(solution)/shard_map/ppermute | solution.py:146
  73.2 1.0 copy-start.1
  91.5 21.1 %all-to-all-start.1 = ((bf16[4,528,256]{2,1,0:T(8,128)(2,1)}), bf16[4,528,256]{2,1,0:T(8,128)(2,1)S(1)}, u32[]{:S(2)}, u32[]{:S(2)}) async-start(bf16[4,528,256]{2,1,0:T(8,128)(2,1)} %shard_map.96), calls=%async_computation.1 | async-start | bytes 2162688 | tf_op jit(solution)/shard_map/all_to_all | solution.py:218
  98.4 55.0 %copy-start.5 = (f32[64,256]{1,0:T(8,128)S(1)}, f32[64,256]{1,0:T(8,128)}, u32[]{:S(2)}) copy-start(f32[64,256]{1,0:T(8,128)} %param.13) | copy-start | bytes 196612
  116.8 8.9 %collective-permute-start.8 = (f16[8,64,256]{2,1,0:T(8,128)(2,1)S(1)}, f16[8,64,256]{2,1,0:T(8,128)(2,1)S(1)}, u32[]{:S(2)}, u32[]{:S(2)}) collective-permute-start(f16[8,64,256]{2,1,0:T(8,128)(2,1)S(1)} %multiply_convert_fusion.1), channel_id=1, source_target_pairs={{0,8},{8,0},{1,9},{9,1},{2,10},{10,2},{3,11},{11,3},{4,12},{12,4},... | collective-permute-start | bytes 786440 | tf_op jit(solution)/shard_map/ppermute | solution.py:238
  126.6 26.7 %all-to-all-start.2 = ((f16[8,64,256]{2,1,0:T(8,128)(2,1)}), f16[8,64,256]{2,1,0:T(8,128)(2,1)S(1)}, u32[]{:S(2)}, u32[]{:S(2)}) async-start(f16[8,64,256]{2,1,0:T(8,128)(2,1)} %multiply_convert_fusion), calls=%async_computation.2 | async-start | bytes 524288 | tf_op jit(solution)/shard_map/all_to_all | solution.py:240
  153.4 0.7 copy-start.4
Sparse Core Ops, SparseCore 0:
  10.2 47.6 all-gather.3
  60.0 43.3 all-gather.5

commit v10 on v8

--- a/solution.py
+++ b/solution.py
@@ -37,14 +37,13 @@
     return copies
 
 
-def gram_kernel(h_hbm, n_hbm, after, h_ref, n_ref, gram_ref, h_sems, n_sems):
+def gram_kernel(h_hbm, after, h_ref, gram_ref, h_sems):
     recs, rows, _ = gram_ref.shape
     blocks = h_ref.shape[0]
     nx = blocks // 2
     here = lax.axis_index("x")
     order = [lax.rem(here + k // 2, nx) * 2 + k % 2 for k in range(blocks)]
     h_copies = fetch(h_hbm, h_ref, h_sems, order)
-    n_copies = fetch(n_hbm, n_ref, n_sems)
     for r in range(recs):
         total = None
         for k in range(blocks):
@@ -54,24 +53,30 @@
             q = dot(h, h, 1, 1)
             total = q if total is None else total + q
         gram_ref[r] = total
-    for copy in n_copies:
-        copy.wait()
 
 
 def grad_kernel(*refs):
-    h_ref, n_ref, gram_ref, b_ref, t_ref = refs[:5]
-    w_refs, (g_ref, sq_ref) = refs[5:-2], refs[-2:]
+    h_ref, n_ref, gram_ref, cond_ref, emb_ref, t_ref = refs[:6]
+    w_refs, (g_ref, sq_ref) = refs[6:-2], refs[-2:]
     recs, rows, _ = gram_ref.shape
     events = rows // t_ref.shape[1]
     lane = lax.broadcasted_iota(jnp.int32, sq_ref.shape, 1)
     out = jnp.zeros(sq_ref.shape, F32)
+    shape = (8, emb_ref.shape[0])
+    ids = lax.broadcasted_iota(jnp.int32, shape, 1)
+    owner = lax.broadcasted_iota(jnp.int32, shape, 0)
+    counts = jnp.zeros(shape, F32)
+    for r in range(recs):
+        for k in range(cond_ref.shape[1]):
+            counts += jnp.where((owner == r) & (ids == cond_ref[r, k]), 1.0, 0.0)
+    bias = dot(counts.astype(BF16), emb_ref[...], 1, 0)
     for r in range(recs):
         at = slice(r * rows, (r + 1) * rows)
         pred = None
         for k, w_ref in enumerate(w_refs):
             p = dot(h_ref[k, at, :], w_ref[...], 1, 0)
             pred = p if pred is None else pred + p
-        diff = pred + b_ref[r : r + 1, :] - n_ref[r].astype(F32)
+        diff = pred + bias[r : r + 1, :] - n_ref[r].astype(F32)
         parts = []
         for a in range(t_ref.shape[1]):
             wgt = 1.0 / (t_ref[r : r + 1, a : a + 1] + 0.25)
@@ -167,30 +172,25 @@
     mine = lax.all_gather(swapped, tensor, axis=0, tiled=False)
     w_blocks = ring_gather(wz)
 
-    vocab_ids = lax.broadcasted_iota(jnp.int32, (1, 1, emb.shape[0]), 2)
-    counts = jnp.sum((cond[:, :, None] == vocab_ids).astype(F32), axis=1).astype(BF16)
-    bias = jnp.dot(counts, emb, preferred_element_type=F32)
-
     vmem = pl.BlockSpec(memory_space=pltpu.VMEM)
     hbm = pl.BlockSpec(memory_space=pltpu.HBM)
-    h, n, gram = pl.pallas_call(
+    h, gram = pl.pallas_call(
         gram_kernel,
-        in_specs=[hbm, hbm, pl.BlockSpec(memory_space=pl.ANY)],
-        out_specs=[vmem, vmem, vmem],
+        in_specs=[hbm, pl.BlockSpec(memory_space=pl.ANY)],
+        out_specs=[vmem, vmem],
         out_shape=[
             jax.ShapeDtypeStruct((nt, recs * rows, feats), BF16),
-            jax.ShapeDtypeStruct((recs, rows, local_out), BF16),
             jax.ShapeDtypeStruct((recs, rows, rows), F32),
         ],
-        scratch_shapes=[pltpu.SemaphoreType.DMA((nt,)), pltpu.SemaphoreType.DMA((recs,))],
+        scratch_shapes=[pltpu.SemaphoreType.DMA((nt,))],
         compiler_params=params(48),
         cost_estimate=pl.CostEstimate(
             flops=2 * recs * rows * rows * D, bytes_accessed=4 * recs * rows * D, transcendentals=0
         ),
-    )(full, noise_draws.reshape(recs, rows, local_out), w_blocks[AFTER])
+    )(full, w_blocks[AFTER])
     grads, sq = pl.pallas_call(
         grad_kernel,
-        in_specs=[vmem] * 13,
+        in_specs=[vmem] * 3 + [pl.BlockSpec(memory_space=pltpu.SMEM)] + [vmem] * 10,
         out_specs=[vmem, vmem],
         out_shape=[
             jax.ShapeDtypeStruct((recs * rows, local_out), BF16),
@@ -202,7 +202,7 @@
             bytes_accessed=2 * recs * rows * D + 2 * D * local_out,
             transcendentals=0,
         ),
-    )(h, n, gram, bias, times, *w_blocks)
+    )(h, noise_draws.reshape(recs, rows, local_out), gram, cond, emb, times, *w_blocks)
 
     sq_all = lax.all_to_all(sq.reshape(nt, 1, 128), tensor, 0, 0).reshape(nt, 128)
     norms = jnp.sqrt(jnp.sum(sq_all[:, :recs], axis=0))

time: 158 us -> 157 us (level)
  transfers between devices with their start and end apart: 12 -> 12, of which waited for: 5 -> 5; matrix products, arithmetic and copies ran while one was open for 1% -> 0% of each run, Pallas kernels for 5% -> 5%
where the time goes in v10:
time: 157 us; the launch traced here: 156 us
  blocking collectives  47.2 us (30%)
  waiting for transfers between devices  42.9 us (27%)
  starting transfers between devices  37.2 us (24%)
  between operations  14.3 us (9%)
  Pallas kernels  11.6 us (7%)
  other arithmetic  1.78 us (1%)
    all_gather x1, blocking collectives, on_device(): wz = lax.all_gather(weight, ('zg', 'zp'), axis=0, tiled=True)  38.8 us
    all_to_all x1, waiting for transfers between devices, on_device(): clipped_sum = jnp.sum(unroot(lax.all_to_all(sent, 'zg', 0, 0)), axis=0)  18.6 us
    all_to_all x1, blocking collectives, on_device(): lax.all_to_all(sq.reshape(nt, 1, 128), tensor, 0, 0).reshape(nt, 128)  8.38 us
    all_to_all x1, waiting for transfers between devices, on_device(): packed = lax.all_to_all(packed, 'x', 0, 0)  8.07 us
    ppermute x1, waiting for transfers between devices, on_device(): got = lax.ppermute(root(send).astype(F16), 'zp', [(0, 1), (1, 0)])  6.88 us
    all_to_all x1, starting transfers between devices, on_device(): clipped_sum = jnp.sum(unroot(lax.all_to_all(sent, 'zg', 0, 0)), axis=0)  6.79 us
    ppermute x2, starting transfers between devices, ring_gather(): a3, b1 = (lax.ppermute(a, 'x', up), lax.ppermute(b, 'x', down))  6.7 us
    all_to_all x1, starting transfers between devices, on_device(): packed = lax.all_to_all(packed, 'x', 0, 0)  6.58 us
  transfers between devices with their start and end apart: 12, of which 5 were waited for; matrix products, arithmetic and copies ran while one was open for 0% of the time, Pallas kernels for 5%

profile of v10, /device:TPU:2, one launch (start us, length us, event | category | flops | bytes accessed | tf_op | source)
XLA Modules:
  0.0 156.3 jit_solution(3044467271354913637)
XLA Ops:
  7.3 0.7 all-gather.4.cloned.1.call-update
  8.0 3.5 %collective-permute-start = (bf16[512,512]{1,0:T(8,128)(2,1)}, bf16[512,512]{1,0:T(8,128)(2,1)S(1)}, u32[]{:S(2)}, u32[]{:S(2)}) collective-permute-start(bf16[512,512]{1,0:T(8,128)(2,1)} %bitcast.14), channel_id=1, source_target_pairs={{0,0},{2,128},{4,256},{6,384},{128,2},{130,130},{132,258},{134,386... | collective-permute-start | bytes 1572872 | tf_op jit(solution)/shard_map/ppermute | solution.py:168
  11.5 38.8 %all_gather.12 = bf16[1024,256]{1,0:T(8,128)(2,1)S(1)} all-gather(bf16[64,256]{1,0:T(8,128)(2,1)} %param.12), channel_id=1, replica_groups=mesh['x'=4,'zg'=8,'zp'=2,'y'=4,'core'=2] {'zg','zp'}, dimensions={0}, use_global_device_ids=true | all-gather | bytes 557056 | tf_op jit(solution)/shard_map/all_gather | solution.py:170
  50.2 0.9 copy-done.4
  51.2 4.8 %collective-permute-start.1 = (bf16[512,256]{1,0:T(8,128)(2,1)S(1)}, bf16[512,256]{1,0:T(8,128)(2,1)S(1)}, u32[]{:S(2)}, u32[]{:S(2)}) collective-permute-start(bf16[512,256]{1,0:T(8,128)(2,1)S(1)} %get-tuple-element.20.refs_6_), channel_id=1, source_target_pairs={{0,128},{128,256},{256,384},{384,0},{1,129},{129,257},{257,385},{3... | collective-permute-start | bytes 786440 | tf_op jit(solution)/shard_map/ppermute | solution.py:149
  55.9 1.9 %collective-permute-start.3 = (bf16[512,256]{1,0:T(8,128)(2,1)S(1)}, bf16[512,256]{1,0:T(8,128)(2,1)S(1)}, u32[]{:S(2)}, u32[]{:S(2)}) collective-permute-start(bf16[512,256]{1,0:T(8,128)(2,1)S(1)} %get-tuple-element.19.refs_7_), channel_id=1, source_target_pairs={{0,384},{128,0},{256,128},{384,256},{1,385},{129,1},{257,129},{385... | collective-permute-start | bytes 786440 | tf_op jit(solution)/shard_map/ppermute | solution.py:149
  57.9 3.5 %collective-permute-start.2 = (bf16[512,256]{1,0:T(8,128)(2,1)S(1)}, bf16[512,256]{1,0:T(8,128)(2,1)S(1)}, u32[]{:S(2)}, u32[]{:S(2)}) collective-permute-start(bf16[512,256]{1,0:T(8,128)(2,1)S(1)} %get-tuple-element.20.refs_6_), channel_id=1, source_target_pairs={{0,384},{128,0},{256,128},{384,256},{1,385},{129,1},{257,129},{385... | collective-permute-start | bytes 786440 | tf_op jit(solution)/shard_map/ppermute | solution.py:150
  61.4 2.3 %collective-permute-start.6 = (bf16[512,256]{1,0:T(8,128)(2,1)S(1)}, bf16[512,256]{1,0:T(8,128)(2,1)S(1)}, u32[]{:S(2)}, u32[]{:S(2)}) collective-permute-start(bf16[512,256]{1,0:T(8,128)(2,1)S(1)} %get-tuple-element.19.refs_7_), channel_id=1, source_target_pairs={{0,128},{128,256},{256,384},{384,0},{1,129},{129,257},{257,385},{3... | collective-permute-start | bytes 786440 | tf_op jit(solution)/shard_map/ppermute | solution.py:150
  63.7 3.9 %collective-permute-start.4 = (bf16[512,256]{1,0:T(8,128)(2,1)S(1)}, bf16[512,256]{1,0:T(8,128)(2,1)S(1)}, u32[]{:S(2)}, u32[]{:S(2)}) collective-permute-start(bf16[512,256]{1,0:T(8,128)(2,1)S(1)} %collective-permute-done.1.after.refs_12_), channel_id=1, source_target_pairs={{0,128},{128,256},{256,384},{384,0},{1,129},{129,257},{257,385},{3... | collective-permute-start | bytes 786440 | tf_op jit(solution)/shard_map/ppermute | solution.py:151
  67.7 1.9 %collective-permute-start.5 = (bf16[512,256]{1,0:T(8,128)(2,1)S(1)}, bf16[512,256]{1,0:T(8,128)(2,1)S(1)}, u32[]{:S(2)}, u32[]{:S(2)}) collective-permute-start(bf16[512,256]{1,0:T(8,128)(2,1)S(1)} %collective-permute-done.3.refs_9_), channel_id=1, source_target_pairs={{0,384},{128,0},{256,128},{384,256},{1,385},{129,1},{257,129},{385... | collective-permute-start | bytes 786440 | tf_op jit(solution)/shard_map/ppermute | solution.py:151
  69.6 3.9 %shard_map.94 = (bf16[8,512,512]{2,1,0:T(8,128)(2,1)S(1)}, f32[2,256,256]{2,1,0:T(8,128)S(1)}) custom-call(bf16[8,512,512]{2,1,0:T(8,128)(2,1)} %all-gather.4.cloned.1.call-done.h_hbm, bf16[512,256]{1,0:T(8,128)(2,1)S(1)} %collective-permute-done.1.after.refs_12_), custom_call_target="tpu_custom_call" | custom-call | flops 1073741824 | bytes 8388608 | tf_op jit(solution)/shard_map/pallas_call | solution.py:177
  73.6 2.6 %collective-permute-done.5.refs_11_ = bf16[512,256]{1,0:T(8,128)(2,1)S(1)} collective-permute-done((bf16[512,256]{1,0:T(8,128)(2,1)S(1)}, bf16[512,256]{1,0:T(8,128)(2,1)S(1)}, u32[]{:S(2)}, u32[]{:S(2)}) %collective-permute-start.5) | collective-permute-done | bytes 262176 | tf_op jit(solution)/shard_map/ppermute | solution.py:151
  76.2 2.5 %shard_map.95 = (bf16[512,256]{1,0:T(8,128)(2,1)S(1)}, f32[8,128]{1,0:T(8,128)S(1)}) custom-call(bf16[8,512,512]{2,1,0:T(8,128)(2,1)S(1)} %get-tuple-element.13.refs_0_, bf16[2,256,256]{2,1,0:T(8,128)(2,1)S(1)} %bitcast.8, f32[2,256,256]{2,1,0:T(8,128)S(1)} %get-tuple-element.14.refs_2_, s32[2,16]{1,0:T(2,128)S(1)} %copy-done.2, ...), custom_call_target="tpu_custom_call" | custom-call | flops 1073741824 | bytes 6291456 | tf_op jit(solution)/shard_map/pallas_call | solution.py:191
  78.7 8.4 %all_to_all.15 = f32[8,1,128]{2,1,0:T(1,128)S(1)} all-to-all(f32[8,1,128]{2,1,0:T(1,128)S(1)} %bitcast.11), channel_id=1, replica_groups=mesh['x'=4,'zg'=8,'zp'=2,'y'=4,'core'=2] {'y','core'}, dimensions={0} | all-to-all | bytes 8192 | tf_op jit(solution)/shard_map/all_to_all | solution.py:207
  87.0 1.1 shard_map.96
  88.2 6.6 %all-to-all-start.1 = ((bf16[4,528,256]{2,1,0:T(8,128)(2,1)}), bf16[4,528,256]{2,1,0:T(8,128)(2,1)S(1)}, u32[]{:S(2)}, u32[]{:S(2)}) async-start(bf16[4,528,256]{2,1,0:T(8,128)(2,1)} %shard_map.96), calls=%async_computation.1 | async-start | bytes 2162688 | tf_op jit(solution)/shard_map/all_to_all | solution.py:215
  94.7 6.0 %all-gather.6.cloned.1.call-done = bf16[4096,512]{1,0:T(8,128)(2,1)} async-done(((bf16[512,512]{1,0:T(8,128)(2,1)}), bf16[4096,512]{1,0:T(8,128)(2,1)}) %all-gather.6.cloned.1.call-update) | async-done | bytes 4194320 | tf_op jit(solution)/shard_map/all_gather | solution.py:172
  100.7 8.1 %all-to-all-done.1.g_ref = bf16[4,528,256]{2,1,0:T(8,128)(2,1)S(1)} async-done(((bf16[4,528,256]{2,1,0:T(8,128)(2,1)}), bf16[4,528,256]{2,1,0:T(8,128)(2,1)S(1)}, u32[]{:S(2)}, u32[]{:S(2)}) %all-to-all-start.1) | async-done | bytes 1081376 | tf_op jit(solution)/shard_map/all_to_all | solution.py:215
  108.8 4.1 %shard_map.97 = (f32[8,64,256]{2,1,0:T(8,128)S(1)}, f32[8,64,256]{2,1,0:T(8,128)S(1)}) custom-call(bf16[8,512,512]{2,1,0:T(8,128)(2,1)} %bitcast.12, bf16[4,528,256]{2,1,0:T(8,128)(2,1)S(1)} %all-to-all-done.1.g_ref), custom_call_target="tpu_custom_call" | custom-call | flops 1073741824 | bytes 6291456 | tf_op jit(solution)/shard_map/pallas_call | solution.py:217
  113.1 1.9 %collective-permute-start.7 = (f16[8,64,256]{2,1,0:T(8,128)(2,1)S(1)}, f16[8,64,256]{2,1,0:T(8,128)(2,1)S(1)}, u32[]{:S(2)}, u32[]{:S(2)}) collective-permute-start(f16[8,64,256]{2,1,0:T(8,128)(2,1)S(1)} %multiply_convert_fusion.1), channel_id=1, source_target_pairs={{0,8},{8,0},{1,9},{9,1},{2,10},{10,2},{3,11},{11,3},{4,12},{12,4},... | collective-permute-start | bytes 786440 | tf_op jit(solution)/shard_map/ppermute | solution.py:235
  115.0 6.9 %collective-permute-done.7 = f16[8,64,256]{2,1,0:T(8,128)(2,1)S(1)} collective-permute-done((f16[8,64,256]{2,1,0:T(8,128)(2,1)S(1)}, f16[8,64,256]{2,1,0:T(8,128)(2,1)S(1)}, u32[]{:S(2)}, u32[]{:S(2)}) %collective-permute-start.7) | collective-permute-done | bytes 262176 | tf_op jit(solution)/shard_map/ppermute | solution.py:235
  121.9 0.9 multiply_convert_fusion
  122.8 6.8 %all-to-all-start.2 = ((f16[8,64,256]{2,1,0:T(8,128)(2,1)}), f16[8,64,256]{2,1,0:T(8,128)(2,1)S(1)}, u32[]{:S(2)}, u32[]{:S(2)}) async-start(f16[8,64,256]{2,1,0:T(8,128)(2,1)} %multiply_convert_fusion), calls=%async_computation.2 | async-start | bytes 524288 | tf_op jit(solution)/shard_map/all_to_all | solution.py:237
  130.1 18.6 %all-to-all-done.2 = f16[8,64,256]{2,1,0:T(8,128)(2,1)S(1)} async-done(((f16[8,64,256]{2,1,0:T(8,128)(2,1)}), f16[8,64,256]{2,1,0:T(8,128)(2,1)S(1)}, u32[]{:S(2)}, u32[]{:S(2)}) %all-to-all-start.2) | async-done | bytes 262176 | tf_op jit(solution)/shard_map/all_to_all | solution.py:237
  (29 shorter events, 1.6 us)
Async XLA Ops:
  7.2 69.0 %copy-start.1 = (bf16[2,4,64,256]{3,2,1,0:T(8,128)(2,1)S(1)}, bf16[2,4,64,256]{3,2,1,0:T(8,128)(2,1)}, u32[]{:S(2)}) copy-start(bf16[2,4,64,256]{3,2,1,0:T(8,128)(2,1)} %param.8) | copy-start | bytes 786436
  7.2 69.0 %copy-start.2 = (s32[2,16]{1,0:T(2,128)S(1)}, s32[2,16]{1,0:T(2,128)}, u32[]{:S(2)}) copy-start(s32[2,16]{1,0:T(2,128)} %refs_3_.1) | copy-start | bytes 388
  7.2 69.0 %copy-start = (bf16[1024,256]{1,0:T(8,128)(2,1)S(1)}, bf16[1024,256]{1,0:T(8,128)(2,1)}, u32[]{:S(2)}) copy-start(bf16[1024,256]{1,0:T(8,128)(2,1)} %refs_4_.1) | copy-start | bytes 1572868
  7.2 69.0 %copy-start.3 = (f32[2,4]{1,0:T(2,128)S(1)}, f32[2,4]{1,0:T(2,128)}, u32[]{:S(2)}) copy-start(f32[2,4]{1,0:T(2,128)} %refs_5_.1) | copy-start | bytes 100
  7.2 62.4 %all-gather.4.cloned.1.call-start = ((), (), s32[]{:S(2)}) async-start(), calls=%async_computation.3 | async-start | bytes 4718592 | tf_op jit(solution)/shard_map/all_gather | solution.py:166
  7.9 92.8 %all-gather.6.cloned.1.call-start = ((), (), s32[]{:S(2)}) async-start(), calls=%async_computation.4 | async-start | bytes 4718592 | tf_op jit(solution)/shard_map/all_gather | solution.py:172
  8.0 42.2 %collective-permute-start = (bf16[512,512]{1,0:T(8,128)(2,1)}, bf16[512,512]{1,0:T(8,128)(2,1)S(1)}, u32[]{:S(2)}, u32[]{:S(2)}) collective-permute-start(bf16[512,512]{1,0:T(8,128)(2,1)} %bitcast.14), channel_id=1, source_target_pairs={{0,0},{2,128},{4,256},{6,384},{128,2},{130,130},{132,258},{134,386... | collective-permute-start | bytes 1572872 | tf_op jit(solution)/shard_map/ppermute | solution.py:168
  50.2 0.9 copy-start.4
  51.2 12.6 %collective-permute-start.1 = (bf16[512,256]{1,0:T(8,128)(2,1)S(1)}, bf16[512,256]{1,0:T(8,128)(2,1)S(1)}, u32[]{:S(2)}, u32[]{:S(2)}) collective-permute-start(bf16[512,256]{1,0:T(8,128)(2,1)S(1)} %get-tuple-element.20.refs_6_), channel_id=1, source_target_pairs={{0,128},{128,256},{256,384},{384,0},{1,129},{129,257},{257,385},{3... | collective-permute-start | bytes 786440 | tf_op jit(solution)/shard_map/ppermute | solution.py:149
  55.9 11.7 %collective-permute-start.3 = (bf16[512,256]{1,0:T(8,128)(2,1)S(1)}, bf16[512,256]{1,0:T(8,128)(2,1)S(1)}, u32[]{:S(2)}, u32[]{:S(2)}) collective-permute-start(bf16[512,256]{1,0:T(8,128)(2,1)S(1)} %get-tuple-element.19.refs_7_), channel_id=1, source_target_pairs={{0,384},{128,0},{256,128},{384,256},{1,385},{129,1},{257,129},{385... | collective-permute-start | bytes 786440 | tf_op jit(solution)/shard_map/ppermute | solution.py:149
  57.9 15.7 %collective-permute-start.2 = (bf16[512,256]{1,0:T(8,128)(2,1)S(1)}, bf16[512,256]{1,0:T(8,128)(2,1)S(1)}, u32[]{:S(2)}, u32[]{:S(2)}) collective-permute-start(bf16[512,256]{1,0:T(8,128)(2,1)S(1)} %get-tuple-element.20.refs_6_), channel_id=1, source_target_pairs={{0,384},{128,0},{256,128},{384,256},{1,385},{129,1},{257,129},{385... | collective-permute-start | bytes 786440 | tf_op jit(solution)/shard_map/ppermute | solution.py:150
  61.4 12.2 %collective-permute-start.6 = (bf16[512,256]{1,0:T(8,128)(2,1)S(1)}, bf16[512,256]{1,0:T(8,128)(2,1)S(1)}, u32[]{:S(2)}, u32[]{:S(2)}) collective-permute-start(bf16[512,256]{1,0:T(8,128)(2,1)S(1)} %get-tuple-element.19.refs_7_), channel_id=1, source_target_pairs={{0,128},{128,256},{256,384},{384,0},{1,129},{129,257},{257,385},{3... | collective-permute-start | bytes 786440 | tf_op jit(solution)/shard_map/ppermute | solution.py:150
  63.7 9.8 %collective-permute-start.4 = (bf16[512,256]{1,0:T(8,128)(2,1)S(1)}, bf16[512,256]{1,0:T(8,128)(2,1)S(1)}, u32[]{:S(2)}, u32[]{:S(2)}) collective-permute-start(bf16[512,256]{1,0:T(8,128)(2,1)S(1)} %collective-permute-done.1.after.refs_12_), channel_id=1, source_target_pairs={{0,128},{128,256},{256,384},{384,0},{1,129},{129,257},{257,385},{3... | collective-permute-start | bytes 786440 | tf_op jit(solution)/shard_map/ppermute | solution.py:151
  67.7 8.5 %collective-permute-start.5 = (bf16[512,256]{1,0:T(8,128)(2,1)S(1)}, bf16[512,256]{1,0:T(8,128)(2,1)S(1)}, u32[]{:S(2)}, u32[]{:S(2)}) collective-permute-start(bf16[512,256]{1,0:T(8,128)(2,1)S(1)} %collective-permute-done.3.refs_9_), channel_id=1, source_target_pairs={{0,384},{128,0},{256,128},{384,256},{1,385},{129,1},{257,129},{385... | collective-permute-start | bytes 786440 | tf_op jit(solution)/shard_map/ppermute | solution.py:151
  88.2 20.6 %all-to-all-start.1 = ((bf16[4,528,256]{2,1,0:T(8,128)(2,1)}), bf16[4,528,256]{2,1,0:T(8,128)(2,1)S(1)}, u32[]{:S(2)}, u32[]{:S(2)}) async-start(bf16[4,528,256]{2,1,0:T(8,128)(2,1)} %shard_map.96), calls=%async_computation.1 | async-start | bytes 2162688 | tf_op jit(solution)/shard_map/all_to_all | solution.py:215
  94.7 54.1 %copy-start.6 = (f32[64,256]{1,0:T(8,128)S(1)}, f32[64,256]{1,0:T(8,128)}, u32[]{:S(2)}) copy-start(f32[64,256]{1,0:T(8,128)} %param.13) | copy-start | bytes 196612
  113.1 8.8 %collective-permute-start.7 = (f16[8,64,256]{2,1,0:T(8,128)(2,1)S(1)}, f16[8,64,256]{2,1,0:T(8,128)(2,1)S(1)}, u32[]{:S(2)}, u32[]{:S(2)}) collective-permute-start(f16[8,64,256]{2,1,0:T(8,128)(2,1)S(1)} %multiply_convert_fusion.1), channel_id=1, source_target_pairs={{0,8},{8,0},{1,9},{9,1},{2,10},{10,2},{3,11},{11,3},{4,12},{12,4},... | collective-permute-start | bytes 786440 | tf_op jit(solution)/shard_map/ppermute | solution.py:235
  122.8 25.9 %all-to-all-start.2 = ((f16[8,64,256]{2,1,0:T(8,128)(2,1)}), f16[8,64,256]{2,1,0:T(8,128)(2,1)S(1)}, u32[]{:S(2)}, u32[]{:S(2)}) async-start(f16[8,64,256]{2,1,0:T(8,128)(2,1)} %multiply_convert_fusion), calls=%async_computation.2 | async-start | bytes 524288 | tf_op jit(solution)/shard_map/all_to_all | solution.py:237
  148.8 0.7 copy-start.5
Sparse Core Ops, SparseCore 0:
  10.2 44.2 all-gather.3
  56.6 44.0 all-gather.5

commit v11 on v10

--- a/solution.py
+++ b/solution.py
@@ -13,7 +13,7 @@
 F32 = jnp.float32
 BF16 = jnp.bfloat16
 F16 = jnp.float16
-SCALE = 256.0
+SCALE = 128.0
 AFTER = 6
 TAIL = 16
 MIB = 1024 * 1024

time: 157 us -> 157 us (level)
  no operation moved by 1% of the time
where the time goes in v11:
time: 157 us; the launch traced here: 156 us
  blocking collectives  47.2 us (30%)
  waiting for transfers between devices  42.9 us (27%)
  starting transfers between devices  37.2 us (24%)
  between operations  14.3 us (9%)
  Pallas kernels  11.6 us (7%)
  other arithmetic  1.78 us (1%)
    all_gather x1, blocking collectives, on_device(): wz = lax.all_gather(weight, ('zg', 'zp'), axis=0, tiled=True)  38.8 us
    all_to_all x1, waiting for transfers between devices, on_device(): clipped_sum = jnp.sum(unroot(lax.all_to_all(sent, 'zg', 0, 0)), axis=0)  18.6 us
    all_to_all x1, blocking collectives, on_device(): lax.all_to_all(sq.reshape(nt, 1, 128), tensor, 0, 0).reshape(nt, 128)  8.38 us
    all_to_all x1, waiting for transfers between devices, on_device(): packed = lax.all_to_all(packed, 'x', 0, 0)  8.07 us
    ppermute x1, waiting for transfers between devices, on_device(): got = lax.ppermute(root(send).astype(F16), 'zp', [(0, 1), (1, 0)])  6.88 us
    all_to_all x1, starting transfers between devices, on_device(): clipped_sum = jnp.sum(unroot(lax.all_to_all(sent, 'zg', 0, 0)), axis=0)  6.79 us
    ppermute x2, starting transfers between devices, ring_gather(): a3, b1 = (lax.ppermute(a, 'x', up), lax.ppermute(b, 'x', down))  6.7 us
    all_to_all x1, starting transfers between devices, on_device(): packed = lax.all_to_all(packed, 'x', 0, 0)  6.58 us
  transfers between devices with their start and end apart: 12, of which 5 were waited for; matrix products, arithmetic and copies ran while one was open for 0% of the time, Pallas kernels for 5%

profile of v11, /device:TPU:2, one launch (start us, length us, event | category | flops | bytes accessed | tf_op | source)
XLA Modules:
  0.0 156.3 jit_solution(15584167564351810266)
XLA Ops:
  7.3 0.7 all-gather.4.cloned.1.call-update
  8.0 3.5 %collective-permute-start = (bf16[512,512]{1,0:T(8,128)(2,1)}, bf16[512,512]{1,0:T(8,128)(2,1)S(1)}, u32[]{:S(2)}, u32[]{:S(2)}) collective-permute-start(bf16[512,512]{1,0:T(8,128)(2,1)} %bitcast.14), channel_id=1, source_target_pairs={{0,0},{2,128},{4,256},{6,384},{128,2},{130,130},{132,258},{134,386... | collective-permute-start | bytes 1572872 | tf_op jit(solution)/shard_map/ppermute | solution.py:168
  11.5 38.8 %all_gather.12 = bf16[1024,256]{1,0:T(8,128)(2,1)S(1)} all-gather(bf16[64,256]{1,0:T(8,128)(2,1)} %param.12), channel_id=1, replica_groups=mesh['x'=4,'zg'=8,'zp'=2,'y'=4,'core'=2] {'zg','zp'}, dimensions={0}, use_global_device_ids=true | all-gather | bytes 557056 | tf_op jit(solution)/shard_map/all_gather | solution.py:170
  50.2 0.9 copy-done.4
  51.2 4.8 %collective-permute-start.1 = (bf16[512,256]{1,0:T(8,128)(2,1)S(1)}, bf16[512,256]{1,0:T(8,128)(2,1)S(1)}, u32[]{:S(2)}, u32[]{:S(2)}) collective-permute-start(bf16[512,256]{1,0:T(8,128)(2,1)S(1)} %get-tuple-element.20.refs_6_), channel_id=1, source_target_pairs={{0,128},{128,256},{256,384},{384,0},{1,129},{129,257},{257,385},{3... | collective-permute-start | bytes 786440 | tf_op jit(solution)/shard_map/ppermute | solution.py:149
  55.9 1.9 %collective-permute-start.3 = (bf16[512,256]{1,0:T(8,128)(2,1)S(1)}, bf16[512,256]{1,0:T(8,128)(2,1)S(1)}, u32[]{:S(2)}, u32[]{:S(2)}) collective-permute-start(bf16[512,256]{1,0:T(8,128)(2,1)S(1)} %get-tuple-element.19.refs_7_), channel_id=1, source_target_pairs={{0,384},{128,0},{256,128},{384,256},{1,385},{129,1},{257,129},{385... | collective-permute-start | bytes 786440 | tf_op jit(solution)/shard_map/ppermute | solution.py:149
  57.9 3.5 %collective-permute-start.2 = (bf16[512,256]{1,0:T(8,128)(2,1)S(1)}, bf16[512,256]{1,0:T(8,128)(2,1)S(1)}, u32[]{:S(2)}, u32[]{:S(2)}) collective-permute-start(bf16[512,256]{1,0:T(8,128)(2,1)S(1)} %get-tuple-element.20.refs_6_), channel_id=1, source_target_pairs={{0,384},{128,0},{256,128},{384,256},{1,385},{129,1},{257,129},{385... | collective-permute-start | bytes 786440 | tf_op jit(solution)/shard_map/ppermute | solution.py:150
  61.4 2.3 %collective-permute-start.6 = (bf16[512,256]{1,0:T(8,128)(2,1)S(1)}, bf16[512,256]{1,0:T(8,128)(2,1)S(1)}, u32[]{:S(2)}, u32[]{:S(2)}) collective-permute-start(bf16[512,256]{1,0:T(8,128)(2,1)S(1)} %get-tuple-element.19.refs_7_), channel_id=1, source_target_pairs={{0,128},{128,256},{256,384},{384,0},{1,129},{129,257},{257,385},{3... | collective-permute-start | bytes 786440 | tf_op jit(solution)/shard_map/ppermute | solution.py:150
  63.7 3.9 %collective-permute-start.4 = (bf16[512,256]{1,0:T(8,128)(2,1)S(1)}, bf16[512,256]{1,0:T(8,128)(2,1)S(1)}, u32[]{:S(2)}, u32[]{:S(2)}) collective-permute-start(bf16[512,256]{1,0:T(8,128)(2,1)S(1)} %collective-permute-done.1.after.refs_12_), channel_id=1, source_target_pairs={{0,128},{128,256},{256,384},{384,0},{1,129},{129,257},{257,385},{3... | collective-permute-start | bytes 786440 | tf_op jit(solution)/shard_map/ppermute | solution.py:151
  67.7 1.9 %collective-permute-start.5 = (bf16[512,256]{1,0:T(8,128)(2,1)S(1)}, bf16[512,256]{1,0:T(8,128)(2,1)S(1)}, u32[]{:S(2)}, u32[]{:S(2)}) collective-permute-start(bf16[512,256]{1,0:T(8,128)(2,1)S(1)} %collective-permute-done.3.refs_9_), channel_id=1, source_target_pairs={{0,384},{128,0},{256,128},{384,256},{1,385},{129,1},{257,129},{385... | collective-permute-start | bytes 786440 | tf_op jit(solution)/shard_map/ppermute | solution.py:151
  69.6 3.9 %shard_map.94 = (bf16[8,512,512]{2,1,0:T(8,128)(2,1)S(1)}, f32[2,256,256]{2,1,0:T(8,128)S(1)}) custom-call(bf16[8,512,512]{2,1,0:T(8,128)(2,1)} %all-gather.4.cloned.1.call-done.h_hbm, bf16[512,256]{1,0:T(8,128)(2,1)S(1)} %collective-permute-done.1.after.refs_12_), custom_call_target="tpu_custom_call" | custom-call | flops 1073741824 | bytes 8388608 | tf_op jit(solution)/shard_map/pallas_call | solution.py:177
  73.6 2.6 %collective-permute-done.5.refs_11_ = bf16[512,256]{1,0:T(8,128)(2,1)S(1)} collective-permute-done((bf16[512,256]{1,0:T(8,128)(2,1)S(1)}, bf16[512,256]{1,0:T(8,128)(2,1)S(1)}, u32[]{:S(2)}, u32[]{:S(2)}) %collective-permute-start.5) | collective-permute-done | bytes 262176 | tf_op jit(solution)/shard_map/ppermute | solution.py:151
  76.2 2.5 %shard_map.95 = (bf16[512,256]{1,0:T(8,128)(2,1)S(1)}, f32[8,128]{1,0:T(8,128)S(1)}) custom-call(bf16[8,512,512]{2,1,0:T(8,128)(2,1)S(1)} %get-tuple-element.13.refs_0_, bf16[2,256,256]{2,1,0:T(8,128)(2,1)S(1)} %bitcast.8, f32[2,256,256]{2,1,0:T(8,128)S(1)} %get-tuple-element.14.refs_2_, s32[2,16]{1,0:T(2,128)S(1)} %copy-done.2, ...), custom_call_target="tpu_custom_call" | custom-call | flops 1073741824 | bytes 6291456 | tf_op jit(solution)/shard_map/pallas_call | solution.py:191
  78.7 8.4 %all_to_all.15 = f32[8,1,128]{2,1,0:T(1,128)S(1)} all-to-all(f32[8,1,128]{2,1,0:T(1,128)S(1)} %bitcast.11), channel_id=1, replica_groups=mesh['x'=4,'zg'=8,'zp'=2,'y'=4,'core'=2] {'y','core'}, dimensions={0} | all-to-all | bytes 8192 | tf_op jit(solution)/shard_map/all_to_all | solution.py:207
  87.0 1.1 shard_map.96
  88.2 6.6 %all-to-all-start.1 = ((bf16[4,528,256]{2,1,0:T(8,128)(2,1)}), bf16[4,528,256]{2,1,0:T(8,128)(2,1)S(1)}, u32[]{:S(2)}, u32[]{:S(2)}) async-start(bf16[4,528,256]{2,1,0:T(8,128)(2,1)} %shard_map.96), calls=%async_computation.1 | async-start | bytes 2162688 | tf_op jit(solution)/shard_map/all_to_all | solution.py:215
  94.7 6.0 %all-gather.6.cloned.1.call-done = bf16[4096,512]{1,0:T(8,128)(2,1)} async-done(((bf16[512,512]{1,0:T(8,128)(2,1)}), bf16[4096,512]{1,0:T(8,128)(2,1)}) %all-gather.6.cloned.1.call-update) | async-done | bytes 4194320 | tf_op jit(solution)/shard_map/all_gather | solution.py:172
  100.7 8.1 %all-to-all-done.1.g_ref = bf16[4,528,256]{2,1,0:T(8,128)(2,1)S(1)} async-done(((bf16[4,528,256]{2,1,0:T(8,128)(2,1)}), bf16[4,528,256]{2,1,0:T(8,128)(2,1)S(1)}, u32[]{:S(2)}, u32[]{:S(2)}) %all-to-all-start.1) | async-done | bytes 1081376 | tf_op jit(solution)/shard_map/all_to_all | solution.py:215
  108.8 4.1 %shard_map.97 = (f32[8,64,256]{2,1,0:T(8,128)S(1)}, f32[8,64,256]{2,1,0:T(8,128)S(1)}) custom-call(bf16[8,512,512]{2,1,0:T(8,128)(2,1)} %bitcast.12, bf16[4,528,256]{2,1,0:T(8,128)(2,1)S(1)} %all-to-all-done.1.g_ref), custom_call_target="tpu_custom_call" | custom-call | flops 1073741824 | bytes 6291456 | tf_op jit(solution)/shard_map/pallas_call | solution.py:217
  113.1 1.9 %collective-permute-start.7 = (f16[8,64,256]{2,1,0:T(8,128)(2,1)S(1)}, f16[8,64,256]{2,1,0:T(8,128)(2,1)S(1)}, u32[]{:S(2)}, u32[]{:S(2)}) collective-permute-start(f16[8,64,256]{2,1,0:T(8,128)(2,1)S(1)} %multiply_convert_fusion.1), channel_id=1, source_target_pairs={{0,8},{8,0},{1,9},{9,1},{2,10},{10,2},{3,11},{11,3},{4,12},{12,4},... | collective-permute-start | bytes 786440 | tf_op jit(solution)/shard_map/ppermute | solution.py:235
  115.0 6.9 %collective-permute-done.7 = f16[8,64,256]{2,1,0:T(8,128)(2,1)S(1)} collective-permute-done((f16[8,64,256]{2,1,0:T(8,128)(2,1)S(1)}, f16[8,64,256]{2,1,0:T(8,128)(2,1)S(1)}, u32[]{:S(2)}, u32[]{:S(2)}) %collective-permute-start.7) | collective-permute-done | bytes 262176 | tf_op jit(solution)/shard_map/ppermute | solution.py:235
  121.9 0.9 multiply_convert_fusion
  122.8 6.8 %all-to-all-start.2 = ((f16[8,64,256]{2,1,0:T(8,128)(2,1)}), f16[8,64,256]{2,1,0:T(8,128)(2,1)S(1)}, u32[]{:S(2)}, u32[]{:S(2)}) async-start(f16[8,64,256]{2,1,0:T(8,128)(2,1)} %multiply_convert_fusion), calls=%async_computation.2 | async-start | bytes 524288 | tf_op jit(solution)/shard_map/all_to_all | solution.py:237
  130.1 18.6 %all-to-all-done.2 = f16[8,64,256]{2,1,0:T(8,128)(2,1)S(1)} async-done(((f16[8,64,256]{2,1,0:T(8,128)(2,1)}), f16[8,64,256]{2,1,0:T(8,128)(2,1)S(1)}, u32[]{:S(2)}, u32[]{:S(2)}) %all-to-all-start.2) | async-done | bytes 262176 | tf_op jit(solution)/shard_map/all_to_all | solution.py:237
  (29 shorter events, 1.6 us)
Async XLA Ops:
  7.2 69.0 %copy-start.1 = (bf16[2,4,64,256]{3,2,1,0:T(8,128)(2,1)S(1)}, bf16[2,4,64,256]{3,2,1,0:T(8,128)(2,1)}, u32[]{:S(2)}) copy-start(bf16[2,4,64,256]{3,2,1,0:T(8,128)(2,1)} %param.8) | copy-start | bytes 786436
  7.2 69.0 %copy-start.2 = (s32[2,16]{1,0:T(2,128)S(1)}, s32[2,16]{1,0:T(2,128)}, u32[]{:S(2)}) copy-start(s32[2,16]{1,0:T(2,128)} %refs_3_.1) | copy-start | bytes 388
  7.2 69.0 %copy-start = (bf16[1024,256]{1,0:T(8,128)(2,1)S(1)}, bf16[1024,256]{1,0:T(8,128)(2,1)}, u32[]{:S(2)}) copy-start(bf16[1024,256]{1,0:T(8,128)(2,1)} %refs_4_.1) | copy-start | bytes 1572868
  7.2 69.0 %copy-start.3 = (f32[2,4]{1,0:T(2,128)S(1)}, f32[2,4]{1,0:T(2,128)}, u32[]{:S(2)}) copy-start(f32[2,4]{1,0:T(2,128)} %refs_5_.1) | copy-start | bytes 100
  7.2 62.4 %all-gather.4.cloned.1.call-start = ((), (), s32[]{:S(2)}) async-start(), calls=%async_computation.3 | async-start | bytes 4718592 | tf_op jit(solution)/shard_map/all_gather | solution.py:166
  7.9 92.8 %all-gather.6.cloned.1.call-start = ((), (), s32[]{:S(2)}) async-start(), calls=%async_computation.4 | async-start | bytes 4718592 | tf_op jit(solution)/shard_map/all_gather | solution.py:172
  8.0 42.2 %collective-permute-start = (bf16[512,512]{1,0:T(8,128)(2,1)}, bf16[512,512]{1,0:T(8,128)(2,1)S(1)}, u32[]{:S(2)}, u32[]{:S(2)}) collective-permute-start(bf16[512,512]{1,0:T(8,128)(2,1)} %bitcast.14), channel_id=1, source_target_pairs={{0,0},{2,128},{4,256},{6,384},{128,2},{130,130},{132,258},{134,386... | collective-permute-start | bytes 1572872 | tf_op jit(solution)/shard_map/ppermute | solution.py:168
  50.2 0.9 copy-start.4
  51.2 12.6 %collective-permute-start.1 = (bf16[512,256]{1,0:T(8,128)(2,1)S(1)}, bf16[512,256]{1,0:T(8,128)(2,1)S(1)}, u32[]{:S(2)}, u32[]{:S(2)}) collective-permute-start(bf16[512,256]{1,0:T(8,128)(2,1)S(1)} %get-tuple-element.20.refs_6_), channel_id=1, source_target_pairs={{0,128},{128,256},{256,384},{384,0},{1,129},{129,257},{257,385},{3... | collective-permute-start | bytes 786440 | tf_op jit(solution)/shard_map/ppermute | solution.py:149
  55.9 11.7 %collective-permute-start.3 = (bf16[512,256]{1,0:T(8,128)(2,1)S(1)}, bf16[512,256]{1,0:T(8,128)(2,1)S(1)}, u32[]{:S(2)}, u32[]{:S(2)}) collective-permute-start(bf16[512,256]{1,0:T(8,128)(2,1)S(1)} %get-tuple-element.19.refs_7_), channel_id=1, source_target_pairs={{0,384},{128,0},{256,128},{384,256},{1,385},{129,1},{257,129},{385... | collective-permute-start | bytes 786440 | tf_op jit(solution)/shard_map/ppermute | solution.py:149
  57.9 15.7 %collective-permute-start.2 = (bf16[512,256]{1,0:T(8,128)(2,1)S(1)}, bf16[512,256]{1,0:T(8,128)(2,1)S(1)}, u32[]{:S(2)}, u32[]{:S(2)}) collective-permute-start(bf16[512,256]{1,0:T(8,128)(2,1)S(1)} %get-tuple-element.20.refs_6_), channel_id=1, source_target_pairs={{0,384},{128,0},{256,128},{384,256},{1,385},{129,1},{257,129},{385... | collective-permute-start | bytes 786440 | tf_op jit(solution)/shard_map/ppermute | solution.py:150
  61.4 12.2 %collective-permute-start.6 = (bf16[512,256]{1,0:T(8,128)(2,1)S(1)}, bf16[512,256]{1,0:T(8,128)(2,1)S(1)}, u32[]{:S(2)}, u32[]{:S(2)}) collective-permute-start(bf16[512,256]{1,0:T(8,128)(2,1)S(1)} %get-tuple-element.19.refs_7_), channel_id=1, source_target_pairs={{0,128},{128,256},{256,384},{384,0},{1,129},{129,257},{257,385},{3... | collective-permute-start | bytes 786440 | tf_op jit(solution)/shard_map/ppermute | solution.py:150
  63.7 9.8 %collective-permute-start.4 = (bf16[512,256]{1,0:T(8,128)(2,1)S(1)}, bf16[512,256]{1,0:T(8,128)(2,1)S(1)}, u32[]{:S(2)}, u32[]{:S(2)}) collective-permute-start(bf16[512,256]{1,0:T(8,128)(2,1)S(1)} %collective-permute-done.1.after.refs_12_), channel_id=1, source_target_pairs={{0,128},{128,256},{256,384},{384,0},{1,129},{129,257},{257,385},{3... | collective-permute-start | bytes 786440 | tf_op jit(solution)/shard_map/ppermute | solution.py:151
  67.7 8.5 %collective-permute-start.5 = (bf16[512,256]{1,0:T(8,128)(2,1)S(1)}, bf16[512,256]{1,0:T(8,128)(2,1)S(1)}, u32[]{:S(2)}, u32[]{:S(2)}) collective-permute-start(bf16[512,256]{1,0:T(8,128)(2,1)S(1)} %collective-permute-done.3.refs_9_), channel_id=1, source_target_pairs={{0,384},{128,0},{256,128},{384,256},{1,385},{129,1},{257,129},{385... | collective-permute-start | bytes 786440 | tf_op jit(solution)/shard_map/ppermute | solution.py:151
  88.2 20.6 %all-to-all-start.1 = ((bf16[4,528,256]{2,1,0:T(8,128)(2,1)}), bf16[4,528,256]{2,1,0:T(8,128)(2,1)S(1)}, u32[]{:S(2)}, u32[]{:S(2)}) async-start(bf16[4,528,256]{2,1,0:T(8,128)(2,1)} %shard_map.96), calls=%async_computation.1 | async-start | bytes 2162688 | tf_op jit(solution)/shard_map/all_to_all | solution.py:215
  94.7 54.1 %copy-start.6 = (f32[64,256]{1,0:T(8,128)S(1)}, f32[64,256]{1,0:T(8,128)}, u32[]{:S(2)}) copy-start(f32[64,256]{1,0:T(8,128)} %param.13) | copy-start | bytes 196612
  113.1 8.8 %collective-permute-start.7 = (f16[8,64,256]{2,1,0:T(8,128)(2,1)S(1)}, f16[8,64,256]{2,1,0:T(8,128)(2,1)S(1)}, u32[]{:S(2)}, u32[]{:S(2)}) collective-permute-start(f16[8,64,256]{2,1,0:T(8,128)(2,1)S(1)} %multiply_convert_fusion.1), channel_id=1, source_target_pairs={{0,8},{8,0},{1,9},{9,1},{2,10},{10,2},{3,11},{11,3},{4,12},{12,4},... | collective-permute-start | bytes 786440 | tf_op jit(solution)/shard_map/ppermute | solution.py:235
  122.8 25.9 %all-to-all-start.2 = ((f16[8,64,256]{2,1,0:T(8,128)(2,1)}), f16[8,64,256]{2,1,0:T(8,128)(2,1)S(1)}, u32[]{:S(2)}, u32[]{:S(2)}) async-start(f16[8,64,256]{2,1,0:T(8,128)(2,1)} %multiply_convert_fusion), calls=%async_computation.2 | async-start | bytes 524288 | tf_op jit(solution)/shard_map/all_to_all | solution.py:237
  148.8 0.7 copy-start.5
Sparse Core Ops, SparseCore 0:
  10.2 44.2 all-gather.3
  56.6 44.0 all-gather.5

commit v12 on v11

--- a/solution.py
+++ b/solution.py
@@ -206,6 +206,7 @@
 
     sq_all = lax.all_to_all(sq.reshape(nt, 1, 128), tensor, 0, 0).reshape(nt, 128)
     norms = jnp.sqrt(jnp.sum(sq_all[:, :recs], axis=0))
+    mine, norms = lax.optimization_barrier((mine, norms))
 
     packed = pl.pallas_call(
         functools.partial(pack_kernel, bound=bound),

time: 157 us -> 156 us (level)
  blocking collectives: 47.2 us -> 72.9 us
  waiting for transfers between devices: 42.9 us -> 23.7 us
  starting transfers between devices: 37.2 us -> 30.4 us
    all_to_all x0 -> x1, blocking collectives: none -> 25.7 us  [on_device(): clipped_sum = jnp.sum(unroot(lax.all_to_all(sent, 'zg', 0, 0)), axis=0)]
    all_to_all x1 -> x0, waiting for transfers between devices: 18.6 us -> none  [on_device(): clipped_sum = jnp.sum(unroot(lax.all_to_all(sent, 'zg', 0, 0)), axis=0)]
    all_to_all x1 -> x0, starting transfers between devices: 6.79 us -> none  [on_device(): clipped_sum = jnp.sum(unroot(lax.all_to_all(sent, 'zg', 0, 0)), axis=0)]
  transfers between devices with their start and end apart: 12 -> 11, of which waited for: 5 -> 4; matrix products, arithmetic and copies ran while one was open for 0% -> 0% of each run, Pallas kernels for 5% -> 5%
where the time goes in v12:
time: 156 us; the launch traced here: 155 us
  blocking collectives  72.9 us (47%)
  starting transfers between devices  30.4 us (19%)
  waiting for transfers between devices  23.7 us (15%)
  between operations  14.3 us (9%)
  Pallas kernels  11.6 us (7%)
    all_gather x1, blocking collectives, on_device(): wz = lax.all_gather(weight, ('zg', 'zp'), axis=0, tiled=True)  38.8 us
    all_to_all x1, blocking collectives, on_device(): clipped_sum = jnp.sum(unroot(lax.all_to_all(sent, 'zg', 0, 0)), axis=0)  25.7 us
    all_to_all x1, blocking collectives, on_device(): lax.all_to_all(sq.reshape(nt, 1, 128), tensor, 0, 0).reshape(nt, 128)  8.41 us
    all_to_all x1, waiting for transfers between devices, on_device(): packed = lax.all_to_all(packed, 'x', 0, 0)  8.05 us
    ppermute x1, waiting for transfers between devices, on_device(): got = lax.ppermute(root(send).astype(F16), 'zp', [(0, 1), (1, 0)])  6.88 us
    ppermute x2, starting transfers between devices, ring_gather(): a3, b1 = (lax.ppermute(a, 'x', up), lax.ppermute(b, 'x', down))  6.7 us
    all_to_all x1, starting transfers between devices, on_device(): packed = lax.all_to_all(packed, 'x', 0, 0)  6.58 us
    ppermute x2, starting transfers between devices, ring_gather(): a2, b2 = (lax.ppermute(a3, 'x', up), lax.ppermute(b1, 'x', down))  5.84 us
  transfers between devices with their start and end apart: 11, of which 4 were waited for; matrix products, arithmetic and copies ran while one was open for 0% of the time, Pallas kernels for 5%

profile of v12, /device:TPU:2, one launch (start us, length us, event | category | flops | bytes accessed | tf_op | source)
XLA Modules:
  0.0 155.4 jit_solution(10209195897134043692)
XLA Ops:
  7.3 0.7 all-gather.4.cloned.1.call-update
  8.0 3.5 %collective-permute-start = (bf16[512,512]{1,0:T(8,128)(2,1)}, bf16[512,512]{1,0:T(8,128)(2,1)S(1)}, u32[]{:S(2)}, u32[]{:S(2)}) collective-permute-start(bf16[512,512]{1,0:T(8,128)(2,1)} %bitcast.14), channel_id=1, source_target_pairs={{0,0},{2,128},{4,256},{6,384},{128,2},{130,130},{132,258},{134,386... | collective-permute-start | bytes 1572872 | tf_op jit(solution)/shard_map/ppermute | solution.py:168
  11.5 38.8 %all_gather.12 = bf16[1024,256]{1,0:T(8,128)(2,1)S(1)} all-gather(bf16[64,256]{1,0:T(8,128)(2,1)} %param.12), channel_id=1, replica_groups=mesh['x'=4,'zg'=8,'zp'=2,'y'=4,'core'=2] {'zg','zp'}, dimensions={0}, use_global_device_ids=true | all-gather | bytes 557056 | tf_op jit(solution)/shard_map/all_gather | solution.py:170
  50.2 0.9 copy-done.4
  51.2 4.8 %collective-permute-start.1 = (bf16[512,256]{1,0:T(8,128)(2,1)S(1)}, bf16[512,256]{1,0:T(8,128)(2,1)S(1)}, u32[]{:S(2)}, u32[]{:S(2)}) collective-permute-start(bf16[512,256]{1,0:T(8,128)(2,1)S(1)} %get-tuple-element.24.refs_6_), channel_id=1, source_target_pairs={{0,128},{128,256},{256,384},{384,0},{1,129},{129,257},{257,385},{3... | collective-permute-start | bytes 786440 | tf_op jit(solution)/shard_map/ppermute | solution.py:149
  55.9 1.9 %collective-permute-start.3 = (bf16[512,256]{1,0:T(8,128)(2,1)S(1)}, bf16[512,256]{1,0:T(8,128)(2,1)S(1)}, u32[]{:S(2)}, u32[]{:S(2)}) collective-permute-start(bf16[512,256]{1,0:T(8,128)(2,1)S(1)} %get-tuple-element.23.refs_7_), channel_id=1, source_target_pairs={{0,384},{128,0},{256,128},{384,256},{1,385},{129,1},{257,129},{385... | collective-permute-start | bytes 786440 | tf_op jit(solution)/shard_map/ppermute | solution.py:149
  57.9 3.5 %collective-permute-start.2 = (bf16[512,256]{1,0:T(8,128)(2,1)S(1)}, bf16[512,256]{1,0:T(8,128)(2,1)S(1)}, u32[]{:S(2)}, u32[]{:S(2)}) collective-permute-start(bf16[512,256]{1,0:T(8,128)(2,1)S(1)} %get-tuple-element.24.refs_6_), channel_id=1, source_target_pairs={{0,384},{128,0},{256,128},{384,256},{1,385},{129,1},{257,129},{385... | collective-permute-start | bytes 786440 | tf_op jit(solution)/shard_map/ppermute | solution.py:150
  61.4 2.3 %collective-permute-start.6 = (bf16[512,256]{1,0:T(8,128)(2,1)S(1)}, bf16[512,256]{1,0:T(8,128)(2,1)S(1)}, u32[]{:S(2)}, u32[]{:S(2)}) collective-permute-start(bf16[512,256]{1,0:T(8,128)(2,1)S(1)} %get-tuple-element.23.refs_7_), channel_id=1, source_target_pairs={{0,128},{128,256},{256,384},{384,0},{1,129},{129,257},{257,385},{3... | collective-permute-start | bytes 786440 | tf_op jit(solution)/shard_map/ppermute | solution.py:150
  63.7 3.9 %collective-permute-start.4 = (bf16[512,256]{1,0:T(8,128)(2,1)S(1)}, bf16[512,256]{1,0:T(8,128)(2,1)S(1)}, u32[]{:S(2)}, u32[]{:S(2)}) collective-permute-start(bf16[512,256]{1,0:T(8,128)(2,1)S(1)} %collective-permute-done.1.after.refs_12_), channel_id=1, source_target_pairs={{0,128},{128,256},{256,384},{384,0},{1,129},{129,257},{257,385},{3... | collective-permute-start | bytes 786440 | tf_op jit(solution)/shard_map/ppermute | solution.py:151
  67.7 1.9 %collective-permute-start.5 = (bf16[512,256]{1,0:T(8,128)(2,1)S(1)}, bf16[512,256]{1,0:T(8,128)(2,1)S(1)}, u32[]{:S(2)}, u32[]{:S(2)}) collective-permute-start(bf16[512,256]{1,0:T(8,128)(2,1)S(1)} %collective-permute-done.3.refs_9_), channel_id=1, source_target_pairs={{0,384},{128,0},{256,128},{384,256},{1,385},{129,1},{257,129},{385... | collective-permute-start | bytes 786440 | tf_op jit(solution)/shard_map/ppermute | solution.py:151
  69.6 3.9 %shard_map.94 = (bf16[8,512,512]{2,1,0:T(8,128)(2,1)S(1)}, f32[2,256,256]{2,1,0:T(8,128)S(1)}) custom-call(bf16[8,512,512]{2,1,0:T(8,128)(2,1)} %all-gather.4.cloned.1.call-done.h_hbm, bf16[512,256]{1,0:T(8,128)(2,1)S(1)} %collective-permute-done.1.after.refs_12_), custom_call_target="tpu_custom_call" | custom-call | flops 1073741824 | bytes 8388608 | tf_op jit(solution)/shard_map/pallas_call | solution.py:177
  73.6 2.6 %collective-permute-done.5.refs_11_ = bf16[512,256]{1,0:T(8,128)(2,1)S(1)} collective-permute-done((bf16[512,256]{1,0:T(8,128)(2,1)S(1)}, bf16[512,256]{1,0:T(8,128)(2,1)S(1)}, u32[]{:S(2)}, u32[]{:S(2)}) %collective-permute-start.5) | collective-permute-done | bytes 262176 | tf_op jit(solution)/shard_map/ppermute | solution.py:151
  76.2 2.5 %shard_map.95 = (bf16[512,256]{1,0:T(8,128)(2,1)S(1)}, f32[8,128]{1,0:T(8,128)S(1)}) custom-call(bf16[8,512,512]{2,1,0:T(8,128)(2,1)S(1)} %get-tuple-element.15.refs_0_, bf16[2,256,256]{2,1,0:T(8,128)(2,1)S(1)} %bitcast.8, f32[2,256,256]{2,1,0:T(8,128)S(1)} %get-tuple-element.16.refs_2_, s32[2,16]{1,0:T(2,128)S(1)} %copy-done.2, ...), custom_call_target="tpu_custom_call" | custom-call | flops 1073741824 | bytes 6291456 | tf_op jit(solution)/shard_map/pallas_call | solution.py:191
  78.6 8.4 %all_to_all.15 = f32[8,1,128]{2,1,0:T(1,128)S(1)} all-to-all(f32[8,1,128]{2,1,0:T(1,128)S(1)} %bitcast.11), channel_id=1, replica_groups=mesh['x'=4,'zg'=8,'zp'=2,'y'=4,'core'=2] {'y','core'}, dimensions={0} | all-to-all | bytes 8192 | tf_op jit(solution)/shard_map/all_to_all | solution.py:207
  87.1 1.1 shard_map.96
  88.1 6.6 %all-to-all-start.1 = ((bf16[4,528,256]{2,1,0:T(8,128)(2,1)}), bf16[4,528,256]{2,1,0:T(8,128)(2,1)S(1)}, u32[]{:S(2)}, u32[]{:S(2)}) async-start(bf16[4,528,256]{2,1,0:T(8,128)(2,1)} %shard_map.96), calls=%async_computation.1 | async-start | bytes 2162688 | tf_op jit(solution)/shard_map/all_to_all | solution.py:216
  94.7 0.5 sqrt.3
  95.3 5.5 %all-gather.6.cloned.1.call-done = bf16[4096,512]{1,0:T(8,128)(2,1)} async-done(((bf16[512,512]{1,0:T(8,128)(2,1)}), bf16[4096,512]{1,0:T(8,128)(2,1)}) %all-gather.6.cloned.1.call-update) | async-done | bytes 4194320 | tf_op jit(solution)/shard_map/all_gather | solution.py:172
  100.7 8.1 %all-to-all-done.1.g_ref = bf16[4,528,256]{2,1,0:T(8,128)(2,1)S(1)} async-done(((bf16[4,528,256]{2,1,0:T(8,128)(2,1)}), bf16[4,528,256]{2,1,0:T(8,128)(2,1)S(1)}, u32[]{:S(2)}, u32[]{:S(2)}) %all-to-all-start.1) | async-done | bytes 1081376 | tf_op jit(solution)/shard_map/all_to_all | solution.py:216
  108.8 4.1 %shard_map.97 = (f32[8,64,256]{2,1,0:T(8,128)S(1)}, f32[8,64,256]{2,1,0:T(8,128)S(1)}) custom-call(bf16[8,512,512]{2,1,0:T(8,128)(2,1)} %bitcast.12, bf16[4,528,256]{2,1,0:T(8,128)(2,1)S(1)} %all-to-all-done.1.g_ref), custom_call_target="tpu_custom_call" | custom-call | flops 1073741824 | bytes 6291456 | tf_op jit(solution)/shard_map/pallas_call | solution.py:218
  113.0 1.9 %collective-permute-start.7 = (f16[8,64,256]{2,1,0:T(8,128)(2,1)S(1)}, f16[8,64,256]{2,1,0:T(8,128)(2,1)S(1)}, u32[]{:S(2)}, u32[]{:S(2)}) collective-permute-start(f16[8,64,256]{2,1,0:T(8,128)(2,1)S(1)} %multiply_convert_fusion.1), channel_id=1, source_target_pairs={{0,8},{8,0},{1,9},{9,1},{2,10},{10,2},{3,11},{11,3},{4,12},{12,4},... | collective-permute-start | bytes 786440 | tf_op jit(solution)/shard_map/ppermute | solution.py:236
  115.0 6.9 %collective-permute-done.7 = f16[8,64,256]{2,1,0:T(8,128)(2,1)S(1)} collective-permute-done((f16[8,64,256]{2,1,0:T(8,128)(2,1)S(1)}, f16[8,64,256]{2,1,0:T(8,128)(2,1)S(1)}, u32[]{:S(2)}, u32[]{:S(2)}) %collective-permute-start.7) | collective-permute-done | bytes 262176 | tf_op jit(solution)/shard_map/ppermute | solution.py:236
  122.1 25.7 %all_to_all.16 = f16[8,64,256]{2,1,0:T(8,128)(2,1)S(1)} all-to-all(f16[8,64,256]{2,1,0:T(8,128)(2,1)S(1)} %multiply_convert_fusion), channel_id=1, replica_groups=mesh['x'=4,'zg'=8,'zp'=2,'y'=4,'core'=2] {'zg'}, dimensions={0} | all-to-all | bytes 524288 | tf_op jit(solution)/shard_map/all_to_all | solution.py:238
  147.9 0.7 add_multiply_fusion
  (28 shorter events, 0.6 us)
Async XLA Ops:
  7.2 69.0 %copy-start.1 = (bf16[2,4,64,256]{3,2,1,0:T(8,128)(2,1)S(1)}, bf16[2,4,64,256]{3,2,1,0:T(8,128)(2,1)}, u32[]{:S(2)}) copy-start(bf16[2,4,64,256]{3,2,1,0:T(8,128)(2,1)} %param.8) | copy-start | bytes 786436
  7.2 69.0 %copy-start.2 = (s32[2,16]{1,0:T(2,128)S(1)}, s32[2,16]{1,0:T(2,128)}, u32[]{:S(2)}) copy-start(s32[2,16]{1,0:T(2,128)} %refs_3_.1) | copy-start | bytes 388
  7.2 69.0 %copy-start = (bf16[1024,256]{1,0:T(8,128)(2,1)S(1)}, bf16[1024,256]{1,0:T(8,128)(2,1)}, u32[]{:S(2)}) copy-start(bf16[1024,256]{1,0:T(8,128)(2,1)} %refs_4_.1) | copy-start | bytes 1572868
  7.2 68.9 %copy-start.3 = (f32[2,4]{1,0:T(2,128)S(1)}, f32[2,4]{1,0:T(2,128)}, u32[]{:S(2)}) copy-start(f32[2,4]{1,0:T(2,128)} %refs_5_.1) | copy-start | bytes 100
  7.2 62.4 %all-gather.4.cloned.1.call-start = ((), (), s32[]{:S(2)}) async-start(), calls=%async_computation.3 | async-start | bytes 4718592 | tf_op jit(solution)/shard_map/all_gather | solution.py:166
  7.9 92.8 %all-gather.6.cloned.1.call-start = ((), (), s32[]{:S(2)}) async-start(), calls=%async_computation.4 | async-start | bytes 4718592 | tf_op jit(solution)/shard_map/all_gather | solution.py:172
  8.0 42.2 %collective-permute-start = (bf16[512,512]{1,0:T(8,128)(2,1)}, bf16[512,512]{1,0:T(8,128)(2,1)S(1)}, u32[]{:S(2)}, u32[]{:S(2)}) collective-permute-start(bf16[512,512]{1,0:T(8,128)(2,1)} %bitcast.14), channel_id=1, source_target_pairs={{0,0},{2,128},{4,256},{6,384},{128,2},{130,130},{132,258},{134,386... | collective-permute-start | bytes 1572872 | tf_op jit(solution)/shard_map/ppermute | solution.py:168
  50.2 0.9 copy-start.4
  51.2 12.6 %collective-permute-start.1 = (bf16[512,256]{1,0:T(8,128)(2,1)S(1)}, bf16[512,256]{1,0:T(8,128)(2,1)S(1)}, u32[]{:S(2)}, u32[]{:S(2)}) collective-permute-start(bf16[512,256]{1,0:T(8,128)(2,1)S(1)} %get-tuple-element.24.refs_6_), channel_id=1, source_target_pairs={{0,128},{128,256},{256,384},{384,0},{1,129},{129,257},{257,385},{3... | collective-permute-start | bytes 786440 | tf_op jit(solution)/shard_map/ppermute | solution.py:149
  55.9 11.7 %collective-permute-start.3 = (bf16[512,256]{1,0:T(8,128)(2,1)S(1)}, bf16[512,256]{1,0:T(8,128)(2,1)S(1)}, u32[]{:S(2)}, u32[]{:S(2)}) collective-permute-start(bf16[512,256]{1,0:T(8,128)(2,1)S(1)} %get-tuple-element.23.refs_7_), channel_id=1, source_target_pairs={{0,384},{128,0},{256,128},{384,256},{1,385},{129,1},{257,129},{385... | collective-permute-start | bytes 786440 | tf_op jit(solution)/shard_map/ppermute | solution.py:149
  57.9 15.7 %collective-permute-start.2 = (bf16[512,256]{1,0:T(8,128)(2,1)S(1)}, bf16[512,256]{1,0:T(8,128)(2,1)S(1)}, u32[]{:S(2)}, u32[]{:S(2)}) collective-permute-start(bf16[512,256]{1,0:T(8,128)(2,1)S(1)} %get-tuple-element.24.refs_6_), channel_id=1, source_target_pairs={{0,384},{128,0},{256,128},{384,256},{1,385},{129,1},{257,129},{385... | collective-permute-start | bytes 786440 | tf_op jit(solution)/shard_map/ppermute | solution.py:150
  61.4 12.2 %collective-permute-start.6 = (bf16[512,256]{1,0:T(8,128)(2,1)S(1)}, bf16[512,256]{1,0:T(8,128)(2,1)S(1)}, u32[]{:S(2)}, u32[]{:S(2)}) collective-permute-start(bf16[512,256]{1,0:T(8,128)(2,1)S(1)} %get-tuple-element.23.refs_7_), channel_id=1, source_target_pairs={{0,128},{128,256},{256,384},{384,0},{1,129},{129,257},{257,385},{3... | collective-permute-start | bytes 786440 | tf_op jit(solution)/shard_map/ppermute | solution.py:150
  63.7 9.8 %collective-permute-start.4 = (bf16[512,256]{1,0:T(8,128)(2,1)S(1)}, bf16[512,256]{1,0:T(8,128)(2,1)S(1)}, u32[]{:S(2)}, u32[]{:S(2)}) collective-permute-start(bf16[512,256]{1,0:T(8,128)(2,1)S(1)} %collective-permute-done.1.after.refs_12_), channel_id=1, source_target_pairs={{0,128},{128,256},{256,384},{384,0},{1,129},{129,257},{257,385},{3... | collective-permute-start | bytes 786440 | tf_op jit(solution)/shard_map/ppermute | solution.py:151
  67.7 8.5 %collective-permute-start.5 = (bf16[512,256]{1,0:T(8,128)(2,1)S(1)}, bf16[512,256]{1,0:T(8,128)(2,1)S(1)}, u32[]{:S(2)}, u32[]{:S(2)}) collective-permute-start(bf16[512,256]{1,0:T(8,128)(2,1)S(1)} %collective-permute-done.3.refs_9_), channel_id=1, source_target_pairs={{0,384},{128,0},{256,128},{384,256},{1,385},{129,1},{257,129},{385... | collective-permute-start | bytes 786440 | tf_op jit(solution)/shard_map/ppermute | solution.py:151
  88.1 20.6 %all-to-all-start.1 = ((bf16[4,528,256]{2,1,0:T(8,128)(2,1)}), bf16[4,528,256]{2,1,0:T(8,128)(2,1)S(1)}, u32[]{:S(2)}, u32[]{:S(2)}) async-start(bf16[4,528,256]{2,1,0:T(8,128)(2,1)} %shard_map.96), calls=%async_computation.1 | async-start | bytes 2162688 | tf_op jit(solution)/shard_map/all_to_all | solution.py:216
  94.7 53.2 %copy-start.6 = (f32[64,256]{1,0:T(8,128)S(1)}, f32[64,256]{1,0:T(8,128)}, u32[]{:S(2)}) copy-start(f32[64,256]{1,0:T(8,128)} %param.13) | copy-start | bytes 196612
  113.0 8.8 %collective-permute-start.7 = (f16[8,64,256]{2,1,0:T(8,128)(2,1)S(1)}, f16[8,64,256]{2,1,0:T(8,128)(2,1)S(1)}, u32[]{:S(2)}, u32[]{:S(2)}) collective-permute-start(f16[8,64,256]{2,1,0:T(8,128)(2,1)S(1)} %multiply_convert_fusion.1), channel_id=1, source_target_pairs={{0,8},{8,0},{1,9},{9,1},{2,10},{10,2},{3,11},{11,3},{4,12},{12,4},... | collective-permute-start | bytes 786440 | tf_op jit(solution)/shard_map/ppermute | solution.py:236
  147.9 0.7 copy-start.5
Sparse Core Ops, SparseCore 0:
  10.2 44.2 all-gather.3
  56.6 44.0 all-gather.5
